TPU v7x, 32 devices: a whole 2x2x4 slice. The times are simulated.
32 devices in a mesh: group: 2 (over x), shard: 16 (over z, y, core).
Axes of the slice: x: 2, y: 2, z: 4, core: 2. Of those that a mesh axis runs over, the one named last changes fastest.
Arguments:
- tokens: bfloat16 [128, 3072], P('group', 'shard'), may hold values from -6 to 6
- cotangent: bfloat16 [128, 3072], P('group', 'shard'), may hold values from -1.5 to 1.5
- expert_ids: int32 [128, 2], P('group'), may hold values from 0 to 7, all different within a row; in each aligned block of 64 rows (0 to 63, 64 to 127, ...) at most 36 rows name the same one
- route_weight: float32 [128, 2], P('group'), may hold values from 0.1 to 0.9
- w_gate: bfloat16 [8, 3072, 8192], P('group', None, 'shard'), may hold values from -0.109375 to 0.109375
- w_up: bfloat16 [8, 3072, 8192], P('group', None, 'shard'), may hold values from -0.109375 to 0.109375
- w_down: bfloat16 [8, 8192, 3072], P('group', 'shard'), may hold values from -0.109375 to 0.109375
Outputs:
- grad_tokens: bfloat16 [128, 3072], P('group', 'shard')
- grad_gate: bfloat16 [8, 3072, 8192], P('group', None, 'shard')
- grad_up: bfloat16 [8, 3072, 8192], P('group', None, 'shard')
Inputs may be any that keep to these rules, and one draw needn't show every extreme that they name: `expert_ids`: each token names 2 different experts. Among the 64 tokens of one aligned block (the tokens of one index of group), no expert is named by more than 36 tokens.
All inputs are finite; a program needn't handle non-finite values.
Results may differ from a plain program's by a relative error of at most 0.0064.
Values may be sent and summed in bfloat16 or wider, within the bound.
No kernel may reach another device: no remote copies, remote signals or barrier semaphores. Data moves between devices by JAX's collectives and lax.ppermute only.
A program may use at most 192 MiB of HBM per device.

v0:
```python
import jax
import jax.numpy as jnp
from jax import lax
from jax.sharding import PartitionSpec as P

EXPERTS = 8
CAP = 36


exact_mode = lax.Precision.HIGHEST


def slot_table(expert_ids, capacity):
    experts_axis = jnp.arange(EXPERTS, dtype=jnp.int32)
    counted = jnp.sum(
        (expert_ids[:, :, None] == experts_axis[None, None, :]).astype(jnp.int32), axis=1
    )
    ranking = jnp.cumsum(counted, axis=0) - 1
    places = jnp.arange(capacity, dtype=jnp.int32)
    slot_map = (counted.T[:, None, :] == 1) & (ranking.T[:, None, :] == places[None, :, None])
    return (counted, slot_map)


def slot_scales(slot_map, expert_ids, route_weight):
    experts_axis = jnp.arange(EXPERTS, dtype=jnp.int32)
    per_expert = jnp.sum(
        jnp.where(
            expert_ids[:, :, None] == experts_axis[None, None, :],
            route_weight[:, :, None],
            jnp.float32(0.0),
        ),
        axis=1,
    )
    return jnp.einsum("ect,te->ec", slot_map.astype(jnp.float32), per_expert, precision=exact_mode)


def place_rows(slot_map, scales, inputs, cotangents):
    selector = slot_map.astype(jnp.bfloat16)
    picked_inputs = jnp.einsum(
        "ect,td->ecd", selector, inputs, preferred_element_type=jnp.float32
    ).astype(jnp.bfloat16)
    picked_cot = jnp.einsum("ect,td->ecd", selector, cotangents, preferred_element_type=jnp.float32)
    scaled_cot = (scales[:, :, None] * picked_cot).astype(jnp.bfloat16)
    return (picked_inputs, scaled_cot)


def slot_grads(slot_inputs, slot_cotangents, paired, down_weight):
    hidden_width = down_weight.shape[0]
    joined = jnp.dot(slot_inputs, paired, preferred_element_type=jnp.float32)
    gate_pre = joined[:, :hidden_width]
    up_value = joined[:, hidden_width:]
    sigmoid_gate = jax.nn.sigmoid(gate_pre)
    active = gate_pre * sigmoid_gate
    hidden_grad = lax.dot_general(
        slot_cotangents, down_weight, (((1,), (1,)), ((), ())), preferred_element_type=jnp.float32
    )
    gate_grad = (
        hidden_grad * up_value * sigmoid_gate * (1.0 + gate_pre * (1.0 - sigmoid_gate))
    ).astype(jnp.bfloat16)
    up_grad = (hidden_grad * active).astype(jnp.bfloat16)
    stacked = jnp.concatenate([gate_grad, up_grad], axis=1)
    input_grad = lax.dot_general(
        stacked, paired, (((1,), (1,)), ((), ())), preferred_element_type=jnp.float32
    )
    return (input_grad, stacked)


def source_partials(slot_inputs, stacked, sources):
    capacity = slot_inputs.shape[0] // sources

    def accumulate(source, running):
        begin = (source * capacity).astype(jnp.int32)
        piece_inputs = lax.dynamic_slice_in_dim(slot_inputs, begin, capacity, 0)
        piece_grads = lax.dynamic_slice_in_dim(stacked, begin, capacity, 0)
        partial_sum = lax.dot_general(
            piece_inputs, piece_grads, (((0,), (0,)), ((), ())), preferred_element_type=jnp.float32
        )
        return running + lax.optimization_barrier(partial_sum.astype(jnp.bfloat16)).astype(
            jnp.float32
        )

    initial = jnp.zeros((slot_inputs.shape[1], stacked.shape[1]), jnp.float32)
    return lax.fori_loop(jnp.int32(0), jnp.int32(sources), accumulate, initial)


def body(tokens, cotangent, expert_ids, route_weight, w_gate, w_up, w_down):
    groups = lax.axis_size("group")
    local_count = w_gate.shape[0]
    hidden_width = w_gate.shape[2]
    counted, slot_map = slot_table(expert_ids, CAP)
    scales = slot_scales(slot_map, expert_ids, route_weight)
    paired_local = jnp.concatenate([w_gate, w_up], axis=2)
    full_tokens, full_cot = (
        lax.all_gather(tokens, "shard", axis=1, tiled=True),
        lax.all_gather(cotangent, "shard", axis=1, tiled=True),
    )
    sent_inputs, sent_cot = place_rows(slot_map, scales, full_tokens, full_cot)
    slot_inputs, slot_cot = (
        lax.all_to_all(sent_inputs, "group", split_axis=0, concat_axis=1, tiled=True),
        lax.all_to_all(sent_cot, "group", split_axis=0, concat_axis=1, tiled=True),
    )
    grads_rows = []
    weight_totals = []
    for position in range(local_count):
        input_grad, stacked = slot_grads(
            slot_inputs[position], slot_cot[position], paired_local[position], w_down[position]
        )
        grads_rows.append(input_grad)
        weight_totals.append(source_partials(slot_inputs[position], stacked, groups))
    slot_grad = jnp.stack(grads_rows)
    summed_rows = lax.psum_scatter(slot_grad, "shard", scatter_dimension=2, tiled=True)
    returned = lax.all_to_all(summed_rows, "group", split_axis=1, concat_axis=0, tiled=True)
    grad_total = jnp.einsum(
        "ect,ecd->td", slot_map.astype(jnp.float32), returned, precision=exact_mode
    )
    stacked_totals = jnp.stack(weight_totals)
    grad_gate = stacked_totals[:, :, :hidden_width].astype(jnp.bfloat16)
    grad_up = stacked_totals[:, :, hidden_width:].astype(jnp.bfloat16)
    return (grad_total.astype(jnp.bfloat16), grad_gate, grad_up)


def solution(mesh):
    in_specs = (
        P("group", "shard"),
        P("group", "shard"),
        P("group", None),
        P("group", None),
        P("group", None, "shard"),
        P("group", None, "shard"),
        P("group", "shard", None),
    )
    out_specs = (P("group", "shard"), P("group", None, "shard"), P("group", None, "shard"))
    return jax.shard_map(body, mesh=mesh, in_specs=in_specs, out_specs=out_specs, check_vma=False)
```

profile of v0, /device:TPU:0, one launch (start us, length us, event | category | flops | bytes accessed | tf_op | source)
XLA Modules:
  0.0 371.5 jit_solution(14438549994853910742)
XLA Ops:
  8.0 24.8 %all-gather.1 = bf16[16,192,64]{1,2,0:T(8,128)(2,1)S(1)} all-gather(bf16[1,192,64]{1,2,0:T(8,128)(2,1)} %bitcast.116), channel_id=1, replica_groups=mesh['group'=2,'shard'=16] {'shard'}, dimensions={0}, use_global_device_ids=true | all-gather | bytes 417792 | tf_op jit(solution)/shard_map/all_gather | solution.py:94
  39.5 19.1 %all-gather = bf16[16,192,64]{1,2,0:T(8,128)(2,1)S(1)} all-gather(bf16[1,192,64]{1,2,0:T(8,128)(2,1)} %bitcast.117), channel_id=1, replica_groups=mesh['group'=2,'shard'=16] {'shard'}, dimensions={0}, use_global_device_ids=true | all-gather | bytes 417792 | tf_op jit(solution)/shard_map/all_gather | solution.py:95
  62.3 10.6 %constant_dynamic-update-slice_fusion.1 = bf16[4,3072,1024]{2,1,0:T(8,128)(2,1)} fusion(bf16[4,3072,512]{2,1,0:T(8,128)(2,1)} %param.19), kind=kLoop, calls=%fused_computation.101 | loop fusion | bytes 25165824
  77.7 10.8 %constant_dynamic-update-slice_fusion = bf16[4,3072,1024]{2,1,0:T(8,128)(2,1)} fusion(bf16[4,3072,1024]{2,1,0:T(8,128)(2,1)} %constant_dynamic-update-slice_fusion.1, bf16[4,3072,512]{2,1,0:T(8,128)(2,1)} %param.20), kind=kLoop, calls=%fused_computation.100 | loop fusion | bytes 25165824 | tf_op jit(solution)/shard_map/concatenate | solution.py:92
  88.9 13.2 %all-to-all-done = bf16[8,36,3072]{2,1,0:T(8,128)(2,1)} async-done(((bf16[8,36,3072]{2,1,0:T(8,128)(2,1)}), bf16[8,36,3072]{2,1,0:T(8,128)(2,1)}, u32[]{:S(2)}, u32[]{:S(2)}) %all-to-all-start) | async-done | bytes 1769504 | tf_op jit(solution)/shard_map/all_to_all | solution.py:100
  113.7 5.8 %fusion.21 = f32[1,72,3072]{2,1,0:T(8,128)} fusion(bf16[4,3072,1024]{2,1,0:T(8,128)(2,1)} %constant_dynamic-update-slice_fusion, bf16[72,512]{1,0:T(8,128)(2,1)S(1)} %get-tuple-element.204, bf16[72,512]{1,0:T(8,128)(2,1)S(1)} %get-tuple-element.203), kind=kOutput, calls=%fused_computation.37 | convolution fusion | flops 453279744 | bytes 7323648 | tf_op jit(solution)/shard_map/dot_general | solution.py:62
  120.3 4.9 %fusion.17 = f32[72,1024]{1,0:T(8,128)} fusion(bf16[72,3072]{1,0:T(8,128)(2,1)S(1)} %squeeze.62, bf16[4,3072,1024]{2,1,0:T(8,128)(2,1)} %constant_dynamic-update-slice_fusion), kind=kOutput, calls=%fused_computation.30 | convolution fusion | flops 452984832 | bytes 7028736 | tf_op jit(solution)/shard_map/dot_general | solution.py:49
  128.3 5.8 %fusion.22 = f32[1,72,3072]{2,1,0:T(8,128)} fusion(bf16[4,3072,1024]{2,1,0:T(8,128)(2,1)} %constant_dynamic-update-slice_fusion, bf16[72,512]{1,0:T(8,128)(2,1)S(1)} %get-tuple-element.202, bf16[72,512]{1,0:T(8,128)(2,1)S(1)} %get-tuple-element.201), kind=kOutput, calls=%fused_computation.38 | convolution fusion | flops 453279744 | bytes 7323648 | tf_op jit(solution)/shard_map/dot_general | solution.py:62
  142.2 5.7 %fusion.23 = f32[1,72,3072]{2,1,0:T(8,128)} fusion(bf16[4,3072,1024]{2,1,0:T(8,128)(2,1)} %constant_dynamic-update-slice_fusion, bf16[72,512]{1,0:T(8,128)(2,1)S(1)} %get-tuple-element.200, bf16[72,512]{1,0:T(8,128)(2,1)S(1)} %get-tuple-element.199), kind=kOutput, calls=%fused_computation.39 | convolution fusion | flops 453279744 | bytes 7323648 | tf_op jit(solution)/shard_map/dot_general | solution.py:62
  168.0 7.7 %reshape.39 = f32[3072,288]{1,0:T(8,128)} reshape(f32[3072,4,72]{2,1,0:T(4,128)} %bitcast.109) | data formatting | bytes 7077888
  175.8 35.1 %while.47 = (s32[]{:T(128)}, f32[3072,1024]{1,0:T(8,128)}, bf16[72,3072]{1,0:T(8,128)(2,1)S(1)}, bf16[72,1024]{1,0:T(8,128)(2,1)S(1)}, s32[]{:T(128)}, /*index=5*/s32[]{:T(128)}, s32[]{:T(128)}, s32[]{:T(128)}) while((s32[]{:T(128)}, f32[3072,1024]{1,0:T(8,128)}, bf16[72,3072]{1,0:T(8,128)(2,1)S(1)}, ...), condition=%wide.region_11.12_spmd.clone, body=%wide.region_10.11_spmd.clone.sunk | while | flops 239075328 | bytes 38077588 | solution.py:83
  180.3 11.5 %select_add_fusion.11 = f32[3072,1024]{1,0:T(8,128)} fusion(f32[3072,1024]{1,0:T(8,128)} %get-tuple-element.314, bf16[3072,1024]{1,0:T(8,128)(2,1)} %convolution_convert_fusion.12, pred[]{:T(512)S(6)} %compare.15), kind=kLoop, calls=%fused_computation.15.clone.1 | loop fusion | flops 9437184 | bytes 31457280 | tf_op jit(solution)/shard_map/while/body/add | solution.py:78
  196.3 14.5 %select_add_fusion.11 = f32[3072,1024]{1,0:T(8,128)} fusion(f32[3072,1024]{1,0:T(8,128)} %get-tuple-element.314, bf16[3072,1024]{1,0:T(8,128)(2,1)} %convolution_convert_fusion.12, pred[]{:T(512)S(6)} %compare.15), kind=kLoop, calls=%fused_computation.15.clone.1 | loop fusion | flops 9437184 | bytes 31457280 | tf_op jit(solution)/shard_map/while/body/add | solution.py:78
  210.9 34.8 %while.46 = (s32[]{:T(128)}, f32[3072,1024]{1,0:T(8,128)}, bf16[72,3072]{1,0:T(8,128)(2,1)S(1)}, bf16[72,1024]{1,0:T(8,128)(2,1)S(1)}, s32[]{:T(128)}, /*index=5*/s32[]{:T(128)}, s32[]{:T(128)}, s32[]{:T(128)}) while((s32[]{:T(128)}, f32[3072,1024]{1,0:T(8,128)}, bf16[72,3072]{1,0:T(8,128)(2,1)S(1)}, ...), condition=%wide.region_9.10_spmd.clone, body=%wide.region_8.9_spmd.clone.sunk | while | flops 239075328 | bytes 38077588 | solution.py:83
  215.4 11.0 %select_add_fusion.10 = f32[3072,1024]{1,0:T(8,128)} fusion(f32[3072,1024]{1,0:T(8,128)} %get-tuple-element.338, bf16[3072,1024]{1,0:T(8,128)(2,1)} %convolution_convert_fusion.11, pred[]{:T(512)S(6)} %compare.14), kind=kLoop, calls=%fused_computation.10.clone.1 | loop fusion | flops 9437184 | bytes 31457280 | tf_op jit(solution)/shard_map/while/body/add | solution.py:78
  230.9 14.7 %select_add_fusion.10 = f32[3072,1024]{1,0:T(8,128)} fusion(f32[3072,1024]{1,0:T(8,128)} %get-tuple-element.338, bf16[3072,1024]{1,0:T(8,128)(2,1)} %convolution_convert_fusion.11, pred[]{:T(512)S(6)} %compare.14), kind=kLoop, calls=%fused_computation.10.clone.1 | loop fusion | flops 9437184 | bytes 31457280 | tf_op jit(solution)/shard_map/while/body/add | solution.py:78
  245.6 34.2 %while.45 = (s32[]{:T(128)}, f32[3072,1024]{1,0:T(8,128)}, bf16[72,3072]{1,0:T(8,128)(2,1)S(1)}, bf16[72,1024]{1,0:T(8,128)(2,1)S(1)}, s32[]{:T(128)}, /*index=5*/s32[]{:T(128)}, s32[]{:T(128)}, s32[]{:T(128)}) while((s32[]{:T(128)}, f32[3072,1024]{1,0:T(8,128)}, bf16[72,3072]{1,0:T(8,128)(2,1)S(1)}, ...), condition=%wide.region_7.8_spmd.clone, body=%wide.region_6.7_spmd.clone.sunk | while | flops 239075328 | bytes 38077588 | solution.py:83
  250.4 10.6 %select_add_fusion.9 = f32[3072,1024]{1,0:T(8,128)} fusion(f32[3072,1024]{1,0:T(8,128)} %get-tuple-element.362, bf16[3072,1024]{1,0:T(8,128)(2,1)} %convolution_convert_fusion.10, pred[]{:T(512)S(6)} %compare.13), kind=kLoop, calls=%fused_computation.5.clone.1 | loop fusion | flops 9437184 | bytes 31457280 | tf_op jit(solution)/shard_map/while/body/add | solution.py:78
  265.6 14.2 %select_add_fusion.9 = f32[3072,1024]{1,0:T(8,128)} fusion(f32[3072,1024]{1,0:T(8,128)} %get-tuple-element.362, bf16[3072,1024]{1,0:T(8,128)(2,1)} %convolution_convert_fusion.10, pred[]{:T(512)S(6)} %compare.13), kind=kLoop, calls=%fused_computation.5.clone.1 | loop fusion | flops 9437184 | bytes 31457280 | tf_op jit(solution)/shard_map/while/body/add | solution.py:78
  279.8 34.2 %while.44 = (s32[]{:T(128)}, f32[3072,1024]{1,0:T(8,128)}, bf16[72,3072]{1,0:T(8,128)(2,1)S(1)}, bf16[72,1024]{1,0:T(8,128)(2,1)S(1)}, s32[]{:T(128)}, /*index=5*/s32[]{:T(128)}, s32[]{:T(128)}, s32[]{:T(128)}) while((s32[]{:T(128)}, f32[3072,1024]{1,0:T(8,128)}, bf16[72,3072]{1,0:T(8,128)(2,1)S(1)}, ...), condition=%wide.region_5.6_spmd.clone, body=%wide.region_4.5_spmd.clone.sunk | while | flops 239075328 | bytes 38077588 | solution.py:83
  284.3 10.8 %select_add_fusion.8 = f32[3072,1024]{1,0:T(8,128)} fusion(f32[3072,1024]{1,0:T(8,128)} %get-tuple-element.386, bf16[3072,1024]{1,0:T(8,128)(2,1)} %convolution_convert_fusion.9, pred[]{:T(512)S(6)} %compare.12), kind=kLoop, calls=%fused_computation.clone.1 | loop fusion | flops 9437184 | bytes 31457280 | tf_op jit(solution)/shard_map/while/body/add | solution.py:78
  299.6 14.4 %select_add_fusion.8 = f32[3072,1024]{1,0:T(8,128)} fusion(f32[3072,1024]{1,0:T(8,128)} %get-tuple-element.386, bf16[3072,1024]{1,0:T(8,128)(2,1)} %convolution_convert_fusion.9, pred[]{:T(512)S(6)} %compare.12), kind=kLoop, calls=%fused_computation.clone.1 | loop fusion | flops 9437184 | bytes 31457280 | tf_op jit(solution)/shard_map/while/body/add | solution.py:78
  314.0 26.4 %maximum_convert_fusion = bf16[4,3072,1024]{2,1,0:T(8,128)(2,1)} fusion(f32[1,3072,1024]{2,1,0:T(8,128)} %bitcast.108, f32[1,3072,1024]{2,1,0:T(8,128)} %bitcast.107, f32[1,3072,1024]{2,1,0:T(8,128)} %bitcast.106, f32[1,3072,1024]{2,1,0:T(8,128)} %bitcast.105), kind=kLoop, calls=%fused_computation.20 | loop fusion | flops 37748736 | bytes 75497472 | tf_op jit(solution)/shard_map/convert.1
  346.0 17.2 %fusion.64 = (bf16[4,3072,512]{2,1,0:T(8,128)(2,1)}, bf16[4,3072,512]{2,1,0:T(8,128)(2,1)}) fusion(bf16[4,3072,1024]{2,1,0:T(8,128)(2,1)} %maximum_convert_fusion), kind=kLoop, calls=%fused_computation.103 | loop fusion | bytes 50331648 | tf_op jit(solution)/shard_map/slice | solution.py:118
  (98 shorter events, 102.8 us)
Async XLA Ops:
  7.9 64.9 %copy-start.15 = (pred[8,64]{1,0:T(8,128)(4,1)}, pred[8,64]{1,0:T(8,128)(4,1)S(1)}, u32[]{:S(2)}) copy-start(pred[8,64]{1,0:T(8,128)(4,1)S(1)} %compare_bitcast_fusion) | copy-start | bytes 1540
  33.8 39.1 %copy-start.13 = (s32[8,64]{1,0:T(8,128)}, s32[8,64]{1,0:T(8,128)S(1)}, u32[]{:S(2)}) copy-start(s32[8,64]{1,0:T(8,128)S(1)} %copy.38) | copy-start | bytes 6148
  35.7 37.2 %all-to-all-start.1 = ((bf16[8,36,3072]{2,1,0:T(8,128)(2,1)}), bf16[8,36,3072]{2,1,0:T(8,128)(2,1)S(1)}, u32[]{:S(2)}, u32[]{:S(2)}) async-start(bf16[8,36,3072]{2,1,0:T(8,128)(2,1)} %convolution_convert_fusion.4), calls=%async_computation.1 | async-start | bytes 3932160 | tf_op jit(solution)/shard_map/all_to_all | solution.py:99
  72.9 29.2 %all-to-all-start = ((bf16[8,36,3072]{2,1,0:T(8,128)(2,1)}), bf16[8,36,3072]{2,1,0:T(8,128)(2,1)}, u32[]{:S(2)}, u32[]{:S(2)}) async-start(bf16[8,36,3072]{2,1,0:T(8,128)(2,1)} %fusion.20), calls=%async_computation | async-start | bytes 3932160 | tf_op jit(solution)/shard_map/all_to_all | solution.py:100
  77.6 262.7 %reduce-scatter.4.cloned.1.call-start = ((), (), s32[]{:S(2)}) async-start(), calls=%async_computation.4 | async-start | bytes 5013504
  88.9 30.6 %copy-start.6 = (bf16[72,3072]{1,0:T(8,128)(2,1)}, bf16[72,3072]{1,0:T(8,128)(2,1)S(1)}, u32[]{:S(2)}) copy-start(bf16[72,3072]{1,0:T(8,128)(2,1)S(1)} %squeeze.66) | copy-start | bytes 1327108
  120.3 14.5 %copy-start.4 = (bf16[72,3072]{1,0:T(8,128)(2,1)}, bf16[72,3072]{1,0:T(8,128)(2,1)S(1)}, u32[]{:S(2)}) copy-start(bf16[72,3072]{1,0:T(8,128)(2,1)S(1)} %squeeze.62) | copy-start | bytes 1327108
  134.9 13.7 %copy-start.2 = (bf16[72,3072]{1,0:T(8,128)(2,1)}, bf16[72,3072]{1,0:T(8,128)(2,1)S(1)}, u32[]{:S(2)}) copy-start(bf16[72,3072]{1,0:T(8,128)(2,1)S(1)} %squeeze.58) | copy-start | bytes 1327108
  148.7 12.4 %copy-start = (bf16[72,3072]{1,0:T(8,128)(2,1)}, bf16[72,3072]{1,0:T(8,128)(2,1)S(1)}, u32[]{:S(2)}) copy-start(bf16[72,3072]{1,0:T(8,128)(2,1)S(1)} %squeeze.54) | copy-start | bytes 1327108
  152.9 8.8 %copy-start.12 = (f32[1,72,3072]{2,1,0:T(8,128)S(1)}, f32[1,72,3072]{2,1,0:T(8,128)}, u32[]{:S(2)}) copy-start(f32[1,72,3072]{2,1,0:T(8,128)} %fusion.23) | copy-start | bytes 2654212
  168.0 7.8 %copy-start.7 = (bf16[72,3072]{1,0:T(8,128)(2,1)S(1)}, bf16[72,3072]{1,0:T(8,128)(2,1)}, u32[]{:S(2)}) copy-start(bf16[72,3072]{1,0:T(8,128)(2,1)} %copy-done.6) | copy-start | bytes 1327108
  168.0 7.8 %copy-start.11 = (bf16[72,1024]{1,0:T(8,128)(2,1)S(1)}, bf16[72,1024]{1,0:T(8,128)(2,1)}, u32[]{:S(2)}) copy-start(bf16[72,1024]{1,0:T(8,128)(2,1)} %pad_maximum_fusion.4) | copy-start | bytes 442372
  175.8 35.1 %copy-start.5 = (bf16[72,3072]{1,0:T(8,128)(2,1)S(1)}, bf16[72,3072]{1,0:T(8,128)(2,1)}, u32[]{:S(2)}) copy-start(bf16[72,3072]{1,0:T(8,128)(2,1)} %copy-done.4) | copy-start | bytes 1327108
  175.8 35.1 %copy-start.10 = (bf16[72,1024]{1,0:T(8,128)(2,1)S(1)}, bf16[72,1024]{1,0:T(8,128)(2,1)}, u32[]{:S(2)}) copy-start(bf16[72,1024]{1,0:T(8,128)(2,1)} %pad_maximum_fusion.3) | copy-start | bytes 442372
  210.8 34.8 %copy-start.3 = (bf16[72,3072]{1,0:T(8,128)(2,1)S(1)}, bf16[72,3072]{1,0:T(8,128)(2,1)}, u32[]{:S(2)}) copy-start(bf16[72,3072]{1,0:T(8,128)(2,1)} %copy-done.2) | copy-start | bytes 1327108
  210.9 34.8 %copy-start.9 = (bf16[72,1024]{1,0:T(8,128)(2,1)S(1)}, bf16[72,1024]{1,0:T(8,128)(2,1)}, u32[]{:S(2)}) copy-start(bf16[72,1024]{1,0:T(8,128)(2,1)} %pad_maximum_fusion.2) | copy-start | bytes 442372
  245.6 34.2 %copy-start.1 = (bf16[72,3072]{1,0:T(8,128)(2,1)S(1)}, bf16[72,3072]{1,0:T(8,128)(2,1)}, u32[]{:S(2)}) copy-start(bf16[72,3072]{1,0:T(8,128)(2,1)} %copy-done) | copy-start | bytes 1327108
  245.6 34.2 %copy-start.8 = (bf16[72,1024]{1,0:T(8,128)(2,1)S(1)}, bf16[72,1024]{1,0:T(8,128)(2,1)}, u32[]{:S(2)}) copy-start(bf16[72,1024]{1,0:T(8,128)(2,1)} %pad_maximum_fusion.1) | copy-start | bytes 442372
  342.5 20.7 %all-to-all-start.2 = ((f32[4,72,192]{2,0,1:T(4,128)}), f32[4,72,192]{2,0,1:T(4,128)S(1)}, u32[]{:S(2)}, u32[]{:S(2)}) async-start(f32[4,72,192]{2,0,1:T(4,128)} %copy.43), calls=%async_computation.2 | async-start | bytes 589824 | tf_op jit(solution)/shard_map/all_to_all | solution.py:112
  346.0 17.3 %copy-start.14 = (s32[8,64]{1,0:T(8,128)S(1)}, s32[8,64]{1,0:T(8,128)}, u32[]{:S(2)}) copy-start(s32[8,64]{1,0:T(8,128)} %copy-done.13) | copy-start | bytes 6148
  346.0 17.3 %copy-start.16 = (pred[8,64]{1,0:T(8,128)(4,1)S(1)}, pred[8,64]{1,0:T(8,128)(4,1)}, u32[]{:S(2)}) copy-start(pred[8,64]{1,0:T(8,128)(4,1)} %copy-done.15) | copy-start | bytes 1540
Sparse Core Ops, SparseCore 0:
  175.9 73.1 reduce-scatter.3
where the time goes:
time: 376 us; the launch traced here: 372 us
  other arithmetic  134 us (36%)
  matrix products  93 us (25%)
  local copies, waits for them, and re-layouts  60.4 us (16%)
  blocking collectives  43.9 us (12%)
  between operations  14.8 us (4%)
  waiting for transfers between devices  13.2 us (4%)
  starting transfers between devices  12 us (3%)
    add x8, other arithmetic, accumulate(): running + lax.optimization_barrier(partial_sum.astype(jnp.bfloat16)).asty...  102 us
    dot_general x8, matrix products, accumulate(): lax.dot_general(piece_inputs, piece_grads, (((0,), (0,)), ((), ())), pref...  36.2 us
    another operation x1, other arithmetic  26.4 us
    unnamed x40, local copies, waits for them, and re-layouts  25.2 us
    all_gather x1, blocking collectives, body(): lax.all_gather(tokens, 'shard', axis=1, tiled=True)  24.8 us
    dot_general x4, matrix products, slot_grads(): lax.dot_general(stacked, paired, (((1,), (1,)), ((), ())), preferred_elem...  22.1 us
    all_gather x1, blocking collectives, body(): lax.all_gather(cotangent, 'shard', axis=1, tiled=True)  19.1 us
    slice x1, local copies, waits for them, and re-layouts, body(): grad_up = stacked_totals[:, :, hidden_width:].astype(jnp.bfloat16)  17.2 us
  transfers between devices with their start and end apart: 4, of which 1 were waited for; matrix products, arithmetic and copies ran while one was open for 56% of the time, Pallas kernels for 0%

commit v1 on v0

v1 whole, which is shorter than its diff:
```python
import jax
import jax.numpy as jnp
from jax import lax
from jax.experimental import pallas as pl
from jax.experimental.pallas import tpu as pltpu
from jax.sharding import PartitionSpec as P

BF = jnp.bfloat16
F32 = jnp.float32
BOTH = ("group", "shard")
MIB = 1 << 20
VM = pl.BlockSpec(memory_space=pltpu.VMEM)
SM = pl.BlockSpec(memory_space=pltpu.SMEM)


def dot(a, b, da, db):
    return lax.dot_general(a, b, (((da,), (db,)), ((), ())), preferred_element_type=F32)


def bits_of(size):
    return size.bit_length() - 1


def stage_masks(groups, shards):
    masks = [1 << k for k in range(bits_of(shards) - 1, 0, -1)] + [shards << k for k in range(bits_of(groups))]
    other = masks[:-2] + masks[-2:][::-1]
    return other, masks


def swap(x, groups, shards, masks):
    pairs = [(i, i ^ masks[i & 1]) for i in range(groups * shards)]
    return lax.ppermute(x, BOTH, pairs)


def relative(index, masks, top_first):
    count = len(masks)
    out = 0
    for step, mask in enumerate(masks):
        place = count - 1 - step if top_first else step
        out = out | (((index >> bits_of(mask)) & 1) << place)
    return out


def forward_kernel(gather_masks, scatter_masks, groups, shards, experts,
                   place, own0, own1, oth0, oth1, routes, wg, wu, wd,
                   full, grads, keep, send, x, q, coef, total):
    half = own0.shape[0]
    rows, width = own0.shape[1], own0.shape[2]
    tokens = groups * rows
    hidden = wg.shape[2]
    core = place[0]
    group = place[1]

    def assemble(out, low, high, masks, start):
        for g in range(groups):
            for pair in range(shards // 2):
                r = relative(g * shards + pair * 2, masks, False) ^ start
                into = (pl.ds(g * rows, rows), pl.ds(pair * width, width))

                @pl.when(r < half)
                def _():
                    out[into] = low[jnp.minimum(r, half - 1)]

                @pl.when(r >= half)
                def _():
                    out[into] = high[jnp.maximum(r - half, 0)]

    @pl.when(core == 0)
    def _():
        assemble(x, own0, own1, gather_masks[0], place[2])
        assemble(q, oth0, oth1, gather_masks[1], place[3])

    @pl.when(core == 1)
    def _():
        assemble(x, oth0, oth1, gather_masks[0], place[2])
        assemble(q, own0, own1, gather_masks[1], place[3])

    full[...] = x[...]
    for g in range(groups):
        table = routes[g ^ group].T
        for e in range(experts):
            number = (group * experts + e).astype(F32)
            value = jnp.where(table[:, 0:1] == number, table[:, 2:3], 0.0) + jnp.where(table[:, 1:2] == number, table[:, 3:4], 0.0)
            coef[e, g * rows:(g + 1) * rows, :] = value

    @pl.loop(0, experts)
    def _(e):
        gate_pre = dot(x[...], wg[e], 1, 0)
        up_value = dot(x[...], wu[e], 1, 0)
        hidden_grad = dot(q[...], wd[e], 1, 1) * coef[e]
        s = 1.0 / (1.0 + jnp.exp(-gate_pre))
        gate_grad = (hidden_grad * up_value * s * (1.0 + gate_pre * (1.0 - s))).astype(BF)
        up_grad = (hidden_grad * (gate_pre * s)).astype(BF)
        grads[e, :, :hidden] = gate_grad
        grads[e, :, hidden:] = up_grad
        part = dot(gate_grad, wg[e], 1, 1) + dot(up_grad, wu[e], 1, 1)

        @pl.when(e == 0)
        def _():
            total[...] = part

        @pl.when(e > 0)
        def _():
            total[...] += part

    part_rows = rows // 2
    for g in range(groups):
        for pair in range(shards // 2):
            at = g * shards + pair * 2
            first = relative(at, scatter_masks[0], True) ^ place[4]
            second = relative(at, scatter_masks[1], True) ^ place[5]
            columns = pl.ds(pair * width, width)
            upper = total[g * rows:g * rows + part_rows, columns]
            lower = total[g * rows + part_rows:(g + 1) * rows, columns]

            @pl.when(core == 0)
            def _():
                keep[first] = upper
                send[second] = lower

            @pl.when(core == 1)
            def _():
                keep[second] = lower
                send[first] = upper


def weight_kernel(xt, grads, *rest):
    out_gate, out_up = rest[-2:]
    hidden = out_gate.shape[2]
    block = out_gate.shape[1]
    rows = xt[pl.ds(pl.program_id(0) * block, block), :]
    out_gate[0] = dot(rows, grads[0, :, :hidden], 1, 0).astype(BF)
    out_up[0] = dot(rows, grads[0, :, hidden:], 1, 0).astype(BF)


def weight_grads(xt, grads, expert, so_far, shape):
    features, tokens = xt.shape
    steps = 2
    block = features // steps
    out = jax.ShapeDtypeStruct(shape, BF)
    out_spec = pl.BlockSpec((1, block, shape[2]), lambda j: (expert, j, 0))
    aliases = {2: 0, 3: 1} if so_far else {}
    return pl.pallas_call(
        weight_kernel,
        grid=(steps,),
        out_shape=(out, out),
        in_specs=[
            pl.BlockSpec((features, tokens), lambda j: (0, 0)),
            pl.BlockSpec((1,) + grads.shape[1:], lambda j: (expert, 0, 0)),
        ] + [pl.BlockSpec(memory_space=pl.ANY)] * len(so_far),
        out_specs=(out_spec, out_spec),
        input_output_aliases=aliases,
        compiler_params=pltpu.CompilerParams(vmem_limit_bytes=24 * MIB),
        cost_estimate=pl.CostEstimate(flops=4 * features * tokens * shape[2], bytes_accessed=4 * features * shape[2], transcendentals=0),
        name="weight_grads",
    )(xt, grads, *so_far)


def body(tokens, cotangent, expert_ids, route_weight, w_gate, w_up, w_down):
    groups, shards = lax.axis_size("group"), lax.axis_size("shard")
    group, shard = lax.axis_index("group"), lax.axis_index("shard")
    experts, features, hidden = w_gate.shape
    rows, width = tokens.shape
    core = shard & 1
    me = group * shards + shard
    gather_masks = stage_masks(groups, shards)
    scatter_masks = tuple(m[::-1] for m in gather_masks)
    first = core == 0
    mine, theirs = jnp.where(first, tokens, cotangent), jnp.where(first, cotangent, tokens)
    got = swap(theirs, groups, shards, (1, 1))
    block = jnp.where(first, jnp.concatenate([mine, got], 1), jnp.concatenate([got, mine], 1))[None]
    routes = jnp.concatenate([expert_ids.astype(F32).T, route_weight.T, jnp.zeros((4, rows), F32)], 0)[None]
    for k in range(bits_of(groups)):
        routes = jnp.concatenate([routes, swap(routes, groups, shards, (shards << k,) * 2)], 0)
    count = len(gather_masks[0])
    for step in range(count - 1):
        block = jnp.concatenate([block, swap(block, groups, shards, (gather_masks[0][step], gather_masks[1][step]))], 0)
    low = block
    high = swap(low, groups, shards, (gather_masks[0][-1], gather_masks[1][-1]))
    other_low = swap(low, groups, shards, (1, 1))
    other_high = swap(high, groups, shards, (1, 1))
    place = jnp.stack([core, group, relative(me, gather_masks[0], False), relative(me, gather_masks[1], False),
                       relative(me, scatter_masks[0], True), relative(me, scatter_masks[1], True)]).astype(jnp.int32)
    pairs = groups * shards // 2
    total_rows = groups * rows
    in_vmem = [pltpu.with_memory_space_constraint(w, pltpu.VMEM) for w in (w_gate, w_up, w_down)]
    piece = jax.ShapeDtypeStruct((pairs, rows // 2, 2 * width), F32)

    def forward(*refs):
        forward_kernel(gather_masks, scatter_masks, groups, shards, experts, *refs)

    full, grads, keep, send = pl.pallas_call(
        forward,
        out_shape=(jax.ShapeDtypeStruct((total_rows, features), BF), jax.ShapeDtypeStruct((experts, total_rows, 2 * hidden), BF), piece, piece),
        in_specs=[SM] + [VM] * 8,
        out_specs=(VM,) * 4,
        scratch_shapes=[pltpu.VMEM((total_rows, features), BF), pltpu.VMEM((total_rows, features), BF),
                        pltpu.VMEM((experts, total_rows, 1), F32), pltpu.VMEM((total_rows, features), F32)],
        compiler_params=pltpu.CompilerParams(vmem_limit_bytes=20 * MIB),
        name="forward",
    )(place, low, high, other_low, other_high, routes, *in_vmem)

    xt = full.T
    so_far = ()
    for e in range(experts):
        so_far = weight_grads(xt, grads, e, so_far, w_gate.shape)

    kept = keep + swap(send, groups, shards, (1, 1))
    for step in range(count):
        half = kept.shape[0] // 2
        sent = kept[half:]
        if 2 * step < count:
            sent = sent.astype(BF)
        kept = kept[:half] + swap(sent, groups, shards, (scatter_masks[0][step], scatter_masks[1][step])).astype(F32)
    done = kept[0].astype(BF)
    left, right = done[:, :width], done[:, width:]
    got = swap(jnp.where(first, right, left), groups, shards, (1, 1))
    stay = jnp.where(first, left, right)
    grad_tokens = jnp.where(first, jnp.concatenate([stay, got], 0), jnp.concatenate([got, stay], 0))
    return grad_tokens, so_far[0], so_far[1]


def solution(mesh):
    in_specs = (
        P("group", "shard"),
        P("group", "shard"),
        P("group", None),
        P("group", None),
        P("group", None, "shard"),
        P("group", None, "shard"),
        P("group", "shard", None),
    )
    out_specs = (P("group", "shard"), P("group", None, "shard"), P("group", None, "shard"))
    return jax.shard_map(body, mesh=mesh, in_specs=in_specs, out_specs=out_specs, check_vma=False)
```

time: 376 us -> 105 us (0.28); the launches traced: 372 us -> 105 us
  other arithmetic: 134 us -> 5.03 us
  matrix products: 93 us -> 0 us
  blocking collectives: 43.9 us -> 0 us
  local copies, waits for them, and re-layouts: 60.4 us -> 18.7 us
  Pallas kernels: 0 us -> 35.1 us
  between operations: 14.8 us -> 0.78 us
  waiting for transfers between devices: 13.2 us -> 24.1 us
  starting transfers between devices: 12 us -> 21.3 us
    add x8 -> x4, other arithmetic: 102 us -> 1.31 us  [the longest x1 1.23 us: body(): kept = keep + swap(send, groups, shards, (1, 1))]
    dot_general x24 -> x0, matrix products: 93 us -> none  [the longest x8 36.2 us: accumulate(): lax.dot_general(piece_inputs, piece_grads, (((0,), (0,)), ((), ())), pref...]
    all_gather x2 -> x0, blocking collectives: 43.9 us -> none  [the longest x1 24.8 us: body(): lax.all_gather(tokens, 'shard', axis=1, tiled=True)]
    pallas_call x0 -> x5, Pallas kernels: none -> 35.1 us  [the longest x1 20.9 us: body(): pl.pallas_call(forward, out_shape=(jax.ShapeDtypeStruct((total_rows, feat...]
    another operation x3 -> x0, other arithmetic: 28.2 us -> none
    ppermute x0 -> x14, waiting for transfers between devices: none -> 24.1 us  [swap(): return lax.ppermute(x, BOTH, pairs)]
    ppermute x0 -> x14, starting transfers between devices: none -> 21.3 us  [swap(): return lax.ppermute(x, BOTH, pairs)]
    slice x3 -> x4, local copies, waits for them, and re-layouts: 18.2 us -> 0.05 us  [body(): sent = kept[half:]]
  transfers between devices with their start and end apart: 4 -> 14, of which waited for: 1 -> 9; matrix products, arithmetic and copies ran while one was open for 56% -> 4% of each run, Pallas kernels for 0% -> 13%
where the time goes in v1:
time: 105 us
  Pallas kernels  35.1 us (33%)
  waiting for transfers between devices  24.1 us (23%)
  starting transfers between devices  21.3 us (20%)
  local copies, waits for them, and re-layouts  18.7 us (18%)
  other arithmetic  5.03 us (5%)
    ppermute x14, waiting for transfers between devices, swap(): return lax.ppermute(x, BOTH, pairs)  24.1 us
    ppermute x14, starting transfers between devices, swap(): return lax.ppermute(x, BOTH, pairs)  21.3 us
    pallas_call x1, Pallas kernels, body(): pl.pallas_call(forward, out_shape=(jax.ShapeDtypeStruct((total_rows, feat...  20.9 us
    unnamed x16, local copies, waits for them, and re-layouts  16.4 us
    pallas_call x4, Pallas kernels, weight_grads(): pl.pallas_call(weight_kernel, grid=(steps,), out_shape=(out, out), in_spe...  14.1 us
  transfers between devices with their start and end apart: 14, of which 9 were waited for; matrix products, arithmetic and copies ran while one was open for 4% of the time, Pallas kernels for 13%

profile of v1, /device:TPU:0, one launch (start us, length us, event | category | flops | bytes accessed | tf_op | source)
XLA Modules:
  0.0 105.0 jit_solution(11664402511482919106)
XLA Ops:
  2.9 4.0 %collective-permute-start.1 = (bf16[1,64,384]{2,1,0:T(8,128)(2,1)S(1)}, bf16[1,64,384]{2,1,0:T(8,128)(2,1)S(1)}, u32[]{:S(2)}, u32[]{:S(2)}) collective-permute-start(bf16[1,64,384]{2,1,0:T(8,128)(2,1)S(1)} %maximum_select_fusion), channel_id=1, source_target_pairs={{0,8},{1,9},{2,10},{3,11},{4,12},{5,13},{6,14},{7,15},{8,0},{9,1},... | collective-permute-start | bytes 147464 | tf_op jit(solution)/shard_map/ppermute | solution.py:32
  6.9 2.1 %collective-permute-done.1 = bf16[1,64,384]{2,1,0:T(8,128)(2,1)S(1)} collective-permute-done((bf16[1,64,384]{2,1,0:T(8,128)(2,1)S(1)}, bf16[1,64,384]{2,1,0:T(8,128)(2,1)S(1)}, u32[]{:S(2)}, u32[]{:S(2)}) %collective-permute-start.1) | collective-permute-done | bytes 49184 | tf_op jit(solution)/shard_map/ppermute | solution.py:32
  9.0 2.0 %collective-permute-start.2 = (bf16[2,64,384]{2,1,0:T(8,128)(2,1)S(1)}, bf16[2,64,384]{2,1,0:T(8,128)(2,1)S(1)}, u32[]{:S(2)}, u32[]{:S(2)}) collective-permute-start(bf16[2,64,384]{2,1,0:T(8,128)(2,1)S(1)} %pad_maximum_fusion.2), channel_id=1, source_target_pairs={{0,4},{1,5},{2,6},{3,7},{4,0},{5,1},{6,2},{7,3},{8,12},{9,13},{10,... | collective-permute-start | bytes 294920 | tf_op jit(solution)/shard_map/ppermute | solution.py:32
  10.9 2.7 %collective-permute-done.2 = bf16[2,64,384]{2,1,0:T(8,128)(2,1)S(1)} collective-permute-done((bf16[2,64,384]{2,1,0:T(8,128)(2,1)S(1)}, bf16[2,64,384]{2,1,0:T(8,128)(2,1)S(1)}, u32[]{:S(2)}, u32[]{:S(2)}) %collective-permute-start.2) | collective-permute-done | bytes 98336 | tf_op jit(solution)/shard_map/ppermute | solution.py:32
  13.7 2.9 %collective-permute-start.3 = (bf16[4,64,384]{2,1,0:T(8,128)(2,1)S(1)}, bf16[4,64,384]{2,1,0:T(8,128)(2,1)S(1)}, u32[]{:S(2)}, u32[]{:S(2)}) collective-permute-start(bf16[4,64,384]{2,1,0:T(8,128)(2,1)S(1)} %pad_maximum_fusion.1), channel_id=1, source_target_pairs={{0,16},{1,3},{2,18},{3,1},{4,20},{5,7},{6,22},{7,5},{8,24},{9,11},... | collective-permute-start | bytes 589832 | tf_op jit(solution)/shard_map/ppermute | solution.py:32
  16.6 4.4 %collective-permute-done.3 = bf16[4,64,384]{2,1,0:T(8,128)(2,1)S(1)} collective-permute-done((bf16[4,64,384]{2,1,0:T(8,128)(2,1)S(1)}, bf16[4,64,384]{2,1,0:T(8,128)(2,1)S(1)}, u32[]{:S(2)}, u32[]{:S(2)}) %collective-permute-start.3) | collective-permute-done | bytes 196640 | tf_op jit(solution)/shard_map/ppermute | solution.py:32
  21.1 2.6 %collective-permute-start.4 = (bf16[8,64,384]{2,1,0:T(8,128)(2,1)S(1)}, bf16[8,64,384]{2,1,0:T(8,128)(2,1)S(1)}, u32[]{:S(2)}, u32[]{:S(2)}) collective-permute-start(bf16[8,64,384]{2,1,0:T(8,128)(2,1)S(1)} %pad_maximum_fusion.refs_1_), channel_id=1, source_target_pairs={{0,2},{1,17},{2,0},{3,19},{4,6},{5,21},{6,4},{7,23},{8,10},{9,25},... | collective-permute-start | bytes 1179656 | tf_op jit(solution)/shard_map/ppermute | solution.py:32
  23.7 5.8 %collective-permute-done.4.refs_2_ = bf16[8,64,384]{2,1,0:T(8,128)(2,1)S(1)} collective-permute-done((bf16[8,64,384]{2,1,0:T(8,128)(2,1)S(1)}, bf16[8,64,384]{2,1,0:T(8,128)(2,1)S(1)}, u32[]{:S(2)}, u32[]{:S(2)}) %collective-permute-start.4) | collective-permute-done | bytes 393248 | tf_op jit(solution)/shard_map/ppermute | solution.py:32
  31.0 2.0 %collective-permute-start.7 = (f32[1,8,64]{2,1,0:T(8,128)S(1)}, f32[1,8,64]{2,1,0:T(8,128)S(1)}, u32[]{:S(2)}, u32[]{:S(2)}) collective-permute-start(f32[1,8,64]{2,1,0:T(8,128)S(1)} %maximum_bitcast_fusion), channel_id=1, source_target_pairs={{0,16},{1,17},{2,18},{3,19},{4,20},{5,21},{6,22},{7,23},{8,24},{9,... | collective-permute-start | bytes 6152 | tf_op jit(solution)/shard_map/ppermute | solution.py:32
  36.7 4.6 %copy-done = bf16[4,3072,512]{2,1,0:T(8,128)(2,1)S(1)} copy-done((bf16[4,3072,512]{2,1,0:T(8,128)(2,1)S(1)}, bf16[4,3072,512]{2,1,0:T(8,128)(2,1)}, u32[]{:S(2)}) %copy-start) | copy-done | bytes 12582936
  41.3 4.6 %copy-done.1 = bf16[4,3072,512]{2,1,0:T(8,128)(2,1)S(1)} copy-done((bf16[4,3072,512]{2,1,0:T(8,128)(2,1)S(1)}, bf16[4,3072,512]{2,1,0:T(8,128)(2,1)}, u32[]{:S(2)}) %copy-start.1) | copy-done | bytes 12582936
  45.9 4.6 %copy-done.2 = bf16[4,512,3072]{2,1,0:T(8,128)(2,1)S(1)} copy-done((bf16[4,512,3072]{2,1,0:T(8,128)(2,1)S(1)}, bf16[4,512,3072]{2,1,0:T(8,128)(2,1)}, u32[]{:S(2)}) %copy-start.2) | copy-done | bytes 12582936
  50.4 20.9 %forward.1 = (bf16[128,3072]{1,0:T(8,128)(2,1)}, bf16[4,128,1024]{2,1,0:T(8,128)(2,1)}, f32[16,32,384]{2,1,0:T(8,128)}, f32[16,32,384]{2,1,0:T(8,128)}) custom-call(s32[6]{0:T(128)} %stack.27.refs_0_, bf16[8,64,384]{2,1,0:T(8,128)(2,1)} %copy-done.4, bf16[8,64,384]{2,1,0:T(8,128)(2,1)} %copy-done.5, bf16[8,64,384]{2,1,0:T(8,128)(2,1)} %copy-done.6, ...), custom_call_target="tpu_custom_call" | custom-call | tf_op jit(solution)/shard_map/forward/pallas_call | solution.py:192
  71.4 2.5 %collective-permute-done.8 = f32[16,32,384]{2,1,0:T(8,128)S(1)} collective-permute-done((f32[16,32,384]{2,1,0:T(8,128)}, f32[16,32,384]{2,1,0:T(8,128)S(1)}, u32[]{:S(2)}, u32[]{:S(2)}) %collective-permute-start.8) | collective-permute-done | bytes 786464 | tf_op jit(solution)/shard_map/ppermute | solution.py:32
  73.9 1.2 %add.19 = f32[16,32,384]{2,1,0:T(8,128)S(1)} add(f32[16,32,384]{2,1,0:T(8,128)} %get-tuple-element.15, f32[16,32,384]{2,1,0:T(8,128)S(1)} %collective-permute-done.8) | non-fusion elementwise | flops 196608 | bytes 2359296 | tf_op jit(solution)/shard_map/add | solution.py:208
  75.1 2.1 %collective-permute-start.9 = (bf16[8,32,384]{2,1,0:T(8,128)(2,1)S(1)}, bf16[8,32,384]{2,1,0:T(8,128)(2,1)S(1)}, u32[]{:S(2)}, u32[]{:S(2)}) collective-permute-start(bf16[8,32,384]{2,1,0:T(8,128)(2,1)S(1)} %slice.66), channel_id=1, source_target_pairs={{0,2},{1,17},{2,0},{3,19},{4,6},{5,21},{6,4},{7,23},{8,10},{9,25},... | collective-permute-start | bytes 589832 | tf_op jit(solution)/shard_map/ppermute | solution.py:32
  77.2 3.7 %collective-permute-done.9 = bf16[8,32,384]{2,1,0:T(8,128)(2,1)S(1)} collective-permute-done((bf16[8,32,384]{2,1,0:T(8,128)(2,1)S(1)}, bf16[8,32,384]{2,1,0:T(8,128)(2,1)S(1)}, u32[]{:S(2)}, u32[]{:S(2)}) %collective-permute-start.9) | collective-permute-done | bytes 196640 | tf_op jit(solution)/shard_map/ppermute | solution.py:32
  81.0 2.1 %collective-permute-start.10 = (bf16[4,32,384]{2,1,0:T(8,128)(2,1)S(1)}, bf16[4,32,384]{2,1,0:T(8,128)(2,1)S(1)}, u32[]{:S(2)}, u32[]{:S(2)}) collective-permute-start(bf16[4,32,384]{2,1,0:T(8,128)(2,1)S(1)} %slice.67), channel_id=1, source_target_pairs={{0,16},{1,3},{2,18},{3,1},{4,20},{5,7},{6,22},{7,5},{8,24},{9,11},... | collective-permute-start | bytes 294920 | tf_op jit(solution)/shard_map/ppermute | solution.py:32
  83.0 1.5 %copy.16 = bf16[128,3072]{0,1:T(8,128)(2,1)S(1)} copy(bf16[128,3072]{1,0:T(8,128)(2,1)} %get-tuple-element.17) | data formatting | bytes 1572864 | tf_op jit(solution)/shard_map/forward/pallas_call | solution.py:192
  87.0 3.5 %weight_grads.4 = (bf16[4,3072,512]{2,1,0:T(8,128)(2,1)}, bf16[4,3072,512]{2,1,0:T(8,128)(2,1)}) custom-call(bf16[3072,128]{1,0:T(8,128)(2,1)S(1)} %bitcast.17, bf16[4,128,1024]{2,1,0:T(8,128)(2,1)S(1)} %copy-done.3), custom_call_target="tpu_custom_call" | custom-call | flops 805306368 | bytes 6291456 | tf_op jit(solution)/shard_map/weight_grads/pallas_call | solution.py:143
  90.5 3.5 %weight_grads.5 = (bf16[4,3072,512]{2,1,0:T(8,128)(2,1)}, bf16[4,3072,512]{2,1,0:T(8,128)(2,1)}) custom-call(bf16[3072,128]{1,0:T(8,128)(2,1)S(1)} %bitcast.18, bf16[4,128,1024]{2,1,0:T(8,128)(2,1)S(1)} %copy-done.3, bf16[4,3072,512]{2,1,0:T(8,128)(2,1)} %get-tuple-element.19.rest_0_, ...), custom_call_target="tpu_custom_call", output_to_operand_aliasing={{0}: (2, {}), {1}: (3, {})} | custom-call | flops 805306368 | bytes 6291456 | tf_op jit(solution)/shard_map/weight_grads/pallas_call | solution.py:143
  94.1 3.1 %collective-permute-start.12 = (f32[1,32,384]{2,1,0:T(8,128)S(1)}, f32[1,32,384]{2,1,0:T(8,128)S(1)}, u32[]{:S(2)}, u32[]{:S(2)}) collective-permute-start(f32[1,32,384]{2,1,0:T(8,128)S(1)} %slice.49), channel_id=1, source_target_pairs={{0,8},{1,9},{2,10},{3,11},{4,12},{5,13},{6,14},{7,15},{8,0},{9,1},... | collective-permute-start | bytes 147464 | tf_op jit(solution)/shard_map/ppermute | solution.py:32
  97.1 3.5 %weight_grads.6 = (bf16[4,3072,512]{2,1,0:T(8,128)(2,1)}, bf16[4,3072,512]{2,1,0:T(8,128)(2,1)}) custom-call(bf16[3072,128]{1,0:T(8,128)(2,1)S(1)} %bitcast.19, bf16[4,128,1024]{2,1,0:T(8,128)(2,1)S(1)} %copy-done.3, bf16[4,3072,512]{2,1,0:T(8,128)(2,1)} %get-tuple-element.21.rest_0_, ...), custom_call_target="tpu_custom_call", output_to_operand_aliasing={{0}: (2, {}), {1}: (3, {})} | custom-call | flops 805306368 | bytes 6291456 | tf_op jit(solution)/shard_map/weight_grads/pallas_call | solution.py:143
  100.8 3.6 %weight_grads.7 = (bf16[4,3072,512]{2,1,0:T(8,128)(2,1)}, bf16[4,3072,512]{2,1,0:T(8,128)(2,1)}) custom-call(bf16[3072,128]{1,0:T(8,128)(2,1)S(1)} %bitcast.20, bf16[4,128,1024]{2,1,0:T(8,128)(2,1)S(1)} %copy-done.3, bf16[4,3072,512]{2,1,0:T(8,128)(2,1)} %get-tuple-element.23.rest_0_, ...), custom_call_target="tpu_custom_call", output_to_operand_aliasing={{0}: (2, {}), {1}: (3, {})} | custom-call | flops 805306368 | bytes 6291456 | tf_op jit(solution)/shard_map/weight_grads/pallas_call | solution.py:143
  (48 shorter events, 10.9 us)
Async XLA Ops:
  1.4 1.4 %collective-permute-start = (bf16[64,192]{1,0:T(8,128)(2,1)S(1)}, bf16[64,192]{1,0:T(8,128)(2,1)S(1)}, u32[]{:S(2)}, u32[]{:S(2)}) collective-permute-start(bf16[64,192]{1,0:T(8,128)(2,1)S(1)} %get-tuple-element.28), channel_id=1, source_target_pairs={{0,1},{1,0},{2,3},{3,2},{4,5},{5,4},{6,7},{7,6},{8,9},{9,8},{10,11... | collective-permute-start | bytes 73736 | tf_op jit(solution)/shard_map/ppermute | solution.py:32
  2.9 6.1 %collective-permute-start.1 = (bf16[1,64,384]{2,1,0:T(8,128)(2,1)S(1)}, bf16[1,64,384]{2,1,0:T(8,128)(2,1)S(1)}, u32[]{:S(2)}, u32[]{:S(2)}) collective-permute-start(bf16[1,64,384]{2,1,0:T(8,128)(2,1)S(1)} %maximum_select_fusion), channel_id=1, source_target_pairs={{0,8},{1,9},{2,10},{3,11},{4,12},{5,13},{6,14},{7,15},{8,0},{9,1},... | collective-permute-start | bytes 147464 | tf_op jit(solution)/shard_map/ppermute | solution.py:32
  9.0 4.7 %collective-permute-start.2 = (bf16[2,64,384]{2,1,0:T(8,128)(2,1)S(1)}, bf16[2,64,384]{2,1,0:T(8,128)(2,1)S(1)}, u32[]{:S(2)}, u32[]{:S(2)}) collective-permute-start(bf16[2,64,384]{2,1,0:T(8,128)(2,1)S(1)} %pad_maximum_fusion.2), channel_id=1, source_target_pairs={{0,4},{1,5},{2,6},{3,7},{4,0},{5,1},{6,2},{7,3},{8,12},{9,13},{10,... | collective-permute-start | bytes 294920 | tf_op jit(solution)/shard_map/ppermute | solution.py:32
  13.7 7.4 %collective-permute-start.3 = (bf16[4,64,384]{2,1,0:T(8,128)(2,1)S(1)}, bf16[4,64,384]{2,1,0:T(8,128)(2,1)S(1)}, u32[]{:S(2)}, u32[]{:S(2)}) collective-permute-start(bf16[4,64,384]{2,1,0:T(8,128)(2,1)S(1)} %pad_maximum_fusion.1), channel_id=1, source_target_pairs={{0,16},{1,3},{2,18},{3,1},{4,20},{5,7},{6,22},{7,5},{8,24},{9,11},... | collective-permute-start | bytes 589832 | tf_op jit(solution)/shard_map/ppermute | solution.py:32
  21.1 14.1 %copy-start.4 = (bf16[8,64,384]{2,1,0:T(8,128)(2,1)}, bf16[8,64,384]{2,1,0:T(8,128)(2,1)S(1)}, u32[]{:S(2)}) copy-start(bf16[8,64,384]{2,1,0:T(8,128)(2,1)S(1)} %pad_maximum_fusion.refs_1_) | copy-start | bytes 1179652
  21.1 8.3 %collective-permute-start.4 = (bf16[8,64,384]{2,1,0:T(8,128)(2,1)S(1)}, bf16[8,64,384]{2,1,0:T(8,128)(2,1)S(1)}, u32[]{:S(2)}, u32[]{:S(2)}) collective-permute-start(bf16[8,64,384]{2,1,0:T(8,128)(2,1)S(1)} %pad_maximum_fusion.refs_1_), channel_id=1, source_target_pairs={{0,2},{1,17},{2,0},{3,19},{4,6},{5,21},{6,4},{7,23},{8,10},{9,25},... | collective-permute-start | bytes 1179656 | tf_op jit(solution)/shard_map/ppermute | solution.py:32
  23.7 11.5 %collective-permute-start.5 = (bf16[8,64,384]{2,1,0:T(8,128)(2,1)S(1)}, bf16[8,64,384]{2,1,0:T(8,128)(2,1)S(1)}, u32[]{:S(2)}, u32[]{:S(2)}) collective-permute-start(bf16[8,64,384]{2,1,0:T(8,128)(2,1)S(1)} %pad_maximum_fusion.refs_1_), channel_id=1, source_target_pairs={{0,1},{1,0},{2,3},{3,2},{4,5},{5,4},{6,7},{7,6},{8,9},{9,8},{10,11... | collective-permute-start | bytes 1179656 | tf_op jit(solution)/shard_map/ppermute | solution.py:32
  29.5 5.7 %copy-start.5 = (bf16[8,64,384]{2,1,0:T(8,128)(2,1)}, bf16[8,64,384]{2,1,0:T(8,128)(2,1)S(1)}, u32[]{:S(2)}) copy-start(bf16[8,64,384]{2,1,0:T(8,128)(2,1)S(1)} %collective-permute-done.4.refs_2_) | copy-start | bytes 1179652
  29.5 5.7 %collective-permute-start.6 = (bf16[8,64,384]{2,1,0:T(8,128)(2,1)S(1)}, bf16[8,64,384]{2,1,0:T(8,128)(2,1)S(1)}, u32[]{:S(2)}, u32[]{:S(2)}) collective-permute-start(bf16[8,64,384]{2,1,0:T(8,128)(2,1)S(1)} %collective-permute-done.4.refs_2_), channel_id=1, source_target_pairs={{0,1},{1,0},{2,3},{3,2},{4,5},{5,4},{6,7},{7,6},{8,9},{9,8},{10,11... | collective-permute-start | bytes 1179656 | tf_op jit(solution)/shard_map/ppermute | solution.py:32
  31.0 3.6 %collective-permute-start.7 = (f32[1,8,64]{2,1,0:T(8,128)S(1)}, f32[1,8,64]{2,1,0:T(8,128)S(1)}, u32[]{:S(2)}, u32[]{:S(2)}) collective-permute-start(f32[1,8,64]{2,1,0:T(8,128)S(1)} %maximum_bitcast_fusion), channel_id=1, source_target_pairs={{0,16},{1,17},{2,18},{3,19},{4,20},{5,21},{6,22},{7,23},{8,24},{9,... | collective-permute-start | bytes 6152 | tf_op jit(solution)/shard_map/ppermute | solution.py:32
  35.2 0.8 copy-start.6
  36.0 0.7 copy-start.7
  36.7 4.6 %copy-start = (bf16[4,3072,512]{2,1,0:T(8,128)(2,1)S(1)}, bf16[4,3072,512]{2,1,0:T(8,128)(2,1)}, u32[]{:S(2)}) copy-start(bf16[4,3072,512]{2,1,0:T(8,128)(2,1)} %refs_6_.1) | copy-start | bytes 37748740
  41.3 4.6 %copy-start.1 = (bf16[4,3072,512]{2,1,0:T(8,128)(2,1)S(1)}, bf16[4,3072,512]{2,1,0:T(8,128)(2,1)}, u32[]{:S(2)}) copy-start(bf16[4,3072,512]{2,1,0:T(8,128)(2,1)} %refs_7_.1) | copy-start | bytes 37748740
  45.9 4.6 %copy-start.2 = (bf16[4,512,3072]{2,1,0:T(8,128)(2,1)S(1)}, bf16[4,512,3072]{2,1,0:T(8,128)(2,1)}, u32[]{:S(2)}) copy-start(bf16[4,512,3072]{2,1,0:T(8,128)(2,1)} %refs_8_.1) | copy-start | bytes 37748740
  71.4 2.5 %collective-permute-start.8 = (f32[16,32,384]{2,1,0:T(8,128)}, f32[16,32,384]{2,1,0:T(8,128)S(1)}, u32[]{:S(2)}, u32[]{:S(2)}) collective-permute-start(f32[16,32,384]{2,1,0:T(8,128)} %get-tuple-element.16), channel_id=1, source_target_pairs={{0,1},{1,0},{2,3},{3,2},{4,5},{5,4},{6,7},{7,6},{8,9},{9,8},{10,11... | collective-permute-start | bytes 2359304 | tf_op jit(solution)/shard_map/ppermute | solution.py:32
  75.1 5.7 %collective-permute-start.9 = (bf16[8,32,384]{2,1,0:T(8,128)(2,1)S(1)}, bf16[8,32,384]{2,1,0:T(8,128)(2,1)S(1)}, u32[]{:S(2)}, u32[]{:S(2)}) collective-permute-start(bf16[8,32,384]{2,1,0:T(8,128)(2,1)S(1)} %slice.66), channel_id=1, source_target_pairs={{0,2},{1,17},{2,0},{3,19},{4,6},{5,21},{6,4},{7,23},{8,10},{9,25},... | collective-permute-start | bytes 589832 | tf_op jit(solution)/shard_map/ppermute | solution.py:32
  81.0 4.7 %collective-permute-start.10 = (bf16[4,32,384]{2,1,0:T(8,128)(2,1)S(1)}, bf16[4,32,384]{2,1,0:T(8,128)(2,1)S(1)}, u32[]{:S(2)}, u32[]{:S(2)}) collective-permute-start(bf16[4,32,384]{2,1,0:T(8,128)(2,1)S(1)} %slice.67), channel_id=1, source_target_pairs={{0,16},{1,3},{2,18},{3,1},{4,20},{5,7},{6,22},{7,5},{8,24},{9,11},... | collective-permute-start | bytes 294920 | tf_op jit(solution)/shard_map/ppermute | solution.py:32
  85.7 8.4 %collective-permute-start.11 = (f32[2,32,384]{2,1,0:T(8,128)S(1)}, f32[2,32,384]{2,1,0:T(8,128)S(1)}, u32[]{:S(2)}, u32[]{:S(2)}) collective-permute-start(f32[2,32,384]{2,1,0:T(8,128)S(1)} %slice.47), channel_id=1, source_target_pairs={{0,4},{1,5},{2,6},{3,7},{4,0},{5,1},{6,2},{7,3},{8,12},{9,13},{10,... | collective-permute-start | bytes 294920 | tf_op jit(solution)/shard_map/ppermute | solution.py:32
  85.8 1.2 %copy-start.3 = (bf16[4,128,1024]{2,1,0:T(8,128)(2,1)S(1)}, bf16[4,128,1024]{2,1,0:T(8,128)(2,1)}, u32[]{:S(2)}) copy-start(bf16[4,128,1024]{2,1,0:T(8,128)(2,1)} %get-tuple-element.18.grads) | copy-start | bytes 3145732
  94.1 6.6 %collective-permute-start.12 = (f32[1,32,384]{2,1,0:T(8,128)S(1)}, f32[1,32,384]{2,1,0:T(8,128)S(1)}, u32[]{:S(2)}, u32[]{:S(2)}) collective-permute-start(f32[1,32,384]{2,1,0:T(8,128)S(1)} %slice.49), channel_id=1, source_target_pairs={{0,8},{1,9},{2,10},{3,11},{4,12},{5,13},{6,14},{7,15},{8,0},{9,1},... | collective-permute-start | bytes 147464 | tf_op jit(solution)/shard_map/ppermute | solution.py:32
  100.8 3.6 %collective-permute-start.13 = (bf16[32,192]{1,0:T(8,128)(2,1)S(1)}, bf16[32,192]{1,0:T(8,128)(2,1)S(1)}, u32[]{:S(2)}, u32[]{:S(2)}) collective-permute-start(bf16[32,192]{1,0:T(8,128)(2,1)S(1)} %get-tuple-element.30), channel_id=1, source_target_pairs={{0,1},{1,0},{2,3},{3,2},{4,5},{5,4},{6,7},{7,6},{8,9},{9,8},{10,11... | collective-permute-start | bytes 36872 | tf_op jit(solution)/shard_map/ppermute | solution.py:32

commit v2 on v1

v2 whole, which is shorter than its diff:
```python
import jax
import jax.numpy as jnp
from jax import lax
from jax.experimental import pallas as pl
from jax.experimental.pallas import tpu as pltpu
from jax.sharding import PartitionSpec as P

BF = jnp.bfloat16
F32 = jnp.float32
BOTH = ("group", "shard")
MIB = 1 << 20
VM = pl.BlockSpec(memory_space=pltpu.VMEM)
SM = pl.BlockSpec(memory_space=pltpu.SMEM)


def dot(a, b, da, db):
    return lax.dot_general(a, b, (((da,), (db,)), ((), ())), preferred_element_type=F32)


def bits_of(size):
    return size.bit_length() - 1


def stage_masks(groups, shards):
    masks = [1 << k for k in range(bits_of(shards) - 1, 0, -1)] + [shards << k for k in range(bits_of(groups))]
    other = masks[:-2] + masks[-2:][::-1]
    return other, masks


def swap(x, groups, shards, masks):
    pairs = [(i, i ^ masks[i & 1]) for i in range(groups * shards)]
    return lax.ppermute(x, BOTH, pairs)


def relative(index, masks, top_first):
    count = len(masks)
    out = 0
    for step, mask in enumerate(masks):
        place = count - 1 - step if top_first else step
        out = out | (((index >> bits_of(mask)) & 1) << place)
    return out


def forward_kernel(gather_masks, scatter_masks, groups, shards, experts,
                   t0, t1, t2, t3, c0, c1, c2, c3, routes, wg_hbm, wu_hbm, wd_hbm,
                   full, grads, keep, send, x, q, coef, total, wg, wu, wd, sems):
    half, rows, width = t0.shape[0], t0.shape[1], t0.shape[2] // 2
    tokens = 2 * groups * rows
    hidden = wg.shape[2]
    group, shard = lax.axis_index("group"), lax.axis_index("shard")
    core, me = shard & 1, group * shards + shard
    gather_at = [relative(me, masks, False) for masks in gather_masks]
    scatter_at = [relative(me, masks, True) for masks in scatter_masks]

    def fetch(i, e):
        source, target = ((wg_hbm, wg), (wu_hbm, wu), (wd_hbm, wd))[i]
        return pltpu.make_async_copy(source.at[e], target.at[e], sems.at[i, e])

    for e in range(experts):
        for i in range(3):
            fetch(i, e).start()

    def assemble(out, even, odd):
        for g in range(groups):
            for pair in range(shards // 2):
                at = g * shards + pair * 2
                blocks = []
                for (low, high), masks, start in ((even, gather_masks[0], gather_at[0]), (odd, gather_masks[1], gather_at[1])):
                    r = relative(at, masks, False) ^ start
                    blocks.append(jnp.where(r < half, low[jnp.minimum(r, half - 1)], high[jnp.maximum(r - half, 0)]))
                for k in range(2):
                    out[(2 * g + k) * rows:(2 * g + k + 1) * rows, pair * 2 * width:(pair + 1) * 2 * width] = jnp.concatenate(
                        [block[:, k * width:(k + 1) * width] for block in blocks], axis=1)

    @pl.when(core == 0)
    def _():
        assemble(x, (t0, t1), (t2, t3))
        assemble(q, (c0, c1), (c2, c3))

    @pl.when(core == 1)
    def _():
        assemble(x, (t2, t3), (t0, t1))
        assemble(q, (c2, c3), (c0, c1))

    full[...] = x[...]
    for g in range(groups):
        table = routes[g ^ group].T
        for e in range(experts):
            number = (group * experts + e).astype(F32)
            value = jnp.where(table[:, 0:1] == number, table[:, 2:3], 0.0) + jnp.where(table[:, 1:2] == number, table[:, 3:4], 0.0)
            coef[e, 2 * g * rows:2 * (g + 1) * rows, :] = value

    @pl.loop(0, experts)
    def _(e):
        fetch(0, e).wait()
        gate_pre = dot(x[...], wg[e], 1, 0)
        fetch(1, e).wait()
        up_value = dot(x[...], wu[e], 1, 0)
        fetch(2, e).wait()
        hidden_grad = dot(q[...], wd[e], 1, 1) * coef[e]
        s = 1.0 / (1.0 + jnp.exp(-gate_pre))
        gate_grad = (hidden_grad * up_value * s * (1.0 + gate_pre * (1.0 - s))).astype(BF)
        up_grad = (hidden_grad * (gate_pre * s)).astype(BF)
        grads[e, :, :hidden] = gate_grad
        grads[e, :, hidden:] = up_grad
        part = dot(gate_grad, wg[e], 1, 1) + dot(up_grad, wu[e], 1, 1)

        @pl.when(e == 0)
        def _():
            total[...] = part

        @pl.when(e > 0)
        def _():
            total[...] += part

    for g in range(groups):
        for pair in range(shards // 2):
            at = g * shards + pair * 2
            first = relative(at, scatter_masks[0], True) ^ scatter_at[0]
            second = relative(at, scatter_masks[1], True) ^ scatter_at[1]
            block = total[2 * g * rows:2 * (g + 1) * rows, pair * 2 * width:(pair + 1) * 2 * width]
            even, odd = (jnp.concatenate([block[:rows, k * width:(k + 1) * width], block[rows:, k * width:(k + 1) * width]], axis=1) for k in range(2))

            @pl.when(core == 0)
            def _():
                keep[first] = even
                send[second] = odd.astype(BF)

            @pl.when(core == 1)
            def _():
                keep[second] = odd
                send[first] = even.astype(BF)


def pack_kernel(tokens, cotangent, ids, weights, packed, routes):
    half = tokens.shape[0] // 2
    for i, a in enumerate((tokens, cotangent)):
        packed[i, 0] = jnp.concatenate([a[:half, :], a[half:, :]], axis=1)
    routes[0] = jnp.zeros_like(routes[0])
    routes[0, 0:2, :] = ids[...].astype(F32)
    routes[0, 2:4, :] = weights[...]


def pack(tokens, cotangent, ids, weights):
    rows, width = tokens.shape
    return pl.pallas_call(
        pack_kernel,
        out_shape=(pltpu.VMEM((2, 1, rows // 2, 2 * width), BF), pltpu.VMEM((1, 8, rows), F32)),
        in_specs=[VM] * 4,
        out_specs=(VM, VM),
        name="pack",
    )(tokens, cotangent, ids.T, weights.T)


def weight_kernel(units, blocks, transposed, *refs):
    rows, grads = refs[0], refs[1]
    if transposed:
        out_gate, out_up, token, made, sems = refs[-5:]
        xt = rows
    else:
        out_gate, out_up, token, xt, made, sems = refs[-6:]
        xt[...] = rows[...].T
    features, hidden = xt.shape[0], out_gate.shape[2]
    block = features // blocks
    copies = []
    for k, unit in enumerate(units):
        expert, j = divmod(unit, blocks)
        at = slice(j * block, (j + 1) * block)
        for i, out in enumerate((out_gate, out_up)):
            made[i, k] = dot(xt[at, :], grads[expert, :, i * hidden:(i + 1) * hidden], 1, 0).astype(BF)
            copies.append(pltpu.make_async_copy(made.at[i, k], out.at[expert, at, :], sems.at[i, k]))
            copies[-1].start()
    token[...] = jnp.zeros_like(token)
    for copy in copies:
        copy.wait()


def weight_grads(rows, grads, after, so_far, units, blocks, shape, piece):
    experts, features, hidden = shape
    transposed = bool(so_far)
    array, zero = jax.ShapeDtypeStruct(shape, BF), pltpu.VMEM((1,) + piece[1:], F32)
    anywhere = pl.BlockSpec(memory_space=pl.ANY)

    def kernel(*refs):
        weight_kernel(units, blocks, transposed, *refs)

    return pl.pallas_call(
        kernel,
        out_shape=(array, array, zero) + (() if transposed else (pltpu.VMEM((features, rows.shape[0]), BF),)),
        in_specs=[VM, VM, anywhere] + [anywhere] * len(so_far),
        out_specs=(anywhere, anywhere, VM) + (() if transposed else (VM,)),
        input_output_aliases={3: 0, 4: 1} if transposed else {},
        scratch_shapes=[pltpu.VMEM((2, len(units), features // blocks, hidden), BF), pltpu.SemaphoreType.DMA((2, len(units)))],
        compiler_params=pltpu.CompilerParams(vmem_limit_bytes=16 * MIB),
        cost_estimate=pl.CostEstimate(flops=4 * features * grads.shape[1] * hidden, bytes_accessed=4 * features * hidden, transcendentals=0),
        name="weight_grads",
    )(*(pltpu.with_memory_space_constraint(a, pltpu.VMEM) for a in (rows, grads)), after, *so_far)


def body(tokens, cotangent, expert_ids, route_weight, w_gate, w_up, w_down):
    groups, shards = lax.axis_size("group"), lax.axis_size("shard")
    experts, features, hidden = w_gate.shape
    rows, width = tokens.shape
    half_rows = rows // 2
    gather_masks = stage_masks(groups, shards)
    scatter_masks = tuple(m[::-1] for m in gather_masks)
    count = len(gather_masks[0])
    pairs = groups * shards // 2

    def step_masks(masks, step):
        return masks[0][step], masks[1][step]

    packed, routes = pack(tokens, cotangent, expert_ids, route_weight)
    def exchange(r):
        for k in range(bits_of(groups)):
            r = jnp.concatenate([r, swap(r, groups, shards, (shards << k,) * 2)], 0)
        return r

    routes = exchange(routes)
    for step in range(count - 2):
        packed = jnp.concatenate([packed, swap(packed, groups, shards, step_masks(gather_masks, step))], 1)
    packed, routes = lax.optimization_barrier((packed, routes))
    chains = [packed[0], packed[1]]
    chains = [jnp.concatenate([a, swap(a, groups, shards, step_masks(gather_masks, count - 2))], 0) for a in chains]
    highs = [swap(a, groups, shards, step_masks(gather_masks, count - 1)) for a in chains]
    gathered = []
    for low, high in zip(chains, highs):
        gathered += [low, high, swap(low, groups, shards, (1, 1)), swap(high, groups, shards, (1, 1))]
    total_rows = groups * rows
    gathered = [pltpu.with_memory_space_constraint(a, pltpu.VMEM) for a in gathered + [routes]]
    piece = (pairs, half_rows, 2 * width)

    def forward(*refs):
        forward_kernel(gather_masks, scatter_masks, groups, shards, experts, *refs)

    full, grads, keep, send = pl.pallas_call(
        forward,
        out_shape=(pltpu.VMEM((total_rows, features), BF), pltpu.VMEM((experts, total_rows, 2 * hidden), BF),
                   pltpu.VMEM(piece, F32), pltpu.VMEM(piece, BF)),
        in_specs=[VM] * 9 + [pl.BlockSpec(memory_space=pl.ANY)] * 3,
        out_specs=(VM,) * 4,
        scratch_shapes=[pltpu.VMEM((total_rows, features), BF), pltpu.VMEM((total_rows, features), BF),
                        pltpu.VMEM((experts, total_rows, 1), F32), pltpu.VMEM((total_rows, features), F32),
                        pltpu.VMEM(w_gate.shape, BF), pltpu.VMEM(w_up.shape, BF), pltpu.VMEM(w_down.shape, BF),
                        pltpu.SemaphoreType.DMA((3, experts))],
        compiler_params=pltpu.CompilerParams(vmem_limit_bytes=6 * experts * features * hidden + 16 * total_rows * features + 4 * MIB),
        cost_estimate=pl.CostEstimate(flops=10 * experts * total_rows * features * hidden, bytes_accessed=6 * experts * features * hidden, transcendentals=0),
        name="forward",
    )(*gathered, w_gate, w_up, w_down)

    blocks = 8
    shares = [3, 10, 8] + [5] * (count - 2)
    ends = [experts * blocks * sum(shares[:i + 1]) // sum(shares) for i in range(len(shares))]
    so_far, source, after = (), full, send
    kept = None
    for step in range(count + 1):
        units = list(range(ends[step - 1] if step else 0, ends[step]))
        grad_gate, grad_up, token, *made = weight_grads(source, grads, after, so_far, units, blocks, w_gate.shape, piece)
        so_far, source = (grad_gate, grad_up), made[0] if made else source
        if step == 0:
            kept = keep + swap(send, groups, shards, (1, 1)).astype(F32) + token
        else:
            half = kept.shape[0] // 2
            sent = kept[half:]
            if 2 * (step - 1) < count:
                sent = sent.astype(BF)
            kept = kept[:half] + swap(sent, groups, shards, step_masks(scatter_masks, step - 1)).astype(F32) + token
        after = kept
    done = kept[0].astype(BF)
    grad_tokens = jnp.concatenate([done[:, :width], done[:, width:]], 0)
    return grad_tokens, grad_gate, grad_up


def solution(mesh):
    in_specs = (
        P("group", "shard"),
        P("group", "shard"),
        P("group", None),
        P("group", None),
        P("group", None, "shard"),
        P("group", None, "shard"),
        P("group", "shard", None),
    )
    out_specs = (P("group", "shard"), P("group", None, "shard"), P("group", None, "shard"))
    return jax.shard_map(body, mesh=mesh, in_specs=in_specs, out_specs=out_specs, check_vma=False)
```

time: 105 us -> 73.7 us (0.70)
  local copies, waits for them, and re-layouts: 18.7 us -> 0.15 us
  waiting for transfers between devices: 24.1 us -> 15.2 us
  other arithmetic: 5.03 us -> 0.92 us
    unnamed x16 -> x0, local copies, waits for them, and re-layouts: 16.4 us -> none
    ppermute x14 -> x16, waiting for transfers between devices: 24.1 us -> 15.2 us  [swap(): return lax.ppermute(x, BOTH, pairs)]
    pallas_call x1 -> x0, local copies, waits for them, and re-layouts: 1.5 us -> none  [body(): pl.pallas_call(forward, out_shape=(jax.ShapeDtypeStruct((total_rows, feat...]
    add x1, other arithmetic: 1.23 us -> 0.1 us  [body(): kept = keep + swap(send, groups, shards, (1, 1)).astype(F32) + token]
    pallas_call x5 -> x7, Pallas kernels: 35.1 us -> 36.1 us  [the longest x1 22.2 us: body(): pl.pallas_call(forward, out_shape=(pltpu.VMEM((total_rows, features), BF)...]
    ppermute x14 -> x16, starting transfers between devices: 21.3 us -> 20.3 us  [swap(): return lax.ppermute(x, BOTH, pairs)]
  transfers between devices with their start and end apart: 14 -> 16, of which waited for: 9 -> 10; matrix products, arithmetic and copies ran while one was open for 4% -> 0% of each run, Pallas kernels for 13% -> 18%
where the time goes in v2:
time: 73.7 us; the launch traced here: 73.5 us
  Pallas kernels  36.1 us (49%)
  starting transfers between devices  20.3 us (28%)
  waiting for transfers between devices  15.2 us (21%)
  other arithmetic  0.92 us (1%)
  between operations  0.81 us (1%)
    pallas_call x1, Pallas kernels, body(): pl.pallas_call(forward, out_shape=(pltpu.VMEM((total_rows, features), BF)...  22.2 us
    ppermute x16, starting transfers between devices, swap(): return lax.ppermute(x, BOTH, pairs)  20.3 us
    ppermute x16, waiting for transfers between devices, swap(): return lax.ppermute(x, BOTH, pairs)  15.2 us
    pallas_call x5, Pallas kernels, weight_grads(): pl.pallas_call(kernel, out_shape=(array, array, zero) + (() if transposed...  13.1 us
  transfers between devices with their start and end apart: 16, of which 10 were waited for; matrix products, arithmetic and copies ran while one was open for 0% of the time, Pallas kernels for 18%

profile of v2, /device:TPU:0, one launch (start us, length us, event | category | flops | bytes accessed | tf_op | source)
XLA Modules:
  0.0 73.5 jit_solution(8322281797822030129)
XLA Ops:
  0.6 0.9 %pack.1 = (bf16[2,1,32,384]{3,2,1,0:T(8,128)(2,1)S(1)}, f32[1,8,64]{2,1,0:T(8,128)S(1)}) custom-call(bf16[64,192]{1,0:T(8,128)(2,1)} %tokens.1, bf16[64,192]{1,0:T(8,128)(2,1)} %cotangent.1, s32[2,64]{1,0:T(2,128)} %bitcast.16, f32[2,64]{1,0:T(2,128)} %bitcast.17), custom_call_target="tpu_custom_call" | custom-call | tf_op jit(solution)/shard_map/pack/pallas_call | solution.py:146
  1.5 4.1 %collective-permute-start = (bf16[2,1,32,384]{3,2,1,0:T(8,128)(2,1)S(1)}, bf16[2,1,32,384]{3,2,1,0:T(8,128)(2,1)S(1)}, u32[]{:S(2)}, u32[]{:S(2)}) collective-permute-start(bf16[2,1,32,384]{3,2,1,0:T(8,128)(2,1)S(1)} %get-tuple-element.27), channel_id=1, source_target_pairs={{0,8},{1,9},{2,10},{3,11},{4,12},{5,13},{6,14},{7,15},{8,0},{9,1},... | collective-permute-start | bytes 147464 | tf_op jit(solution)/shard_map/ppermute | solution.py:32
  5.6 1.5 %collective-permute-start.2 = (f32[1,8,64]{2,1,0:T(8,128)S(1)}, f32[1,8,64]{2,1,0:T(8,128)S(1)}, u32[]{:S(2)}, u32[]{:S(2)}) collective-permute-start(f32[1,8,64]{2,1,0:T(8,128)S(1)} %get-tuple-element.28), channel_id=1, source_target_pairs={{0,16},{1,17},{2,18},{3,19},{4,20},{5,21},{6,22},{7,23},{8,24},{9,... | collective-permute-start | bytes 6152 | tf_op jit(solution)/shard_map/ppermute | solution.py:32
  7.1 1.1 %collective-permute-done = bf16[2,1,32,384]{3,2,1,0:T(8,128)(2,1)S(1)} collective-permute-done((bf16[2,1,32,384]{3,2,1,0:T(8,128)(2,1)S(1)}, bf16[2,1,32,384]{3,2,1,0:T(8,128)(2,1)S(1)}, u32[]{:S(2)}, u32[]{:S(2)}) %collective-permute-start) | collective-permute-done | bytes 49184 | tf_op jit(solution)/shard_map/ppermute | solution.py:32
  8.2 1.4 %collective-permute-start.1 = (bf16[2,2,32,384]{3,2,1,0:T(8,128)(2,1)S(1)}, bf16[2,2,32,384]{3,2,1,0:T(8,128)(2,1)S(1)}, u32[]{:S(2)}, u32[]{:S(2)}) collective-permute-start(bf16[2,2,32,384]{3,2,1,0:T(8,128)(2,1)S(1)} %pad_maximum_fusion.3), channel_id=1, source_target_pairs={{0,4},{1,5},{2,6},{3,7},{4,0},{5,1},{6,2},{7,3},{8,12},{9,13},{10,... | collective-permute-start | bytes 294920 | tf_op jit(solution)/shard_map/ppermute | solution.py:32
  9.7 3.2 %collective-permute-done.1 = bf16[2,2,32,384]{3,2,1,0:T(8,128)(2,1)S(1)} collective-permute-done((bf16[2,2,32,384]{3,2,1,0:T(8,128)(2,1)S(1)}, bf16[2,2,32,384]{3,2,1,0:T(8,128)(2,1)S(1)}, u32[]{:S(2)}, u32[]{:S(2)}) %collective-permute-start.1) | collective-permute-done | bytes 98336 | tf_op jit(solution)/shard_map/ppermute | solution.py:32
  12.9 1.8 %collective-permute-start.3 = (bf16[4,32,384]{2,1,0:T(8,128)(2,1)S(1)}, bf16[4,32,384]{2,1,0:T(8,128)(2,1)S(1)}, u32[]{:S(2)}, u32[]{:S(2)}) collective-permute-start(bf16[4,32,384]{2,1,0:T(8,128)(2,1)S(1)} %get-tuple-element.52), channel_id=1, source_target_pairs={{0,16},{1,3},{2,18},{3,1},{4,20},{5,7},{6,22},{7,5},{8,24},{9,11},... | collective-permute-start | bytes 294920 | tf_op jit(solution)/shard_map/ppermute | solution.py:32
  15.1 3.6 %collective-permute-done.3 = bf16[4,32,384]{2,1,0:T(8,128)(2,1)S(1)} collective-permute-done((bf16[4,32,384]{2,1,0:T(8,128)(2,1)S(1)}, bf16[4,32,384]{2,1,0:T(8,128)(2,1)S(1)}, u32[]{:S(2)}, u32[]{:S(2)}) %collective-permute-start.3) | collective-permute-done | bytes 98336 | tf_op jit(solution)/shard_map/ppermute | solution.py:32
  18.7 1.8 %collective-permute-start.4 = (bf16[8,32,384]{2,1,0:T(8,128)(2,1)S(1)}, bf16[8,32,384]{2,1,0:T(8,128)(2,1)S(1)}, u32[]{:S(2)}, u32[]{:S(2)}) collective-permute-start(bf16[8,32,384]{2,1,0:T(8,128)(2,1)S(1)} %pad_maximum_fusion.1.refs_0_), channel_id=1, source_target_pairs={{0,2},{1,17},{2,0},{3,19},{4,6},{5,21},{6,4},{7,23},{8,10},{9,25},... | collective-permute-start | bytes 589832 | tf_op jit(solution)/shard_map/ppermute | solution.py:32
  20.8 1.8 %collective-permute-start.8 = (bf16[8,32,384]{2,1,0:T(8,128)(2,1)S(1)}, bf16[8,32,384]{2,1,0:T(8,128)(2,1)S(1)}, u32[]{:S(2)}, u32[]{:S(2)}) collective-permute-start(bf16[8,32,384]{2,1,0:T(8,128)(2,1)S(1)} %pad_maximum_fusion.2.refs_4_), channel_id=1, source_target_pairs={{0,2},{1,17},{2,0},{3,19},{4,6},{5,21},{6,4},{7,23},{8,10},{9,25},... | collective-permute-start | bytes 589832 | tf_op jit(solution)/shard_map/ppermute | solution.py:32
  23.1 1.3 %collective-permute-done.4.refs_1_ = bf16[8,32,384]{2,1,0:T(8,128)(2,1)S(1)} collective-permute-done((bf16[8,32,384]{2,1,0:T(8,128)(2,1)S(1)}, bf16[8,32,384]{2,1,0:T(8,128)(2,1)S(1)}, u32[]{:S(2)}, u32[]{:S(2)}) %collective-permute-start.4) | collective-permute-done | bytes 196640 | tf_op jit(solution)/shard_map/ppermute | solution.py:32
  24.5 2.1 %collective-permute-done.8.refs_5_ = bf16[8,32,384]{2,1,0:T(8,128)(2,1)S(1)} collective-permute-done((bf16[8,32,384]{2,1,0:T(8,128)(2,1)S(1)}, bf16[8,32,384]{2,1,0:T(8,128)(2,1)S(1)}, u32[]{:S(2)}, u32[]{:S(2)}) %collective-permute-start.8) | collective-permute-done | bytes 196640 | tf_op jit(solution)/shard_map/ppermute | solution.py:32
  26.6 1.4 %collective-permute-done.10.refs_7_ = bf16[8,32,384]{2,1,0:T(8,128)(2,1)S(1)} collective-permute-done((bf16[8,32,384]{2,1,0:T(8,128)(2,1)S(1)}, bf16[8,32,384]{2,1,0:T(8,128)(2,1)S(1)}, u32[]{:S(2)}, u32[]{:S(2)}) %collective-permute-start.10) | collective-permute-done | bytes 196640 | tf_op jit(solution)/shard_map/ppermute | solution.py:32
  28.0 22.2 %forward.1 = (bf16[128,3072]{1,0:T(8,128)(2,1)S(1)}, bf16[4,128,1024]{2,1,0:T(8,128)(2,1)S(1)}, f32[16,32,384]{2,1,0:T(8,128)S(1)}, bf16[16,32,384]{2,1,0:T(8,128)(2,1)S(1)}) custom-call(bf16[8,32,384]{2,1,0:T(8,128)(2,1)S(1)} %pad_maximum_fusion.1.refs_0_, bf16[8,32,384]{2,1,0:T(8,128)(2,1)S(1)} %collective-permute-done.4.refs_1_, ...), custom_call_target="tpu_custom_call" | custom-call | flops 8053063680 | bytes 37748736 | tf_op jit(solution)/shard_map/forward/pallas_call | solution.py:236
  50.5 1.8 %weight_grads.5 = (bf16[4,3072,512]{2,1,0:T(8,128)(2,1)}, bf16[4,3072,512]{2,1,0:T(8,128)(2,1)}, f32[1,32,384]{2,1,0:T(8,128)S(1)}, bf16[3072,128]{1,0:T(8,128)(2,1)S(1)}) custom-call(bf16[128,3072]{1,0:T(8,128)(2,1)S(1)} %get-tuple-element.33.refs_0_, bf16[4,128,1024]{2,1,0:T(8,128)(2,1)S(1)} %get-tuple-element.34.refs_1_, ...), custom_call_target="tpu_custom_call" | custom-call | flops 805306368 | bytes 6291456 | tf_op jit(solution)/shard_map/weight_grads/pallas_call | solution.py:187
  52.4 1.8 %collective-permute-start.12 = (bf16[8,32,384]{2,1,0:T(8,128)(2,1)S(1)}, bf16[8,32,384]{2,1,0:T(8,128)(2,1)S(1)}, u32[]{:S(2)}, u32[]{:S(2)}) collective-permute-start(bf16[8,32,384]{2,1,0:T(8,128)(2,1)S(1)} %slice.80), channel_id=1, source_target_pairs={{0,2},{1,17},{2,0},{3,19},{4,6},{5,21},{6,4},{7,23},{8,10},{9,25},... | collective-permute-start | bytes 589832 | tf_op jit(solution)/shard_map/ppermute | solution.py:32
  54.2 3.5 %weight_grads.6 = (bf16[4,3072,512]{2,1,0:T(8,128)(2,1)}, bf16[4,3072,512]{2,1,0:T(8,128)(2,1)}, f32[1,32,384]{2,1,0:T(8,128)S(1)}) custom-call(bf16[3072,128]{1,0:T(8,128)(2,1)S(1)} %get-tuple-element.36.refs_0_, bf16[4,128,1024]{2,1,0:T(8,128)(2,1)S(1)} %get-tuple-element.34.refs_1_, ...), custom_call_target="tpu_custom_call", output_to_operand_aliasing={{0}: (3, {}), {1}: (4, {})} | custom-call | flops 805306368 | bytes 6291456 | tf_op jit(solution)/shard_map/weight_grads/pallas_call | solution.py:187
  58.2 1.8 %collective-permute-start.13 = (bf16[4,32,384]{2,1,0:T(8,128)(2,1)S(1)}, bf16[4,32,384]{2,1,0:T(8,128)(2,1)S(1)}, u32[]{:S(2)}, u32[]{:S(2)}) collective-permute-start(bf16[4,32,384]{2,1,0:T(8,128)(2,1)S(1)} %slice.81), channel_id=1, source_target_pairs={{0,16},{1,3},{2,18},{3,1},{4,20},{5,7},{6,22},{7,5},{8,24},{9,11},... | collective-permute-start | bytes 294920 | tf_op jit(solution)/shard_map/ppermute | solution.py:32
  59.9 3.0 %weight_grads.7 = (bf16[4,3072,512]{2,1,0:T(8,128)(2,1)}, bf16[4,3072,512]{2,1,0:T(8,128)(2,1)}, f32[1,32,384]{2,1,0:T(8,128)S(1)}) custom-call(bf16[3072,128]{1,0:T(8,128)(2,1)S(1)} %get-tuple-element.36.refs_0_, bf16[4,128,1024]{2,1,0:T(8,128)(2,1)S(1)} %get-tuple-element.34.refs_1_, ...), custom_call_target="tpu_custom_call", output_to_operand_aliasing={{0}: (3, {}), {1}: (4, {})} | custom-call | flops 805306368 | bytes 6291456 | tf_op jit(solution)/shard_map/weight_grads/pallas_call | solution.py:187
  63.0 1.1 %collective-permute-start.14 = (f32[2,32,384]{2,1,0:T(8,128)S(1)}, f32[2,32,384]{2,1,0:T(8,128)S(1)}, u32[]{:S(2)}, u32[]{:S(2)}) collective-permute-start(f32[2,32,384]{2,1,0:T(8,128)S(1)} %slice.55), channel_id=1, source_target_pairs={{0,4},{1,5},{2,6},{3,7},{4,0},{5,1},{6,2},{7,3},{8,12},{9,13},{10,... | collective-permute-start | bytes 294920 | tf_op jit(solution)/shard_map/ppermute | solution.py:32
  64.1 2.2 %weight_grads.8 = (bf16[4,3072,512]{2,1,0:T(8,128)(2,1)}, bf16[4,3072,512]{2,1,0:T(8,128)(2,1)}, f32[1,32,384]{2,1,0:T(8,128)S(1)}) custom-call(bf16[3072,128]{1,0:T(8,128)(2,1)S(1)} %get-tuple-element.36.refs_0_, bf16[4,128,1024]{2,1,0:T(8,128)(2,1)S(1)} %get-tuple-element.34.refs_1_, ...), custom_call_target="tpu_custom_call", output_to_operand_aliasing={{0}: (3, {}), {1}: (4, {})} | custom-call | flops 805306368 | bytes 6291456 | tf_op jit(solution)/shard_map/weight_grads/pallas_call | solution.py:187
  66.4 1.3 %collective-permute-done.14 = f32[2,32,384]{2,1,0:T(8,128)S(1)} collective-permute-done((f32[2,32,384]{2,1,0:T(8,128)S(1)}, f32[2,32,384]{2,1,0:T(8,128)S(1)}, u32[]{:S(2)}, u32[]{:S(2)}) %collective-permute-start.14) | collective-permute-done | bytes 98336 | tf_op jit(solution)/shard_map/ppermute | solution.py:32
  67.8 2.2 %collective-permute-start.15 = (f32[1,32,384]{2,1,0:T(8,128)S(1)}, f32[1,32,384]{2,1,0:T(8,128)S(1)}, u32[]{:S(2)}, u32[]{:S(2)}) collective-permute-start(f32[1,32,384]{2,1,0:T(8,128)S(1)} %slice.57), channel_id=1, source_target_pairs={{0,8},{1,9},{2,10},{3,11},{4,12},{5,13},{6,14},{7,15},{8,0},{9,1},... | collective-permute-start | bytes 147464 | tf_op jit(solution)/shard_map/ppermute | solution.py:32
  69.9 2.5 %weight_grads.9 = (bf16[4,3072,512]{2,1,0:T(8,128)(2,1)}, bf16[4,3072,512]{2,1,0:T(8,128)(2,1)}, f32[1,32,384]{2,1,0:T(8,128)S(1)}) custom-call(bf16[3072,128]{1,0:T(8,128)(2,1)S(1)} %get-tuple-element.36.refs_0_, bf16[4,128,1024]{2,1,0:T(8,128)(2,1)S(1)} %get-tuple-element.34.refs_1_, ...), custom_call_target="tpu_custom_call", output_to_operand_aliasing={{0}: (3, {}), {1}: (4, {})} | custom-call | flops 805306368 | bytes 6291456 | tf_op jit(solution)/shard_map/weight_grads/pallas_call | solution.py:187
  (32 shorter events, 3.3 us)
Async XLA Ops:
  1.5 6.7 %collective-permute-start = (bf16[2,1,32,384]{3,2,1,0:T(8,128)(2,1)S(1)}, bf16[2,1,32,384]{3,2,1,0:T(8,128)(2,1)S(1)}, u32[]{:S(2)}, u32[]{:S(2)}) collective-permute-start(bf16[2,1,32,384]{3,2,1,0:T(8,128)(2,1)S(1)} %get-tuple-element.27), channel_id=1, source_target_pairs={{0,8},{1,9},{2,10},{3,11},{4,12},{5,13},{6,14},{7,15},{8,0},{9,1},... | collective-permute-start | bytes 147464 | tf_op jit(solution)/shard_map/ppermute | solution.py:32
  5.6 4.1 %collective-permute-start.2 = (f32[1,8,64]{2,1,0:T(8,128)S(1)}, f32[1,8,64]{2,1,0:T(8,128)S(1)}, u32[]{:S(2)}, u32[]{:S(2)}) collective-permute-start(f32[1,8,64]{2,1,0:T(8,128)S(1)} %get-tuple-element.28), channel_id=1, source_target_pairs={{0,16},{1,17},{2,18},{3,19},{4,20},{5,21},{6,22},{7,23},{8,24},{9,... | collective-permute-start | bytes 6152 | tf_op jit(solution)/shard_map/ppermute | solution.py:32
  8.2 4.7 %collective-permute-start.1 = (bf16[2,2,32,384]{3,2,1,0:T(8,128)(2,1)S(1)}, bf16[2,2,32,384]{3,2,1,0:T(8,128)(2,1)S(1)}, u32[]{:S(2)}, u32[]{:S(2)}) collective-permute-start(bf16[2,2,32,384]{3,2,1,0:T(8,128)(2,1)S(1)} %pad_maximum_fusion.3), channel_id=1, source_target_pairs={{0,4},{1,5},{2,6},{3,7},{4,0},{5,1},{6,2},{7,3},{8,12},{9,13},{10,... | collective-permute-start | bytes 294920 | tf_op jit(solution)/shard_map/ppermute | solution.py:32
  12.9 5.7 %collective-permute-start.3 = (bf16[4,32,384]{2,1,0:T(8,128)(2,1)S(1)}, bf16[4,32,384]{2,1,0:T(8,128)(2,1)S(1)}, u32[]{:S(2)}, u32[]{:S(2)}) collective-permute-start(bf16[4,32,384]{2,1,0:T(8,128)(2,1)S(1)} %get-tuple-element.52), channel_id=1, source_target_pairs={{0,16},{1,3},{2,18},{3,1},{4,20},{5,7},{6,22},{7,5},{8,24},{9,11},... | collective-permute-start | bytes 294920 | tf_op jit(solution)/shard_map/ppermute | solution.py:32
  14.7 6.1 %collective-permute-start.7 = (bf16[4,32,384]{2,1,0:T(8,128)(2,1)S(1)}, bf16[4,32,384]{2,1,0:T(8,128)(2,1)S(1)}, u32[]{:S(2)}, u32[]{:S(2)}) collective-permute-start(bf16[4,32,384]{2,1,0:T(8,128)(2,1)S(1)} %get-tuple-element.51), channel_id=1, source_target_pairs={{0,16},{1,3},{2,18},{3,1},{4,20},{5,7},{6,22},{7,5},{8,24},{9,11},... | collective-permute-start | bytes 294920 | tf_op jit(solution)/shard_map/ppermute | solution.py:32
  18.7 5.7 %collective-permute-start.4 = (bf16[8,32,384]{2,1,0:T(8,128)(2,1)S(1)}, bf16[8,32,384]{2,1,0:T(8,128)(2,1)S(1)}, u32[]{:S(2)}, u32[]{:S(2)}) collective-permute-start(bf16[8,32,384]{2,1,0:T(8,128)(2,1)S(1)} %pad_maximum_fusion.1.refs_0_), channel_id=1, source_target_pairs={{0,2},{1,17},{2,0},{3,19},{4,6},{5,21},{6,4},{7,23},{8,10},{9,25},... | collective-permute-start | bytes 589832 | tf_op jit(solution)/shard_map/ppermute | solution.py:32
  20.8 5.7 %collective-permute-start.8 = (bf16[8,32,384]{2,1,0:T(8,128)(2,1)S(1)}, bf16[8,32,384]{2,1,0:T(8,128)(2,1)S(1)}, u32[]{:S(2)}, u32[]{:S(2)}) collective-permute-start(bf16[8,32,384]{2,1,0:T(8,128)(2,1)S(1)} %pad_maximum_fusion.2.refs_4_), channel_id=1, source_target_pairs={{0,2},{1,17},{2,0},{3,19},{4,6},{5,21},{6,4},{7,23},{8,10},{9,25},... | collective-permute-start | bytes 589832 | tf_op jit(solution)/shard_map/ppermute | solution.py:32
  22.6 3.9 %collective-permute-start.5 = (bf16[8,32,384]{2,1,0:T(8,128)(2,1)S(1)}, bf16[8,32,384]{2,1,0:T(8,128)(2,1)S(1)}, u32[]{:S(2)}, u32[]{:S(2)}) collective-permute-start(bf16[8,32,384]{2,1,0:T(8,128)(2,1)S(1)} %pad_maximum_fusion.1.refs_0_), channel_id=1, source_target_pairs={{0,1},{1,0},{2,3},{3,2},{4,5},{5,4},{6,7},{7,6},{8,9},{9,8},{10,11... | collective-permute-start | bytes 589832 | tf_op jit(solution)/shard_map/ppermute | solution.py:32
  22.6 3.9 %collective-permute-start.9 = (bf16[8,32,384]{2,1,0:T(8,128)(2,1)S(1)}, bf16[8,32,384]{2,1,0:T(8,128)(2,1)S(1)}, u32[]{:S(2)}, u32[]{:S(2)}) collective-permute-start(bf16[8,32,384]{2,1,0:T(8,128)(2,1)S(1)} %pad_maximum_fusion.2.refs_4_), channel_id=1, source_target_pairs={{0,1},{1,0},{2,3},{3,2},{4,5},{5,4},{6,7},{7,6},{8,9},{9,8},{10,11... | collective-permute-start | bytes 589832 | tf_op jit(solution)/shard_map/ppermute | solution.py:32
  24.4 2.1 %collective-permute-start.6 = (bf16[8,32,384]{2,1,0:T(8,128)(2,1)S(1)}, bf16[8,32,384]{2,1,0:T(8,128)(2,1)S(1)}, u32[]{:S(2)}, u32[]{:S(2)}) collective-permute-start(bf16[8,32,384]{2,1,0:T(8,128)(2,1)S(1)} %collective-permute-done.4.refs_1_), channel_id=1, source_target_pairs={{0,1},{1,0},{2,3},{3,2},{4,5},{5,4},{6,7},{7,6},{8,9},{9,8},{10,11... | collective-permute-start | bytes 589832 | tf_op jit(solution)/shard_map/ppermute | solution.py:32
  26.6 1.4 %collective-permute-start.10 = (bf16[8,32,384]{2,1,0:T(8,128)(2,1)S(1)}, bf16[8,32,384]{2,1,0:T(8,128)(2,1)S(1)}, u32[]{:S(2)}, u32[]{:S(2)}) collective-permute-start(bf16[8,32,384]{2,1,0:T(8,128)(2,1)S(1)} %collective-permute-done.8.refs_5_), channel_id=1, source_target_pairs={{0,1},{1,0},{2,3},{3,2},{4,5},{5,4},{6,7},{7,6},{8,9},{9,8},{10,11... | collective-permute-start | bytes 589832 | tf_op jit(solution)/shard_map/ppermute | solution.py:32
  50.2 2.0 %collective-permute-start.11 = (bf16[16,32,384]{2,1,0:T(8,128)(2,1)S(1)}, bf16[16,32,384]{2,1,0:T(8,128)(2,1)S(1)}, u32[]{:S(2)}, u32[]{:S(2)}) collective-permute-start(bf16[16,32,384]{2,1,0:T(8,128)(2,1)S(1)} %get-tuple-element.32.refs_2_), channel_id=1, source_target_pairs={{0,1},{1,0},{2,3},{3,2},{4,5},{5,4},{6,7},{7,6},{8,9},{9,8},{10,11... | collective-permute-start | bytes 1179656 | tf_op jit(solution)/shard_map/ppermute | solution.py:32
  52.4 5.7 %collective-permute-start.12 = (bf16[8,32,384]{2,1,0:T(8,128)(2,1)S(1)}, bf16[8,32,384]{2,1,0:T(8,128)(2,1)S(1)}, u32[]{:S(2)}, u32[]{:S(2)}) collective-permute-start(bf16[8,32,384]{2,1,0:T(8,128)(2,1)S(1)} %slice.80), channel_id=1, source_target_pairs={{0,2},{1,17},{2,0},{3,19},{4,6},{5,21},{6,4},{7,23},{8,10},{9,25},... | collective-permute-start | bytes 589832 | tf_op jit(solution)/shard_map/ppermute | solution.py:32
  58.2 4.8 %collective-permute-start.13 = (bf16[4,32,384]{2,1,0:T(8,128)(2,1)S(1)}, bf16[4,32,384]{2,1,0:T(8,128)(2,1)S(1)}, u32[]{:S(2)}, u32[]{:S(2)}) collective-permute-start(bf16[4,32,384]{2,1,0:T(8,128)(2,1)S(1)} %slice.81), channel_id=1, source_target_pairs={{0,16},{1,3},{2,18},{3,1},{4,20},{5,7},{6,22},{7,5},{8,24},{9,11},... | collective-permute-start | bytes 294920 | tf_op jit(solution)/shard_map/ppermute | solution.py:32
  63.0 4.7 %collective-permute-start.14 = (f32[2,32,384]{2,1,0:T(8,128)S(1)}, f32[2,32,384]{2,1,0:T(8,128)S(1)}, u32[]{:S(2)}, u32[]{:S(2)}) collective-permute-start(f32[2,32,384]{2,1,0:T(8,128)S(1)} %slice.55), channel_id=1, source_target_pairs={{0,4},{1,5},{2,6},{3,7},{4,0},{5,1},{6,2},{7,3},{8,12},{9,13},{10,... | collective-permute-start | bytes 294920 | tf_op jit(solution)/shard_map/ppermute | solution.py:32
  67.8 5.1 %collective-permute-start.15 = (f32[1,32,384]{2,1,0:T(8,128)S(1)}, f32[1,32,384]{2,1,0:T(8,128)S(1)}, u32[]{:S(2)}, u32[]{:S(2)}) collective-permute-start(f32[1,32,384]{2,1,0:T(8,128)S(1)} %slice.57), channel_id=1, source_target_pairs={{0,8},{1,9},{2,10},{3,11},{4,12},{5,13},{6,14},{7,15},{8,0},{9,1},... | collective-permute-start | bytes 147464 | tf_op jit(solution)/shard_map/ppermute | solution.py:32

commit v3 on v2

v3 whole, which is shorter than its diff:
```python
import jax
import jax.numpy as jnp
from jax import lax
from jax.experimental import pallas as pl
from jax.experimental.pallas import tpu as pltpu
from jax.sharding import PartitionSpec as P

BF = jnp.bfloat16
F32 = jnp.float32
BOTH = ("group", "shard")
MIB = 1 << 20
VM = pl.BlockSpec(memory_space=pltpu.VMEM)
SM = pl.BlockSpec(memory_space=pltpu.SMEM)


def dot(a, b, da, db):
    return lax.dot_general(a, b, (((da,), (db,)), ((), ())), preferred_element_type=F32)


def bits_of(size):
    return size.bit_length() - 1


def stage_masks(groups, shards):
    masks = [1 << k for k in range(bits_of(shards) - 1, 0, -1)] + [shards << k for k in range(bits_of(groups))]
    other = masks[:-2] + masks[-2:][::-1]
    return other, masks


def swap(x, groups, shards, masks):
    pairs = [(i, i ^ masks[i & 1]) for i in range(groups * shards)]
    return lax.ppermute(x, BOTH, pairs)


def relative(index, masks, top_first):
    count = len(masks)
    out = 0
    for step, mask in enumerate(masks):
        place = count - 1 - step if top_first else step
        out = out | (((index >> bits_of(mask)) & 1) << place)
    return out


def load_kernel(experts, *refs):
    count = len(experts)
    sources, targets, token, sems = refs[:count], refs[count + 1:2 * count + 1], refs[-2], refs[-1]
    copies = [pltpu.make_async_copy(sources[k].at[experts[k]], targets[k], sems.at[k]) for k in range(count)]
    for copy in copies:
        copy.start()
    token[...] = jnp.zeros_like(token)
    for copy in copies:
        copy.wait()


def load(weights, items, after):
    experts = [e for _, e in items]
    chosen = [weights[i] for i, _ in items]

    def kernel(*refs):
        load_kernel(experts, *refs)

    *arrays, token = pl.pallas_call(
        kernel,
        out_shape=tuple(pltpu.VMEM(w.shape[1:], BF) for w in chosen) + (pltpu.VMEM((8, 128), F32),),
        in_specs=[pl.BlockSpec(memory_space=pl.ANY)] * len(items) + [VM],
        out_specs=(VM,) * (len(items) + 1),
        scratch_shapes=[pltpu.SemaphoreType.DMA((len(items),))],
        compiler_params=pltpu.CompilerParams(vmem_limit_bytes=MIB),
        cost_estimate=pl.CostEstimate(flops=0, bytes_accessed=sum(2 * w.size // w.shape[0] for w in chosen), transcendentals=0),
        name="load",
    )(*(pltpu.with_memory_space_constraint(w, pltpu.HBM) for w in chosen), pltpu.with_memory_space_constraint(after, pltpu.VMEM))
    return arrays, token


def forward_kernel(gather_masks, scatter_masks, groups, shards, experts, early,
                   t0, t1, t2, t3, c0, c1, c2, c3, routes, *refs):
    loaded, sources = refs[:early], refs[early:early + 3]
    full, grads, keep, send, qt, gt, *stores, sems = refs[-10:]
    half, rows, width = t0.shape[0], t0.shape[1], t0.shape[2] // 2
    tokens = 2 * groups * rows
    hidden = grads.shape[2] // 2
    group, shard = lax.axis_index("group"), lax.axis_index("shard")
    core, me = shard & 1, group * shards + shard
    gather_at = [relative(me, masks, False) for masks in gather_masks]
    scatter_at = [relative(me, masks, True) for masks in scatter_masks]

    order = [(i, e) for e in range(experts) for i in range(3)]
    late = order[early:]
    waiting = list(late)

    def fetch(i, e):
        return pltpu.make_async_copy(sources[i].at[e], stores[i].at[e - (experts - stores[i].shape[0])], sems.at[i, e])

    def release(number):
        for i, e in waiting[:number]:
            fetch(i, e).start()
        del waiting[:number]

    def weight(i, e):
        if (i, e) in late:
            return stores[i].at[e - (experts - stores[i].shape[0])]
        return loaded[order.index((i, e))]

    def arrived(i, e):
        if (i, e) in waiting:
            release(waiting.index((i, e)) + 1)
        if (i, e) in late:
            fetch(i, e).wait()

    release(4 if early else 3)

    def columns(own, other, g, pair):
        at = g * shards + pair * 2
        blocks = []
        for parity in range(2):
            r = relative(at, gather_masks[parity], False) ^ gather_at[parity]
            low, high = jnp.minimum(r, half - 1), jnp.maximum(r - half, 0)
            mine, theirs = (jnp.where(r < half, a[0][low], a[1][high]) for a in (own, other))
            blocks.append(jnp.where(core == parity, mine, theirs))
        return jnp.concatenate([jnp.concatenate([block[:, k * width:(k + 1) * width] for block in blocks], axis=1) for k in range(2)], axis=0)

    for g in range(groups):
        for pair in range(shards // 2):
            at = (slice(2 * g * rows, 2 * (g + 1) * rows), slice(2 * pair * width, 2 * (pair + 1) * width))
            full[at] = columns((t0, t1), (t2, t3), g, pair)
    for pair in range(shards // 2):
        block = jnp.concatenate([columns((c0, c1), (c2, c3), g, pair) for g in range(groups)], axis=0)
        qt[2 * pair * width:2 * (pair + 1) * width, :] = block.T

    tables = [routes[g ^ group].T for g in range(groups)]
    table = jnp.concatenate(tables, axis=0)
    def grads_of(e):
        number = (group * experts + e).astype(F32)
        coef = jnp.where(table[:, 0:1] == number, table[:, 2:3], 0.0) + jnp.where(table[:, 1:2] == number, table[:, 3:4], 0.0)
        arrived(0, e)
        gate_pre = dot(full[...], weight(0, e)[...], 1, 0)
        arrived(1, e)
        up_value = dot(full[...], weight(1, e)[...], 1, 0)
        arrived(2, e)
        hidden_grad = dot(weight(2, e)[...], qt[...], 1, 0).T * coef
        s = 1.0 / (1.0 + jnp.exp(-gate_pre))
        gate_grad = (hidden_grad * up_value * s * (1.0 + gate_pre * (1.0 - s))).astype(BF)
        up_grad = (hidden_grad * (gate_pre * s)).astype(BF)
        grads[e, :, :hidden] = gate_grad
        grads[e, :, hidden:] = up_grad
        gt[e, :hidden, :] = gate_grad.T
        gt[e, hidden:, :] = up_grad.T

    for e in range(experts):
        grads_of(e)
        release(3)
    for pair in range(shards // 2):
        at = slice(2 * pair * width, 2 * (pair + 1) * width)
        parts = [dot(weight(i, e)[at, :], gt[e, i * hidden:(i + 1) * hidden, :], 1, 0) for e in range(experts) for i in range(2)]
        total = sum(parts[1:], parts[0])
        total = total.T
        for g in range(groups):
            at = g * shards + pair * 2
            first = relative(at, scatter_masks[0], True) ^ scatter_at[0]
            second = relative(at, scatter_masks[1], True) ^ scatter_at[1]
            block = total[2 * g * rows:2 * (g + 1) * rows, :]
            even, odd = (jnp.concatenate([block[:rows, k * width:(k + 1) * width], block[rows:, k * width:(k + 1) * width]], axis=1) for k in range(2))
            keep[jnp.where(core == 0, first, second)] = jnp.where(core == 0, even, odd)
            send[jnp.where(core == 0, second, first)] = jnp.where(core == 0, odd, even).astype(BF)


def pack_kernel(tokens, cotangent, packed):
    half = tokens.shape[0] // 2
    for i, a in enumerate((tokens, cotangent)):
        packed[i, 0] = jnp.concatenate([a[:half, :], a[half:, :]], axis=1)


def route_kernel(ids, weights, after, routes):
    routes[0] = jnp.zeros_like(routes[0])
    routes[0, 0:2, :] = ids[...].astype(F32)
    routes[0, 2:4, :] = weights[...]


def pack(tokens, cotangent):
    rows, width = tokens.shape
    return pl.pallas_call(
        pack_kernel,
        out_shape=pltpu.VMEM((2, 1, rows // 2, 2 * width), BF),
        in_specs=[VM] * 2,
        out_specs=VM,
        name="pack",
    )(tokens, cotangent)


def pack_routes(ids, weights, after):
    return pl.pallas_call(
        route_kernel,
        out_shape=pltpu.VMEM((1, 8, ids.shape[0]), F32),
        in_specs=[VM] * 2 + [pl.BlockSpec(memory_space=pl.ANY)],
        out_specs=VM,
        name="pack_routes",
    )(ids.T, weights.T, after)


def weight_kernel(units, blocks, transposed, *refs):
    rows, grads = refs[0], refs[1]
    if transposed:
        out_gate, out_up, token, made, sems = refs[-5:]
        xt = rows
    else:
        out_gate, out_up, token, xt, made, sems = refs[-6:]
        xt[...] = rows[...].T
    features, hidden = xt.shape[0], out_gate.shape[2]
    block = features // blocks
    copies = []
    for k, unit in enumerate(units):
        expert, j = divmod(unit, blocks)
        at = slice(j * block, (j + 1) * block)
        for i, out in enumerate((out_gate, out_up)):
            made[i, k] = dot(xt[at, :], grads[expert, :, i * hidden:(i + 1) * hidden], 1, 0).astype(BF)
            copies.append(pltpu.make_async_copy(made.at[i, k], out.at[expert, at, :], sems.at[i, k]))
            copies[-1].start()
    token[...] = jnp.zeros_like(token)
    for copy in copies:
        copy.wait()


def weight_grads(rows, grads, after, so_far, units, blocks, shape, piece):
    experts, features, hidden = shape
    transposed = bool(so_far)
    array, zero = jax.ShapeDtypeStruct(shape, BF), pltpu.VMEM((1,) + piece[1:], F32)
    anywhere = pl.BlockSpec(memory_space=pl.ANY)

    def kernel(*refs):
        weight_kernel(units, blocks, transposed, *refs)

    return pl.pallas_call(
        kernel,
        out_shape=(array, array, zero) + (() if transposed else (pltpu.VMEM((features, rows.shape[0]), BF),)),
        in_specs=[VM] * 3 + [anywhere] * len(so_far),
        out_specs=(anywhere, anywhere, VM) + (() if transposed else (VM,)),
        input_output_aliases={3: 0, 4: 1} if transposed else {},
        scratch_shapes=[pltpu.VMEM((2, len(units), features // blocks, hidden), BF), pltpu.SemaphoreType.DMA((2, len(units)))],
        compiler_params=pltpu.CompilerParams(vmem_limit_bytes=16 * MIB),
        cost_estimate=pl.CostEstimate(flops=4 * features * grads.shape[1] * hidden, bytes_accessed=4 * features * hidden, transcendentals=0),
        name="weight_grads",
    )(*(pltpu.with_memory_space_constraint(a, pltpu.VMEM) for a in (rows, grads, after)), *so_far)


def body(tokens, cotangent, expert_ids, route_weight, w_gate, w_up, w_down):
    groups, shards = lax.axis_size("group"), lax.axis_size("shard")
    experts, features, hidden = w_gate.shape
    rows, width = tokens.shape
    half_rows = rows // 2
    gather_masks = stage_masks(groups, shards)
    scatter_masks = tuple(m[::-1] for m in gather_masks)
    count = len(gather_masks[0])
    pairs = groups * shards // 2

    def step_masks(masks, step):
        return masks[0][step], masks[1][step]

    packed = pack(tokens, cotangent)
    routes = pack_routes(expert_ids, route_weight, packed)
    def exchange(r):
        for k in range(bits_of(groups)):
            r = jnp.concatenate([r, swap(r, groups, shards, (shards << k,) * 2)], 0)
        return r

    routes = exchange(routes)
    weights = (w_gate, w_up, w_down)
    order = [(i, e) for e in range(experts) for i in range(3)]
    parts = (order[:2], order[2:6], order[6:9]) if experts > 3 else ((), (), ())
    early = sum(len(part) for part in parts)
    loaded, fences = [], []
    for step in range(count - 1):
        before, part = packed, parts[step - count + 3] if step > count - 4 else ()
        packed = jnp.concatenate([packed, swap(packed, groups, shards, step_masks(gather_masks, step))], 1)
        if part:
            arrays, token = load(weights, part, before)
            loaded += arrays
            packed, token = lax.optimization_barrier((packed, token))
            fences.append(token)
        if step == count - 3:
            packed, routes = lax.optimization_barrier((packed, routes))
    chains = [packed[0], packed[1]]
    highs = [swap(a, groups, shards, step_masks(gather_masks, count - 1)) for a in chains]
    others = [swap(a, groups, shards, (1, 1)) for a in chains]
    if parts[2]:
        arrays, token = load(weights, parts[2], others[1])
        loaded += arrays
        highs[0], token = lax.optimization_barrier((highs[0], token))
        fences.append(token)
    gathered = []
    for low, high, other in zip(chains, highs, others):
        gathered += [low, high, other, swap(high, groups, shards, (1, 1))]
    total_rows = groups * rows
    gathered = [pltpu.with_memory_space_constraint(a, pltpu.VMEM) for a in gathered + [routes]]
    piece = (pairs, half_rows, 2 * width)

    def forward(*refs):
        forward_kernel(gather_masks, scatter_masks, groups, shards, experts, early, *refs)

    loaded = [pltpu.with_memory_space_constraint(a, pltpu.VMEM) for a in loaded]
    full, grads, keep, send = pl.pallas_call(
        forward,
        out_shape=(pltpu.VMEM((total_rows, features), BF), pltpu.VMEM((experts, total_rows, 2 * hidden), BF),
                   pltpu.VMEM(piece, F32), pltpu.VMEM(piece, BF)),
        in_specs=[VM] * (9 + len(loaded)) + [pl.BlockSpec(memory_space=pl.ANY)] * (3 + len(fences)),
        out_specs=(VM,) * 4,
        scratch_shapes=[pltpu.VMEM((features, total_rows), BF), pltpu.VMEM((experts, 2 * hidden, total_rows), BF)]
        + [pltpu.VMEM((sum(j == i for j, _ in order[early:]),) + w.shape[1:], BF) for i, w in enumerate(weights)] + [pltpu.SemaphoreType.DMA((3, experts))],
        compiler_params=pltpu.CompilerParams(vmem_limit_bytes=2 * (3 * experts - early) * features * hidden + 20 * total_rows * features + 4 * MIB),
        cost_estimate=pl.CostEstimate(flops=10 * experts * total_rows * features * hidden, bytes_accessed=6 * experts * features * hidden, transcendentals=0),
        name="forward",
    )(*gathered, *loaded, *(pltpu.with_memory_space_constraint(w, pltpu.HBM) for w in weights), *fences)

    blocks = 8
    shares = [3, 10, 8] + [5] * (count - 2)
    ends = [experts * blocks * sum(shares[:i + 1]) // sum(shares) for i in range(len(shares))]
    so_far, source, after = (), full, send
    kept = None
    for step in range(count + 1):
        units = list(range(ends[step - 1] if step else 0, ends[step]))
        grad_gate, grad_up, token, *made = weight_grads(source, grads, after, so_far, units, blocks, w_gate.shape, piece)
        so_far, source = (grad_gate, grad_up), made[0] if made else source
        if step == 0:
            kept = keep + swap(send, groups, shards, (1, 1)).astype(F32) + token
        else:
            half = kept.shape[0] // 2
            sent = kept[half:]
            if 2 * (step - 1) < count:
                sent = sent.astype(BF)
            kept = kept[:half] + swap(sent, groups, shards, step_masks(scatter_masks, step - 1)).astype(F32) + token
        after = kept
    done = kept[0].astype(BF)
    grad_tokens = jnp.concatenate([done[:, :width], done[:, width:]], 0)
    return grad_tokens, grad_gate, grad_up


def solution(mesh):
    in_specs = (
        P("group", "shard"),
        P("group", "shard"),
        P("group", None),
        P("group", None),
        P("group", None, "shard"),
        P("group", None, "shard"),
        P("group", "shard", None),
    )
    out_specs = (P("group", "shard"), P("group", None, "shard"), P("group", None, "shard"))
    return jax.shard_map(body, mesh=mesh, in_specs=in_specs, out_specs=out_specs, check_vma=False)
```

time: 73.7 us -> 70.1 us (0.951)
  waiting for transfers between devices: 15.2 us -> 6.32 us
  Pallas kernels: 36.1 us -> 42.6 us
  starting transfers between devices: 20.3 us -> 18.2 us
  other arithmetic: 0.92 us -> 1.74 us
    pallas_call x1 -> x5, Pallas kernels: 0.85 us -> 12.9 us  [the longest x3 11.3 us: load(): pl.pallas_call(kernel, out_shape=tuple((pltpu.VMEM(w.shape[1:], BF) for w...]
    ppermute x16 -> x15, waiting for transfers between devices: 15.2 us -> 6.32 us  [swap(): return lax.ppermute(x, BOTH, pairs)]
    pallas_call x1, Pallas kernels: 22.2 us -> 16.6 us  [body(): pl.pallas_call(forward, out_shape=(pltpu.VMEM((total_rows, features), BF)...]
    ppermute x16 -> x15, starting transfers between devices: 20.3 us -> 18.2 us  [swap(): return lax.ppermute(x, BOTH, pairs)]
    concatenate x2 -> x3, other arithmetic: 0.04 us -> 0.89 us  [body(): jnp.concatenate([packed, swap(packed, groups, shards, step_masks(gather_m...]
  transfers between devices with their start and end apart: 16 -> 15, of which waited for: 10 -> 8; matrix products, arithmetic and copies ran while one was open for 0% -> 1% of each run, Pallas kernels for 18% -> 36%
where the time goes in v3:
time: 70.1 us; the launch traced here: 69.9 us
  Pallas kernels  42.6 us (61%)
  starting transfers between devices  18.2 us (26%)
  waiting for transfers between devices  6.32 us (9%)
  other arithmetic  1.74 us (2%)
  between operations  0.86 us (1%)
    ppermute x15, starting transfers between devices, swap(): return lax.ppermute(x, BOTH, pairs)  18.2 us
    pallas_call x1, Pallas kernels, body(): pl.pallas_call(forward, out_shape=(pltpu.VMEM((total_rows, features), BF)...  16.6 us
    pallas_call x5, Pallas kernels, weight_grads(): pl.pallas_call(kernel, out_shape=(array, array, zero) + (() if transposed...  13.1 us
    pallas_call x3, Pallas kernels, load(): pl.pallas_call(kernel, out_shape=tuple((pltpu.VMEM(w.shape[1:], BF) for w...  11.3 us
    ppermute x15, waiting for transfers between devices, swap(): return lax.ppermute(x, BOTH, pairs)  6.32 us
  transfers between devices with their start and end apart: 15, of which 8 were waited for; matrix products, arithmetic and copies ran while one was open for 1% of the time, Pallas kernels for 36%

profile of v3, /device:TPU:0, one launch (start us, length us, event | category | flops | bytes accessed | tf_op | source)
XLA Modules:
  0.0 69.9 jit_solution(15109834494201794644)
XLA Ops:
  0.6 0.9 %pack.1.after = bf16[2,1,32,384]{3,2,1,0:T(8,128)(2,1)S(1)} custom-call(bf16[64,192]{1,0:T(8,128)(2,1)} %tokens.1, bf16[64,192]{1,0:T(8,128)(2,1)} %cotangent.1), custom_call_target="tpu_custom_call" | custom-call | tf_op jit(solution)/shard_map/pack/pallas_call | solution.py:181
  1.5 4.1 %collective-permute-start = (bf16[2,1,32,384]{3,2,1,0:T(8,128)(2,1)S(1)}, bf16[2,1,32,384]{3,2,1,0:T(8,128)(2,1)S(1)}, u32[]{:S(2)}, u32[]{:S(2)}) collective-permute-start(bf16[2,1,32,384]{3,2,1,0:T(8,128)(2,1)S(1)} %pack.1.after), channel_id=1, source_target_pairs={{0,8},{1,9},{2,10},{3,11},{4,12},{5,13},{6,14},{7,15},{8,0},{9,1},... | collective-permute-start | bytes 147464 | tf_op jit(solution)/shard_map/ppermute | solution.py:32
  5.6 0.7 pack_routes.1
  6.3 1.5 %collective-permute-start.2 = (f32[1,8,64]{2,1,0:T(8,128)S(1)}, f32[1,8,64]{2,1,0:T(8,128)S(1)}, u32[]{:S(2)}, u32[]{:S(2)}) collective-permute-start(f32[1,8,64]{2,1,0:T(8,128)S(1)} %pack_routes.1), channel_id=1, source_target_pairs={{0,16},{1,17},{2,18},{3,19},{4,20},{5,21},{6,22},{7,23},{8,24},{9,... | collective-permute-start | bytes 6152 | tf_op jit(solution)/shard_map/ppermute | solution.py:32
  8.2 0.8 %pad_maximum_fusion.2.refs_2_ = bf16[2,2,32,384]{3,2,1,0:T(8,128)(2,1)S(1)} fusion(bf16[2,1,32,384]{3,2,1,0:T(8,128)(2,1)S(1)} %collective-permute-done, bf16[2,1,32,384]{3,2,1,0:T(8,128)(2,1)} %copy-done), kind=kLoop, calls=%fused_computation.13 | loop fusion | flops 49152 | bytes 196608 | tf_op jit(solution)/shard_map/concatenate | solution.py:273
  9.0 1.4 %collective-permute-start.1 = (bf16[2,2,32,384]{3,2,1,0:T(8,128)(2,1)S(1)}, bf16[2,2,32,384]{3,2,1,0:T(8,128)(2,1)S(1)}, u32[]{:S(2)}, u32[]{:S(2)}) collective-permute-start(bf16[2,2,32,384]{3,2,1,0:T(8,128)(2,1)S(1)} %pad_maximum_fusion.2.refs_2_), channel_id=1, source_target_pairs={{0,4},{1,5},{2,6},{3,7},{4,0},{5,1},{6,2},{7,3},{8,12},{9,13},{10,... | collective-permute-start | bytes 294920 | tf_op jit(solution)/shard_map/ppermute | solution.py:32
  10.5 2.9 %load.3 = (bf16[3072,512]{1,0:T(8,128)(2,1)S(1)}, bf16[3072,512]{1,0:T(8,128)(2,1)S(1)}, f32[8,128]{1,0:T(8,128)S(1)}) custom-call(bf16[4,3072,512]{2,1,0:T(8,128)(2,1)} %refs_18_.1, bf16[4,3072,512]{2,1,0:T(8,128)(2,1)} %refs_19_.1, bf16[2,2,32,384]{3,2,1,0:T(8,128)(2,1)S(1)} %pad_maximum_fusion.2.refs_2_), custom_call_target="tpu_custom_call" | custom-call | bytes 6291456 | tf_op jit(solution)/shard_map/load/pallas_call | solution.py:62
  13.7 1.8 %collective-permute-start.3 = (bf16[2,4,32,384]{3,2,1,0:T(8,128)(2,1)S(1)}, bf16[2,4,32,384]{3,2,1,0:T(8,128)(2,1)S(1)}, u32[]{:S(2)}, u32[]{:S(2)}) collective-permute-start(bf16[2,4,32,384]{3,2,1,0:T(8,128)(2,1)S(1)} %pad_maximum_fusion.1.refs_4_), channel_id=1, source_target_pairs={{0,16},{1,3},{2,18},{3,1},{4,20},{5,7},{6,22},{7,5},{8,24},{9,11},... | collective-permute-start | bytes 589832 | tf_op jit(solution)/shard_map/ppermute | solution.py:32
  15.5 4.7 %load.4 = (bf16[512,3072]{1,0:T(8,128)(2,1)S(1)}, bf16[3072,512]{1,0:T(8,128)(2,1)S(1)}, bf16[3072,512]{1,0:T(8,128)(2,1)S(1)}, bf16[512,3072]{1,0:T(8,128)(2,1)S(1)}, f32[8,128]{1,0:T(8,128)S(1)}) custom-call(bf16[4,512,3072]{2,1,0:T(8,128)(2,1)} %refs_20_.1, bf16[4,3072,512]{2,1,0:T(8,128)(2,1)} %refs_18_.1, bf16[4,3072,512]{2,1,0:T(8,128)(2,1)} %refs_19_.1, ...), custom_call_target="tpu_custom_call" | custom-call | bytes 12582912 | tf_op jit(solution)/shard_map/load/pallas_call | solution.py:62
  20.4 1.6 %collective-permute-start.4 = (bf16[8,32,384]{2,1,0:T(8,128)(2,1)S(1)}, bf16[8,32,384]{2,1,0:T(8,128)(2,1)S(1)}, u32[]{:S(2)}, u32[]{:S(2)}) collective-permute-start(bf16[8,32,384]{2,1,0:T(8,128)(2,1)S(1)} %get-tuple-element.84.refs_0_), channel_id=1, source_target_pairs={{0,2},{1,17},{2,0},{3,19},{4,6},{5,21},{6,4},{7,23},{8,10},{9,25},... | collective-permute-start | bytes 589832 | tf_op jit(solution)/shard_map/ppermute | solution.py:32
  22.5 3.8 %load.5 = (bf16[3072,512]{1,0:T(8,128)(2,1)S(1)}, bf16[3072,512]{1,0:T(8,128)(2,1)S(1)}, bf16[512,3072]{1,0:T(8,128)(2,1)S(1)}, f32[8,128]{1,0:T(8,128)S(1)}) custom-call(bf16[4,3072,512]{2,1,0:T(8,128)(2,1)} %refs_18_.1, bf16[4,3072,512]{2,1,0:T(8,128)(2,1)} %refs_19_.1, bf16[4,512,3072]{2,1,0:T(8,128)(2,1)} %refs_20_.1, ...), custom_call_target="tpu_custom_call" | custom-call | bytes 9437184 | tf_op jit(solution)/shard_map/load/pallas_call | solution.py:62
  26.3 1.9 %collective-permute-done.8.refs_5_ = bf16[8,32,384]{2,1,0:T(8,128)(2,1)S(1)} collective-permute-done((bf16[8,32,384]{2,1,0:T(8,128)(2,1)S(1)}, bf16[8,32,384]{2,1,0:T(8,128)(2,1)S(1)}, u32[]{:S(2)}, u32[]{:S(2)}) %collective-permute-start.8) | collective-permute-done | bytes 196640 | tf_op jit(solution)/shard_map/ppermute | solution.py:32
  28.7 0.9 %collective-permute-done.9.refs_7_ = bf16[8,32,384]{2,1,0:T(8,128)(2,1)S(1)} collective-permute-done((bf16[8,32,384]{2,1,0:T(8,128)(2,1)S(1)}, bf16[8,32,384]{2,1,0:T(8,128)(2,1)S(1)}, u32[]{:S(2)}, u32[]{:S(2)}) %collective-permute-start.9) | collective-permute-done | bytes 196640 | tf_op jit(solution)/shard_map/ppermute | solution.py:32
  29.9 16.6 %forward.1 = (bf16[128,3072]{1,0:T(8,128)(2,1)S(1)}, bf16[4,128,1024]{2,1,0:T(8,128)(2,1)S(1)}, f32[16,32,384]{2,1,0:T(8,128)S(1)}, bf16[16,32,384]{2,1,0:T(8,128)(2,1)S(1)}) custom-call(bf16[8,32,384]{2,1,0:T(8,128)(2,1)S(1)} %get-tuple-element.84.refs_0_, bf16[8,32,384]{2,1,0:T(8,128)(2,1)S(1)} %collective-permute-done.4.refs_1_, ...), custom_call_target="tpu_custom_call" | custom-call | flops 8053063680 | bytes 37748736 | tf_op jit(solution)/shard_map/forward/pallas_call | solution.py:300
  46.9 1.7 %weight_grads.5 = (bf16[4,3072,512]{2,1,0:T(8,128)(2,1)}, bf16[4,3072,512]{2,1,0:T(8,128)(2,1)}, f32[1,32,384]{2,1,0:T(8,128)S(1)}, bf16[3072,128]{1,0:T(8,128)(2,1)S(1)}) custom-call(bf16[128,3072]{1,0:T(8,128)(2,1)S(1)} %get-tuple-element.65.refs_0_, bf16[4,128,1024]{2,1,0:T(8,128)(2,1)S(1)} %get-tuple-element.66.refs_1_, ...), custom_call_target="tpu_custom_call" | custom-call | flops 805306368 | bytes 6291456 | tf_op jit(solution)/shard_map/weight_grads/pallas_call | solution.py:232
  48.8 1.6 %collective-permute-start.11 = (bf16[8,32,384]{2,1,0:T(8,128)(2,1)S(1)}, bf16[8,32,384]{2,1,0:T(8,128)(2,1)S(1)}, u32[]{:S(2)}, u32[]{:S(2)}) collective-permute-start(bf16[8,32,384]{2,1,0:T(8,128)(2,1)S(1)} %slice.80), channel_id=1, source_target_pairs={{0,2},{1,17},{2,0},{3,19},{4,6},{5,21},{6,4},{7,23},{8,10},{9,25},... | collective-permute-start | bytes 589832 | tf_op jit(solution)/shard_map/ppermute | solution.py:32
  50.4 3.5 %weight_grads.6 = (bf16[4,3072,512]{2,1,0:T(8,128)(2,1)}, bf16[4,3072,512]{2,1,0:T(8,128)(2,1)}, f32[1,32,384]{2,1,0:T(8,128)S(1)}) custom-call(bf16[3072,128]{1,0:T(8,128)(2,1)S(1)} %get-tuple-element.68.refs_0_, bf16[4,128,1024]{2,1,0:T(8,128)(2,1)S(1)} %get-tuple-element.66.refs_1_, ...), custom_call_target="tpu_custom_call", output_to_operand_aliasing={{0}: (3, {}), {1}: (4, {})} | custom-call | flops 805306368 | bytes 6291456 | tf_op jit(solution)/shard_map/weight_grads/pallas_call | solution.py:232
  54.6 1.0 %collective-permute-start.12 = (bf16[4,32,384]{2,1,0:T(8,128)(2,1)S(1)}, bf16[4,32,384]{2,1,0:T(8,128)(2,1)S(1)}, u32[]{:S(2)}, u32[]{:S(2)}) collective-permute-start(bf16[4,32,384]{2,1,0:T(8,128)(2,1)S(1)} %slice.81), channel_id=1, source_target_pairs={{0,16},{1,3},{2,18},{3,1},{4,20},{5,7},{6,22},{7,5},{8,24},{9,11},... | collective-permute-start | bytes 294920 | tf_op jit(solution)/shard_map/ppermute | solution.py:32
  55.7 3.0 %weight_grads.7 = (bf16[4,3072,512]{2,1,0:T(8,128)(2,1)}, bf16[4,3072,512]{2,1,0:T(8,128)(2,1)}, f32[1,32,384]{2,1,0:T(8,128)S(1)}) custom-call(bf16[3072,128]{1,0:T(8,128)(2,1)S(1)} %get-tuple-element.68.refs_0_, bf16[4,128,1024]{2,1,0:T(8,128)(2,1)S(1)} %get-tuple-element.66.refs_1_, ...), custom_call_target="tpu_custom_call", output_to_operand_aliasing={{0}: (3, {}), {1}: (4, {})} | custom-call | flops 805306368 | bytes 6291456 | tf_op jit(solution)/shard_map/weight_grads/pallas_call | solution.py:232
  59.3 1.2 %collective-permute-start.13 = (f32[2,32,384]{2,1,0:T(8,128)S(1)}, f32[2,32,384]{2,1,0:T(8,128)S(1)}, u32[]{:S(2)}, u32[]{:S(2)}) collective-permute-start(f32[2,32,384]{2,1,0:T(8,128)S(1)} %slice.55), channel_id=1, source_target_pairs={{0,4},{1,5},{2,6},{3,7},{4,0},{5,1},{6,2},{7,3},{8,12},{9,13},{10,... | collective-permute-start | bytes 294920 | tf_op jit(solution)/shard_map/ppermute | solution.py:32
  60.6 2.2 %weight_grads.8 = (bf16[4,3072,512]{2,1,0:T(8,128)(2,1)}, bf16[4,3072,512]{2,1,0:T(8,128)(2,1)}, f32[1,32,384]{2,1,0:T(8,128)S(1)}) custom-call(bf16[3072,128]{1,0:T(8,128)(2,1)S(1)} %get-tuple-element.68.refs_0_, bf16[4,128,1024]{2,1,0:T(8,128)(2,1)S(1)} %get-tuple-element.66.refs_1_, ...), custom_call_target="tpu_custom_call", output_to_operand_aliasing={{0}: (3, {}), {1}: (4, {})} | custom-call | flops 805306368 | bytes 6291456 | tf_op jit(solution)/shard_map/weight_grads/pallas_call | solution.py:232
  62.8 1.2 %collective-permute-done.13 = f32[2,32,384]{2,1,0:T(8,128)S(1)} collective-permute-done((f32[2,32,384]{2,1,0:T(8,128)S(1)}, f32[2,32,384]{2,1,0:T(8,128)S(1)}, u32[]{:S(2)}, u32[]{:S(2)}) %collective-permute-start.13) | collective-permute-done | bytes 98336 | tf_op jit(solution)/shard_map/ppermute | solution.py:32
  64.1 2.5 %collective-permute-start.14 = (f32[1,32,384]{2,1,0:T(8,128)S(1)}, f32[1,32,384]{2,1,0:T(8,128)S(1)}, u32[]{:S(2)}, u32[]{:S(2)}) collective-permute-start(f32[1,32,384]{2,1,0:T(8,128)S(1)} %slice.57), channel_id=1, source_target_pairs={{0,8},{1,9},{2,10},{3,11},{4,12},{5,13},{6,14},{7,15},{8,0},{9,1},... | collective-permute-start | bytes 147464 | tf_op jit(solution)/shard_map/ppermute | solution.py:32
  66.6 2.5 %weight_grads.9 = (bf16[4,3072,512]{2,1,0:T(8,128)(2,1)}, bf16[4,3072,512]{2,1,0:T(8,128)(2,1)}, f32[1,32,384]{2,1,0:T(8,128)S(1)}) custom-call(bf16[3072,128]{1,0:T(8,128)(2,1)S(1)} %get-tuple-element.68.refs_0_, bf16[4,128,1024]{2,1,0:T(8,128)(2,1)S(1)} %get-tuple-element.66.refs_1_, ...), custom_call_target="tpu_custom_call", output_to_operand_aliasing={{0}: (3, {}), {1}: (4, {})} | custom-call | flops 805306368 | bytes 6291456 | tf_op jit(solution)/shard_map/weight_grads/pallas_call | solution.py:232
  (37 shorter events, 4.7 us)
Async XLA Ops:
  1.5 4.1 %copy-start = (bf16[2,1,32,384]{3,2,1,0:T(8,128)(2,1)}, bf16[2,1,32,384]{3,2,1,0:T(8,128)(2,1)S(1)}, u32[]{:S(2)}) copy-start(bf16[2,1,32,384]{3,2,1,0:T(8,128)(2,1)S(1)} %pack.1.after) | copy-start | bytes 147460
  1.5 6.7 %collective-permute-start = (bf16[2,1,32,384]{3,2,1,0:T(8,128)(2,1)S(1)}, bf16[2,1,32,384]{3,2,1,0:T(8,128)(2,1)S(1)}, u32[]{:S(2)}, u32[]{:S(2)}) collective-permute-start(bf16[2,1,32,384]{3,2,1,0:T(8,128)(2,1)S(1)} %pack.1.after), channel_id=1, source_target_pairs={{0,8},{1,9},{2,10},{3,11},{4,12},{5,13},{6,14},{7,15},{8,0},{9,1},... | collective-permute-start | bytes 147464 | tf_op jit(solution)/shard_map/ppermute | solution.py:32
  6.3 4.2 %collective-permute-start.2 = (f32[1,8,64]{2,1,0:T(8,128)S(1)}, f32[1,8,64]{2,1,0:T(8,128)S(1)}, u32[]{:S(2)}, u32[]{:S(2)}) collective-permute-start(f32[1,8,64]{2,1,0:T(8,128)S(1)} %pack_routes.1), channel_id=1, source_target_pairs={{0,16},{1,17},{2,18},{3,19},{4,20},{5,21},{6,22},{7,23},{8,24},{9,... | collective-permute-start | bytes 6152 | tf_op jit(solution)/shard_map/ppermute | solution.py:32
  9.0 4.7 %collective-permute-start.1 = (bf16[2,2,32,384]{3,2,1,0:T(8,128)(2,1)S(1)}, bf16[2,2,32,384]{3,2,1,0:T(8,128)(2,1)S(1)}, u32[]{:S(2)}, u32[]{:S(2)}) collective-permute-start(bf16[2,2,32,384]{3,2,1,0:T(8,128)(2,1)S(1)} %pad_maximum_fusion.2.refs_2_), channel_id=1, source_target_pairs={{0,4},{1,5},{2,6},{3,7},{4,0},{5,1},{6,2},{7,3},{8,12},{9,13},{10,... | collective-permute-start | bytes 294920 | tf_op jit(solution)/shard_map/ppermute | solution.py:32
  10.5 3.2 %copy-start.1 = (bf16[2,1,32,384]{3,2,1,0:T(8,128)(2,1)S(1)}, bf16[2,1,32,384]{3,2,1,0:T(8,128)(2,1)}, u32[]{:S(2)}) copy-start(bf16[2,1,32,384]{3,2,1,0:T(8,128)(2,1)} %copy-done) | copy-start | bytes 147460
  13.7 6.5 %collective-permute-start.3 = (bf16[2,4,32,384]{3,2,1,0:T(8,128)(2,1)S(1)}, bf16[2,4,32,384]{3,2,1,0:T(8,128)(2,1)S(1)}, u32[]{:S(2)}, u32[]{:S(2)}) collective-permute-start(bf16[2,4,32,384]{3,2,1,0:T(8,128)(2,1)S(1)} %pad_maximum_fusion.1.refs_4_), channel_id=1, source_target_pairs={{0,16},{1,3},{2,18},{3,1},{4,20},{5,7},{6,22},{7,5},{8,24},{9,11},... | collective-permute-start | bytes 589832 | tf_op jit(solution)/shard_map/ppermute | solution.py:32
  20.3 2.2 %collective-permute-start.5 = (bf16[8,32,384]{2,1,0:T(8,128)(2,1)S(1)}, bf16[8,32,384]{2,1,0:T(8,128)(2,1)S(1)}, u32[]{:S(2)}, u32[]{:S(2)}) collective-permute-start(bf16[8,32,384]{2,1,0:T(8,128)(2,1)S(1)} %get-tuple-element.83.refs_4_), channel_id=1, source_target_pairs={{0,1},{1,0},{2,3},{3,2},{4,5},{5,4},{6,7},{7,6},{8,9},{9,8},{10,11... | collective-permute-start | bytes 589832 | tf_op jit(solution)/shard_map/ppermute | solution.py:32
  20.4 5.9 %collective-permute-start.4 = (bf16[8,32,384]{2,1,0:T(8,128)(2,1)S(1)}, bf16[8,32,384]{2,1,0:T(8,128)(2,1)S(1)}, u32[]{:S(2)}, u32[]{:S(2)}) collective-permute-start(bf16[8,32,384]{2,1,0:T(8,128)(2,1)S(1)} %get-tuple-element.84.refs_0_), channel_id=1, source_target_pairs={{0,2},{1,17},{2,0},{3,19},{4,6},{5,21},{6,4},{7,23},{8,10},{9,25},... | collective-permute-start | bytes 589832 | tf_op jit(solution)/shard_map/ppermute | solution.py:32
  22.0 6.3 %collective-permute-start.8 = (bf16[8,32,384]{2,1,0:T(8,128)(2,1)S(1)}, bf16[8,32,384]{2,1,0:T(8,128)(2,1)S(1)}, u32[]{:S(2)}, u32[]{:S(2)}) collective-permute-start(bf16[8,32,384]{2,1,0:T(8,128)(2,1)S(1)} %get-tuple-element.83.refs_4_), channel_id=1, source_target_pairs={{0,2},{1,17},{2,0},{3,19},{4,6},{5,21},{6,4},{7,23},{8,10},{9,25},... | collective-permute-start | bytes 589832 | tf_op jit(solution)/shard_map/ppermute | solution.py:32
  22.5 6.3 %collective-permute-start.6 = (bf16[8,32,384]{2,1,0:T(8,128)(2,1)S(1)}, bf16[8,32,384]{2,1,0:T(8,128)(2,1)S(1)}, u32[]{:S(2)}, u32[]{:S(2)}) collective-permute-start(bf16[8,32,384]{2,1,0:T(8,128)(2,1)S(1)} %get-tuple-element.84.refs_0_), channel_id=1, source_target_pairs={{0,1},{1,0},{2,3},{3,2},{4,5},{5,4},{6,7},{7,6},{8,9},{9,8},{10,11... | collective-permute-start | bytes 589832 | tf_op jit(solution)/shard_map/ppermute | solution.py:32
  28.2 1.4 %collective-permute-start.9 = (bf16[8,32,384]{2,1,0:T(8,128)(2,1)S(1)}, bf16[8,32,384]{2,1,0:T(8,128)(2,1)S(1)}, u32[]{:S(2)}, u32[]{:S(2)}) collective-permute-start(bf16[8,32,384]{2,1,0:T(8,128)(2,1)S(1)} %collective-permute-done.8.refs_5_), channel_id=1, source_target_pairs={{0,1},{1,0},{2,3},{3,2},{4,5},{5,4},{6,7},{7,6},{8,9},{9,8},{10,11... | collective-permute-start | bytes 589832 | tf_op jit(solution)/shard_map/ppermute | solution.py:32
  28.2 1.7 %collective-permute-start.7 = (bf16[8,32,384]{2,1,0:T(8,128)(2,1)S(1)}, bf16[8,32,384]{2,1,0:T(8,128)(2,1)S(1)}, u32[]{:S(2)}, u32[]{:S(2)}) collective-permute-start(bf16[8,32,384]{2,1,0:T(8,128)(2,1)S(1)} %collective-permute-done.4.refs_1_), channel_id=1, source_target_pairs={{0,1},{1,0},{2,3},{3,2},{4,5},{5,4},{6,7},{7,6},{8,9},{9,8},{10,11... | collective-permute-start | bytes 589832 | tf_op jit(solution)/shard_map/ppermute | solution.py:32
  46.6 2.1 %collective-permute-start.10 = (bf16[16,32,384]{2,1,0:T(8,128)(2,1)S(1)}, bf16[16,32,384]{2,1,0:T(8,128)(2,1)S(1)}, u32[]{:S(2)}, u32[]{:S(2)}) collective-permute-start(bf16[16,32,384]{2,1,0:T(8,128)(2,1)S(1)} %get-tuple-element.64.refs_2_), channel_id=1, source_target_pairs={{0,1},{1,0},{2,3},{3,2},{4,5},{5,4},{6,7},{7,6},{8,9},{9,8},{10,11... | collective-permute-start | bytes 1179656 | tf_op jit(solution)/shard_map/ppermute | solution.py:32
  48.8 5.7 %collective-permute-start.11 = (bf16[8,32,384]{2,1,0:T(8,128)(2,1)S(1)}, bf16[8,32,384]{2,1,0:T(8,128)(2,1)S(1)}, u32[]{:S(2)}, u32[]{:S(2)}) collective-permute-start(bf16[8,32,384]{2,1,0:T(8,128)(2,1)S(1)} %slice.80), channel_id=1, source_target_pairs={{0,2},{1,17},{2,0},{3,19},{4,6},{5,21},{6,4},{7,23},{8,10},{9,25},... | collective-permute-start | bytes 589832 | tf_op jit(solution)/shard_map/ppermute | solution.py:32
  54.6 4.7 %collective-permute-start.12 = (bf16[4,32,384]{2,1,0:T(8,128)(2,1)S(1)}, bf16[4,32,384]{2,1,0:T(8,128)(2,1)S(1)}, u32[]{:S(2)}, u32[]{:S(2)}) collective-permute-start(bf16[4,32,384]{2,1,0:T(8,128)(2,1)S(1)} %slice.81), channel_id=1, source_target_pairs={{0,16},{1,3},{2,18},{3,1},{4,20},{5,7},{6,22},{7,5},{8,24},{9,11},... | collective-permute-start | bytes 294920 | tf_op jit(solution)/shard_map/ppermute | solution.py:32
  59.3 4.7 %collective-permute-start.13 = (f32[2,32,384]{2,1,0:T(8,128)S(1)}, f32[2,32,384]{2,1,0:T(8,128)S(1)}, u32[]{:S(2)}, u32[]{:S(2)}) collective-permute-start(f32[2,32,384]{2,1,0:T(8,128)S(1)} %slice.55), channel_id=1, source_target_pairs={{0,4},{1,5},{2,6},{3,7},{4,0},{5,1},{6,2},{7,3},{8,12},{9,13},{10,... | collective-permute-start | bytes 294920 | tf_op jit(solution)/shard_map/ppermute | solution.py:32
  64.1 5.1 %collective-permute-start.14 = (f32[1,32,384]{2,1,0:T(8,128)S(1)}, f32[1,32,384]{2,1,0:T(8,128)S(1)}, u32[]{:S(2)}, u32[]{:S(2)}) collective-permute-start(f32[1,32,384]{2,1,0:T(8,128)S(1)} %slice.57), channel_id=1, source_target_pairs={{0,8},{1,9},{2,10},{3,11},{4,12},{5,13},{6,14},{7,15},{8,0},{9,1},... | collective-permute-start | bytes 147464 | tf_op jit(solution)/shard_map/ppermute | solution.py:32

commit v4 on v3

--- a/solution.py
+++ b/solution.py
@@ -72,16 +72,50 @@
     return arrays, token
 
 
+def chip_columns(gather_masks, groups, shards, own, other, g, pair):
+    half, width = own[0].shape[0], own[0].shape[2] // 2
+    group, shard = lax.axis_index("group"), lax.axis_index("shard")
+    core, me = shard & 1, group * shards + shard
+    at = g * shards + pair * 2
+    blocks = []
+    for parity in range(2):
+        r = relative(at, gather_masks[parity], False) ^ relative(me, gather_masks[parity], False)
+        low, high = jnp.minimum(r, half - 1), jnp.maximum(r - half, 0)
+        mine, theirs = (jnp.where(r < half, a[0][low], a[1][high]) for a in (own, other))
+        blocks.append(jnp.where(core == parity, mine, theirs))
+    return jnp.concatenate([jnp.concatenate([block[:, k * width:(k + 1) * width] for block in blocks], axis=1) for k in range(2)], axis=0)
+
+
+def assemble_kernel(gather_masks, groups, shards, t0, t1, t2, t3, full):
+    rows, width = t0.shape[1], t0.shape[2] // 2
+    for g in range(groups):
+        for pair in range(shards // 2):
+            at = (slice(2 * g * rows, 2 * (g + 1) * rows), slice(2 * pair * width, 2 * (pair + 1) * width))
+            full[at] = chip_columns(gather_masks, groups, shards, (t0, t1), (t2, t3), g, pair)
+
+
+def assemble(gather_masks, groups, shards, parts, shape):
+    def kernel(*refs):
+        assemble_kernel(gather_masks, groups, shards, *refs)
+
+    return pl.pallas_call(
+        kernel,
+        out_shape=pltpu.VMEM(shape, BF),
+        in_specs=[VM] * 4,
+        out_specs=VM,
+        compiler_params=pltpu.CompilerParams(vmem_limit_bytes=8 * MIB),
+        name="assemble",
+    )(*parts)
+
+
 def forward_kernel(gather_masks, scatter_masks, groups, shards, experts, early,
-                   t0, t1, t2, t3, c0, c1, c2, c3, routes, *refs):
+                   full, c0, c1, c2, c3, routes, *refs):
     loaded, sources = refs[:early], refs[early:early + 3]
-    full, grads, keep, send, qt, gt, *stores, sems = refs[-10:]
-    half, rows, width = t0.shape[0], t0.shape[1], t0.shape[2] // 2
-    tokens = 2 * groups * rows
+    grads, keep, send, qt, gt, *stores, sems = refs[-9:]
+    rows, width = c0.shape[1], c0.shape[2] // 2
     hidden = grads.shape[2] // 2
     group, shard = lax.axis_index("group"), lax.axis_index("shard")
     core, me = shard & 1, group * shards + shard
-    gather_at = [relative(me, masks, False) for masks in gather_masks]
     scatter_at = [relative(me, masks, True) for masks in scatter_masks]
 
     order = [(i, e) for e in range(experts) for i in range(3)]
@@ -109,22 +143,8 @@
 
     release(4 if early else 3)
 
-    def columns(own, other, g, pair):
-        at = g * shards + pair * 2
-        blocks = []
-        for parity in range(2):
-            r = relative(at, gather_masks[parity], False) ^ gather_at[parity]
-            low, high = jnp.minimum(r, half - 1), jnp.maximum(r - half, 0)
-            mine, theirs = (jnp.where(r < half, a[0][low], a[1][high]) for a in (own, other))
-            blocks.append(jnp.where(core == parity, mine, theirs))
-        return jnp.concatenate([jnp.concatenate([block[:, k * width:(k + 1) * width] for block in blocks], axis=1) for k in range(2)], axis=0)
-
-    for g in range(groups):
-        for pair in range(shards // 2):
-            at = (slice(2 * g * rows, 2 * (g + 1) * rows), slice(2 * pair * width, 2 * (pair + 1) * width))
-            full[at] = columns((t0, t1), (t2, t3), g, pair)
     for pair in range(shards // 2):
-        block = jnp.concatenate([columns((c0, c1), (c2, c3), g, pair) for g in range(groups)], axis=0)
+        block = jnp.concatenate([chip_columns(gather_masks, groups, shards, (c0, c1), (c2, c3), g, pair) for g in range(groups)], axis=0)
         qt[2 * pair * width:2 * (pair + 1) * width, :] = block.T
 
     tables = [routes[g ^ group].T for g in range(groups)]
@@ -235,7 +255,7 @@
         in_specs=[VM] * 3 + [anywhere] * len(so_far),
         out_specs=(anywhere, anywhere, VM) + (() if transposed else (VM,)),
         input_output_aliases={3: 0, 4: 1} if transposed else {},
-        scratch_shapes=[pltpu.VMEM((2, len(units), features // blocks, hidden), BF), pltpu.SemaphoreType.DMA((2, len(units)))],
+        scratch_shapes=[pltpu.VMEM((2, max(1, len(units)), features // blocks, hidden), BF), pltpu.SemaphoreType.DMA((2, max(1, len(units))))],
         compiler_params=pltpu.CompilerParams(vmem_limit_bytes=16 * MIB),
         cost_estimate=pl.CostEstimate(flops=4 * features * grads.shape[1] * hidden, bytes_accessed=4 * features * hidden, transcendentals=0),
         name="weight_grads",
@@ -265,7 +285,7 @@
     routes = exchange(routes)
     weights = (w_gate, w_up, w_down)
     order = [(i, e) for e in range(experts) for i in range(3)]
-    parts = (order[:2], order[2:6], order[6:9]) if experts > 3 else ((), (), ())
+    parts = (order[:2], order[2:6], order[6:10]) if experts > 3 else ((), (), ())
     early = sum(len(part) for part in parts)
     loaded, fences = [], []
     for step in range(count - 1):
@@ -297,21 +317,22 @@
         forward_kernel(gather_masks, scatter_masks, groups, shards, experts, early, *refs)
 
     loaded = [pltpu.with_memory_space_constraint(a, pltpu.VMEM) for a in loaded]
-    full, grads, keep, send = pl.pallas_call(
+    full = assemble(gather_masks, groups, shards, gathered[:4], (total_rows, features))
+    grads, keep, send = pl.pallas_call(
         forward,
-        out_shape=(pltpu.VMEM((total_rows, features), BF), pltpu.VMEM((experts, total_rows, 2 * hidden), BF),
+        out_shape=(pltpu.VMEM((experts, total_rows, 2 * hidden), BF),
                    pltpu.VMEM(piece, F32), pltpu.VMEM(piece, BF)),
-        in_specs=[VM] * (9 + len(loaded)) + [pl.BlockSpec(memory_space=pl.ANY)] * (3 + len(fences)),
-        out_specs=(VM,) * 4,
+        in_specs=[VM] * (6 + len(loaded)) + [pl.BlockSpec(memory_space=pl.ANY)] * (3 + len(fences)),
+        out_specs=(VM,) * 3,
         scratch_shapes=[pltpu.VMEM((features, total_rows), BF), pltpu.VMEM((experts, 2 * hidden, total_rows), BF)]
         + [pltpu.VMEM((sum(j == i for j, _ in order[early:]),) + w.shape[1:], BF) for i, w in enumerate(weights)] + [pltpu.SemaphoreType.DMA((3, experts))],
         compiler_params=pltpu.CompilerParams(vmem_limit_bytes=2 * (3 * experts - early) * features * hidden + 20 * total_rows * features + 4 * MIB),
         cost_estimate=pl.CostEstimate(flops=10 * experts * total_rows * features * hidden, bytes_accessed=6 * experts * features * hidden, transcendentals=0),
         name="forward",
-    )(*gathered, *loaded, *(pltpu.with_memory_space_constraint(w, pltpu.HBM) for w in weights), *fences)
+    )(pltpu.with_memory_space_constraint(full, pltpu.VMEM), *gathered[4:], *loaded, *(pltpu.with_memory_space_constraint(w, pltpu.HBM) for w in weights), *fences)
 
     blocks = 8
-    shares = [3, 10, 8] + [5] * (count - 2)
+    shares = [3, 11, 9, 6] + [3] * (count - 3)
     ends = [experts * blocks * sum(shares[:i + 1]) // sum(shares) for i in range(len(shares))]
     so_far, source, after = (), full, send
     kept = None

time: 70.1 us -> 69.2 us (0.987)
  waiting for transfers between devices: 6.32 us -> 4.72 us
    ppermute x15, waiting for transfers between devices: 6.32 us -> 4.72 us  [swap(): return lax.ppermute(x, BOTH, pairs)]
    pallas_call x3, Pallas kernels: 11.3 us -> 12.2 us  [load(): pl.pallas_call(kernel, out_shape=tuple((pltpu.VMEM(w.shape[1:], BF) for w...]
    pallas_call x1 -> x2, Pallas kernels: 16.6 us -> 16.4 us  [the longest x1 16.1 us: body(): pl.pallas_call(forward, out_shape=(pltpu.VMEM((experts, total_rows, 2 * h...]
  transfers between devices with their start and end apart: 15 -> 15, of which waited for: 8 -> 9; matrix products, arithmetic and copies ran while one was open for 1% -> 1% of each run, Pallas kernels for 36% -> 38%
where the time goes in v4:
time: 69.2 us; the launch traced here: 68.9 us
  Pallas kernels  43.2 us (62%)
  starting transfers between devices  18.2 us (26%)
  waiting for transfers between devices  4.72 us (7%)
  other arithmetic  1.74 us (3%)
  between operations  0.85 us (1%)
    ppermute x15, starting transfers between devices, swap(): return lax.ppermute(x, BOTH, pairs)  18.2 us
    pallas_call x1, Pallas kernels, body(): pl.pallas_call(forward, out_shape=(pltpu.VMEM((experts, total_rows, 2 * h...  16.1 us
    pallas_call x5, Pallas kernels, weight_grads(): pl.pallas_call(kernel, out_shape=(array, array, zero) + (() if transposed...  13 us
    pallas_call x3, Pallas kernels, load(): pl.pallas_call(kernel, out_shape=tuple((pltpu.VMEM(w.shape[1:], BF) for w...  12.2 us
    ppermute x15, waiting for transfers between devices, swap(): return lax.ppermute(x, BOTH, pairs)  4.72 us
  transfers between devices with their start and end apart: 15, of which 9 were waited for; matrix products, arithmetic and copies ran while one was open for 1% of the time, Pallas kernels for 38%

profile of v4, /device:TPU:0, one launch (start us, length us, event | category | flops | bytes accessed | tf_op | source)
XLA Modules:
  0.0 68.9 jit_solution(1036359455421043746)
XLA Ops:
  0.6 0.9 %pack.1.after = bf16[2,1,32,384]{3,2,1,0:T(8,128)(2,1)S(1)} custom-call(bf16[64,192]{1,0:T(8,128)(2,1)} %tokens.1, bf16[64,192]{1,0:T(8,128)(2,1)} %cotangent.1), custom_call_target="tpu_custom_call" | custom-call | tf_op jit(solution)/shard_map/pack/pallas_call | solution.py:201
  1.5 4.1 %collective-permute-start = (bf16[2,1,32,384]{3,2,1,0:T(8,128)(2,1)S(1)}, bf16[2,1,32,384]{3,2,1,0:T(8,128)(2,1)S(1)}, u32[]{:S(2)}, u32[]{:S(2)}) collective-permute-start(bf16[2,1,32,384]{3,2,1,0:T(8,128)(2,1)S(1)} %pack.1.after), channel_id=1, source_target_pairs={{0,8},{1,9},{2,10},{3,11},{4,12},{5,13},{6,14},{7,15},{8,0},{9,1},... | collective-permute-start | bytes 147464 | tf_op jit(solution)/shard_map/ppermute | solution.py:32
  5.6 0.7 %pack_routes.1 = f32[1,8,64]{2,1,0:T(8,128)S(1)} custom-call(s32[2,64]{1,0:T(2,128)} %bitcast.16, f32[2,64]{1,0:T(2,128)} %bitcast.17, bf16[2,1,32,384]{3,2,1,0:T(8,128)(2,1)} %copy-done), custom_call_target="tpu_custom_call" | custom-call | tf_op jit(solution)/shard_map/pack_routes/pallas_call | solution.py:211
  6.3 1.5 %collective-permute-start.2 = (f32[1,8,64]{2,1,0:T(8,128)S(1)}, f32[1,8,64]{2,1,0:T(8,128)S(1)}, u32[]{:S(2)}, u32[]{:S(2)}) collective-permute-start(f32[1,8,64]{2,1,0:T(8,128)S(1)} %pack_routes.1), channel_id=1, source_target_pairs={{0,16},{1,17},{2,18},{3,19},{4,20},{5,21},{6,22},{7,23},{8,24},{9,... | collective-permute-start | bytes 6152 | tf_op jit(solution)/shard_map/ppermute | solution.py:32
  8.2 0.8 %pad_maximum_fusion.2.refs_2_ = bf16[2,2,32,384]{3,2,1,0:T(8,128)(2,1)S(1)} fusion(bf16[2,1,32,384]{3,2,1,0:T(8,128)(2,1)S(1)} %collective-permute-done, bf16[2,1,32,384]{3,2,1,0:T(8,128)(2,1)} %copy-done), kind=kLoop, calls=%fused_computation.13 | loop fusion | flops 49152 | bytes 196608 | tf_op jit(solution)/shard_map/concatenate | solution.py:293
  9.0 1.4 %collective-permute-start.1 = (bf16[2,2,32,384]{3,2,1,0:T(8,128)(2,1)S(1)}, bf16[2,2,32,384]{3,2,1,0:T(8,128)(2,1)S(1)}, u32[]{:S(2)}, u32[]{:S(2)}) collective-permute-start(bf16[2,2,32,384]{3,2,1,0:T(8,128)(2,1)S(1)} %pad_maximum_fusion.2.refs_2_), channel_id=1, source_target_pairs={{0,4},{1,5},{2,6},{3,7},{4,0},{5,1},{6,2},{7,3},{8,12},{9,13},{10,... | collective-permute-start | bytes 294920 | tf_op jit(solution)/shard_map/ppermute | solution.py:32
  10.5 2.9 %load.3 = (bf16[3072,512]{1,0:T(8,128)(2,1)S(1)}, bf16[3072,512]{1,0:T(8,128)(2,1)S(1)}, f32[8,128]{1,0:T(8,128)S(1)}) custom-call(bf16[4,3072,512]{2,1,0:T(8,128)(2,1)} %refs_16_.1, bf16[4,3072,512]{2,1,0:T(8,128)(2,1)} %refs_17_.1, bf16[2,2,32,384]{3,2,1,0:T(8,128)(2,1)S(1)} %pad_maximum_fusion.2.refs_2_), custom_call_target="tpu_custom_call" | custom-call | bytes 6291456 | tf_op jit(solution)/shard_map/load/pallas_call | solution.py:62
  13.7 1.8 %collective-permute-start.3 = (bf16[2,4,32,384]{3,2,1,0:T(8,128)(2,1)S(1)}, bf16[2,4,32,384]{3,2,1,0:T(8,128)(2,1)S(1)}, u32[]{:S(2)}, u32[]{:S(2)}) collective-permute-start(bf16[2,4,32,384]{3,2,1,0:T(8,128)(2,1)S(1)} %pad_maximum_fusion.1.refs_4_), channel_id=1, source_target_pairs={{0,16},{1,3},{2,18},{3,1},{4,20},{5,7},{6,22},{7,5},{8,24},{9,11},... | collective-permute-start | bytes 589832 | tf_op jit(solution)/shard_map/ppermute | solution.py:32
  15.5 4.7 %load.4 = (bf16[512,3072]{1,0:T(8,128)(2,1)S(1)}, bf16[3072,512]{1,0:T(8,128)(2,1)S(1)}, bf16[3072,512]{1,0:T(8,128)(2,1)S(1)}, bf16[512,3072]{1,0:T(8,128)(2,1)S(1)}, f32[8,128]{1,0:T(8,128)S(1)}) custom-call(bf16[4,512,3072]{2,1,0:T(8,128)(2,1)} %refs_18_.1, bf16[4,3072,512]{2,1,0:T(8,128)(2,1)} %refs_16_.1, bf16[4,3072,512]{2,1,0:T(8,128)(2,1)} %refs_17_.1, ...), custom_call_target="tpu_custom_call" | custom-call | bytes 12582912 | tf_op jit(solution)/shard_map/load/pallas_call | solution.py:62
  20.4 1.6 %collective-permute-start.4 = (bf16[8,32,384]{2,1,0:T(8,128)(2,1)S(1)}, bf16[8,32,384]{2,1,0:T(8,128)(2,1)S(1)}, u32[]{:S(2)}, u32[]{:S(2)}) collective-permute-start(bf16[8,32,384]{2,1,0:T(8,128)(2,1)S(1)} %get-tuple-element.84.refs_0_), channel_id=1, source_target_pairs={{0,2},{1,17},{2,0},{3,19},{4,6},{5,21},{6,4},{7,23},{8,10},{9,25},... | collective-permute-start | bytes 589832 | tf_op jit(solution)/shard_map/ppermute | solution.py:32
  22.5 4.7 %load.5 = (bf16[3072,512]{1,0:T(8,128)(2,1)S(1)}, bf16[3072,512]{1,0:T(8,128)(2,1)S(1)}, bf16[512,3072]{1,0:T(8,128)(2,1)S(1)}, bf16[3072,512]{1,0:T(8,128)(2,1)S(1)}, f32[8,128]{1,0:T(8,128)S(1)}) custom-call(bf16[4,3072,512]{2,1,0:T(8,128)(2,1)} %refs_16_.1, bf16[4,3072,512]{2,1,0:T(8,128)(2,1)} %refs_17_.1, bf16[4,512,3072]{2,1,0:T(8,128)(2,1)} %refs_18_.1, ...), custom_call_target="tpu_custom_call" | custom-call | bytes 12582912 | tf_op jit(solution)/shard_map/load/pallas_call | solution.py:62
  29.7 16.1 %forward.1 = (bf16[4,128,1024]{2,1,0:T(8,128)(2,1)S(1)}, f32[16,32,384]{2,1,0:T(8,128)S(1)}, bf16[16,32,384]{2,1,0:T(8,128)(2,1)S(1)}) custom-call(bf16[128,3072]{1,0:T(8,128)(2,1)S(1)} %assemble.1.refs_0_, bf16[8,32,384]{2,1,0:T(8,128)(2,1)S(1)} %get-tuple-element.83.refs_1_, bf16[8,32,384]{2,1,0:T(8,128)(2,1)S(1)} %collective-permute-done.8.refs_2_, ...), custom_call_target="tpu_custom_call" | custom-call | flops 8053063680 | bytes 37748736 | tf_op jit(solution)/shard_map/forward/pallas_call | solution.py:321
  46.0 1.8 %weight_grads.5 = (bf16[4,3072,512]{2,1,0:T(8,128)(2,1)}, bf16[4,3072,512]{2,1,0:T(8,128)(2,1)}, f32[1,32,384]{2,1,0:T(8,128)S(1)}, bf16[3072,128]{1,0:T(8,128)(2,1)S(1)}) custom-call(bf16[128,3072]{1,0:T(8,128)(2,1)S(1)} %assemble.1.refs_0_, bf16[4,128,1024]{2,1,0:T(8,128)(2,1)S(1)} %get-tuple-element.66.refs_1_, ...), custom_call_target="tpu_custom_call" | custom-call | flops 805306368 | bytes 6291456 | tf_op jit(solution)/shard_map/weight_grads/pallas_call | solution.py:252
  47.9 1.6 %collective-permute-start.11 = (bf16[8,32,384]{2,1,0:T(8,128)(2,1)S(1)}, bf16[8,32,384]{2,1,0:T(8,128)(2,1)S(1)}, u32[]{:S(2)}, u32[]{:S(2)}) collective-permute-start(bf16[8,32,384]{2,1,0:T(8,128)(2,1)S(1)} %slice.80), channel_id=1, source_target_pairs={{0,2},{1,17},{2,0},{3,19},{4,6},{5,21},{6,4},{7,23},{8,10},{9,25},... | collective-permute-start | bytes 589832 | tf_op jit(solution)/shard_map/ppermute | solution.py:32
  49.5 3.8 %weight_grads.6 = (bf16[4,3072,512]{2,1,0:T(8,128)(2,1)}, bf16[4,3072,512]{2,1,0:T(8,128)(2,1)}, f32[1,32,384]{2,1,0:T(8,128)S(1)}) custom-call(bf16[3072,128]{1,0:T(8,128)(2,1)S(1)} %get-tuple-element.68.refs_0_, bf16[4,128,1024]{2,1,0:T(8,128)(2,1)S(1)} %get-tuple-element.66.refs_1_, ...), custom_call_target="tpu_custom_call", output_to_operand_aliasing={{0}: (3, {}), {1}: (4, {})} | custom-call | flops 805306368 | bytes 6291456 | tf_op jit(solution)/shard_map/weight_grads/pallas_call | solution.py:252
  53.7 1.0 %collective-permute-start.12 = (bf16[4,32,384]{2,1,0:T(8,128)(2,1)S(1)}, bf16[4,32,384]{2,1,0:T(8,128)(2,1)S(1)}, u32[]{:S(2)}, u32[]{:S(2)}) collective-permute-start(bf16[4,32,384]{2,1,0:T(8,128)(2,1)S(1)} %slice.81), channel_id=1, source_target_pairs={{0,16},{1,3},{2,18},{3,1},{4,20},{5,7},{6,22},{7,5},{8,24},{9,11},... | collective-permute-start | bytes 294920 | tf_op jit(solution)/shard_map/ppermute | solution.py:32
  54.8 3.3 %weight_grads.7 = (bf16[4,3072,512]{2,1,0:T(8,128)(2,1)}, bf16[4,3072,512]{2,1,0:T(8,128)(2,1)}, f32[1,32,384]{2,1,0:T(8,128)S(1)}) custom-call(bf16[3072,128]{1,0:T(8,128)(2,1)S(1)} %get-tuple-element.68.refs_0_, bf16[4,128,1024]{2,1,0:T(8,128)(2,1)S(1)} %get-tuple-element.66.refs_1_, ...), custom_call_target="tpu_custom_call", output_to_operand_aliasing={{0}: (3, {}), {1}: (4, {})} | custom-call | flops 805306368 | bytes 6291456 | tf_op jit(solution)/shard_map/weight_grads/pallas_call | solution.py:252
  58.4 1.2 %collective-permute-start.13 = (f32[2,32,384]{2,1,0:T(8,128)S(1)}, f32[2,32,384]{2,1,0:T(8,128)S(1)}, u32[]{:S(2)}, u32[]{:S(2)}) collective-permute-start(f32[2,32,384]{2,1,0:T(8,128)S(1)} %slice.55), channel_id=1, source_target_pairs={{0,4},{1,5},{2,6},{3,7},{4,0},{5,1},{6,2},{7,3},{8,12},{9,13},{10,... | collective-permute-start | bytes 294920 | tf_op jit(solution)/shard_map/ppermute | solution.py:32
  59.7 2.5 %weight_grads.8 = (bf16[4,3072,512]{2,1,0:T(8,128)(2,1)}, bf16[4,3072,512]{2,1,0:T(8,128)(2,1)}, f32[1,32,384]{2,1,0:T(8,128)S(1)}) custom-call(bf16[3072,128]{1,0:T(8,128)(2,1)S(1)} %get-tuple-element.68.refs_0_, bf16[4,128,1024]{2,1,0:T(8,128)(2,1)S(1)} %get-tuple-element.66.refs_1_, ...), custom_call_target="tpu_custom_call", output_to_operand_aliasing={{0}: (3, {}), {1}: (4, {})} | custom-call | flops 805306368 | bytes 6291456 | tf_op jit(solution)/shard_map/weight_grads/pallas_call | solution.py:252
  62.2 0.9 %collective-permute-done.13 = f32[2,32,384]{2,1,0:T(8,128)S(1)} collective-permute-done((f32[2,32,384]{2,1,0:T(8,128)S(1)}, f32[2,32,384]{2,1,0:T(8,128)S(1)}, u32[]{:S(2)}, u32[]{:S(2)}) %collective-permute-start.13) | collective-permute-done | bytes 98336 | tf_op jit(solution)/shard_map/ppermute | solution.py:32
  63.2 2.6 %collective-permute-start.14 = (f32[1,32,384]{2,1,0:T(8,128)S(1)}, f32[1,32,384]{2,1,0:T(8,128)S(1)}, u32[]{:S(2)}, u32[]{:S(2)}) collective-permute-start(f32[1,32,384]{2,1,0:T(8,128)S(1)} %slice.57), channel_id=1, source_target_pairs={{0,8},{1,9},{2,10},{3,11},{4,12},{5,13},{6,14},{7,15},{8,0},{9,1},... | collective-permute-start | bytes 147464 | tf_op jit(solution)/shard_map/ppermute | solution.py:32
  65.7 1.7 %weight_grads.9 = (bf16[4,3072,512]{2,1,0:T(8,128)(2,1)}, bf16[4,3072,512]{2,1,0:T(8,128)(2,1)}, f32[1,32,384]{2,1,0:T(8,128)S(1)}) custom-call(bf16[3072,128]{1,0:T(8,128)(2,1)S(1)} %get-tuple-element.68.refs_0_, bf16[4,128,1024]{2,1,0:T(8,128)(2,1)S(1)} %get-tuple-element.66.refs_1_, ...), custom_call_target="tpu_custom_call", output_to_operand_aliasing={{0}: (3, {}), {1}: (4, {})} | custom-call | flops 805306368 | bytes 6291456 | tf_op jit(solution)/shard_map/weight_grads/pallas_call | solution.py:252
  67.4 0.8 %collective-permute-done.14 = f32[1,32,384]{2,1,0:T(8,128)S(1)} collective-permute-done((f32[1,32,384]{2,1,0:T(8,128)S(1)}, f32[1,32,384]{2,1,0:T(8,128)S(1)}, u32[]{:S(2)}, u32[]{:S(2)}) %collective-permute-start.14) | collective-permute-done | bytes 49184 | tf_op jit(solution)/shard_map/ppermute | solution.py:32
  68.3 0.6 pad_maximum_fusion.3
  (38 shorter events, 5.2 us)
Async XLA Ops:
  1.5 4.1 %copy-start = (bf16[2,1,32,384]{3,2,1,0:T(8,128)(2,1)}, bf16[2,1,32,384]{3,2,1,0:T(8,128)(2,1)S(1)}, u32[]{:S(2)}) copy-start(bf16[2,1,32,384]{3,2,1,0:T(8,128)(2,1)S(1)} %pack.1.after) | copy-start | bytes 147460
  1.5 6.7 %collective-permute-start = (bf16[2,1,32,384]{3,2,1,0:T(8,128)(2,1)S(1)}, bf16[2,1,32,384]{3,2,1,0:T(8,128)(2,1)S(1)}, u32[]{:S(2)}, u32[]{:S(2)}) collective-permute-start(bf16[2,1,32,384]{3,2,1,0:T(8,128)(2,1)S(1)} %pack.1.after), channel_id=1, source_target_pairs={{0,8},{1,9},{2,10},{3,11},{4,12},{5,13},{6,14},{7,15},{8,0},{9,1},... | collective-permute-start | bytes 147464 | tf_op jit(solution)/shard_map/ppermute | solution.py:32
  6.3 4.2 %collective-permute-start.2 = (f32[1,8,64]{2,1,0:T(8,128)S(1)}, f32[1,8,64]{2,1,0:T(8,128)S(1)}, u32[]{:S(2)}, u32[]{:S(2)}) collective-permute-start(f32[1,8,64]{2,1,0:T(8,128)S(1)} %pack_routes.1), channel_id=1, source_target_pairs={{0,16},{1,17},{2,18},{3,19},{4,20},{5,21},{6,22},{7,23},{8,24},{9,... | collective-permute-start | bytes 6152 | tf_op jit(solution)/shard_map/ppermute | solution.py:32
  9.0 4.7 %collective-permute-start.1 = (bf16[2,2,32,384]{3,2,1,0:T(8,128)(2,1)S(1)}, bf16[2,2,32,384]{3,2,1,0:T(8,128)(2,1)S(1)}, u32[]{:S(2)}, u32[]{:S(2)}) collective-permute-start(bf16[2,2,32,384]{3,2,1,0:T(8,128)(2,1)S(1)} %pad_maximum_fusion.2.refs_2_), channel_id=1, source_target_pairs={{0,4},{1,5},{2,6},{3,7},{4,0},{5,1},{6,2},{7,3},{8,12},{9,13},{10,... | collective-permute-start | bytes 294920 | tf_op jit(solution)/shard_map/ppermute | solution.py:32
  10.5 3.2 %copy-start.1 = (bf16[2,1,32,384]{3,2,1,0:T(8,128)(2,1)S(1)}, bf16[2,1,32,384]{3,2,1,0:T(8,128)(2,1)}, u32[]{:S(2)}) copy-start(bf16[2,1,32,384]{3,2,1,0:T(8,128)(2,1)} %copy-done) | copy-start | bytes 147460
  13.7 6.5 %collective-permute-start.3 = (bf16[2,4,32,384]{3,2,1,0:T(8,128)(2,1)S(1)}, bf16[2,4,32,384]{3,2,1,0:T(8,128)(2,1)S(1)}, u32[]{:S(2)}, u32[]{:S(2)}) collective-permute-start(bf16[2,4,32,384]{3,2,1,0:T(8,128)(2,1)S(1)} %pad_maximum_fusion.1.refs_4_), channel_id=1, source_target_pairs={{0,16},{1,3},{2,18},{3,1},{4,20},{5,7},{6,22},{7,5},{8,24},{9,11},... | collective-permute-start | bytes 589832 | tf_op jit(solution)/shard_map/ppermute | solution.py:32
  20.3 2.2 %collective-permute-start.5 = (bf16[8,32,384]{2,1,0:T(8,128)(2,1)S(1)}, bf16[8,32,384]{2,1,0:T(8,128)(2,1)S(1)}, u32[]{:S(2)}, u32[]{:S(2)}) collective-permute-start(bf16[8,32,384]{2,1,0:T(8,128)(2,1)S(1)} %get-tuple-element.83.refs_1_), channel_id=1, source_target_pairs={{0,1},{1,0},{2,3},{3,2},{4,5},{5,4},{6,7},{7,6},{8,9},{9,8},{10,11... | collective-permute-start | bytes 589832 | tf_op jit(solution)/shard_map/ppermute | solution.py:32
  20.4 6.8 %collective-permute-start.4 = (bf16[8,32,384]{2,1,0:T(8,128)(2,1)S(1)}, bf16[8,32,384]{2,1,0:T(8,128)(2,1)S(1)}, u32[]{:S(2)}, u32[]{:S(2)}) collective-permute-start(bf16[8,32,384]{2,1,0:T(8,128)(2,1)S(1)} %get-tuple-element.84.refs_0_), channel_id=1, source_target_pairs={{0,2},{1,17},{2,0},{3,19},{4,6},{5,21},{6,4},{7,23},{8,10},{9,25},... | collective-permute-start | bytes 589832 | tf_op jit(solution)/shard_map/ppermute | solution.py:32
  22.0 6.3 %collective-permute-start.8 = (bf16[8,32,384]{2,1,0:T(8,128)(2,1)S(1)}, bf16[8,32,384]{2,1,0:T(8,128)(2,1)S(1)}, u32[]{:S(2)}, u32[]{:S(2)}) collective-permute-start(bf16[8,32,384]{2,1,0:T(8,128)(2,1)S(1)} %get-tuple-element.83.refs_1_), channel_id=1, source_target_pairs={{0,2},{1,17},{2,0},{3,19},{4,6},{5,21},{6,4},{7,23},{8,10},{9,25},... | collective-permute-start | bytes 589832 | tf_op jit(solution)/shard_map/ppermute | solution.py:32
  22.5 5.8 %collective-permute-start.6 = (bf16[8,32,384]{2,1,0:T(8,128)(2,1)S(1)}, bf16[8,32,384]{2,1,0:T(8,128)(2,1)S(1)}, u32[]{:S(2)}, u32[]{:S(2)}) collective-permute-start(bf16[8,32,384]{2,1,0:T(8,128)(2,1)S(1)} %get-tuple-element.84.refs_0_), channel_id=1, source_target_pairs={{0,1},{1,0},{2,3},{3,2},{4,5},{5,4},{6,7},{7,6},{8,9},{9,8},{10,11... | collective-permute-start | bytes 589832 | tf_op jit(solution)/shard_map/ppermute | solution.py:32
  27.2 1.6 %collective-permute-start.7 = (bf16[8,32,384]{2,1,0:T(8,128)(2,1)S(1)}, bf16[8,32,384]{2,1,0:T(8,128)(2,1)S(1)}, u32[]{:S(2)}, u32[]{:S(2)}) collective-permute-start(bf16[8,32,384]{2,1,0:T(8,128)(2,1)S(1)} %collective-permute-done.4.refs_1_), channel_id=1, source_target_pairs={{0,1},{1,0},{2,3},{3,2},{4,5},{5,4},{6,7},{7,6},{8,9},{9,8},{10,11... | collective-permute-start | bytes 589832 | tf_op jit(solution)/shard_map/ppermute | solution.py:32
  28.2 1.4 %collective-permute-start.9 = (bf16[8,32,384]{2,1,0:T(8,128)(2,1)S(1)}, bf16[8,32,384]{2,1,0:T(8,128)(2,1)S(1)}, u32[]{:S(2)}, u32[]{:S(2)}) collective-permute-start(bf16[8,32,384]{2,1,0:T(8,128)(2,1)S(1)} %collective-permute-done.8.refs_2_), channel_id=1, source_target_pairs={{0,1},{1,0},{2,3},{3,2},{4,5},{5,4},{6,7},{7,6},{8,9},{9,8},{10,11... | collective-permute-start | bytes 589832 | tf_op jit(solution)/shard_map/ppermute | solution.py:32
  45.8 2.0 %collective-permute-start.10 = (bf16[16,32,384]{2,1,0:T(8,128)(2,1)S(1)}, bf16[16,32,384]{2,1,0:T(8,128)(2,1)S(1)}, u32[]{:S(2)}, u32[]{:S(2)}) collective-permute-start(bf16[16,32,384]{2,1,0:T(8,128)(2,1)S(1)} %get-tuple-element.65.refs_2_), channel_id=1, source_target_pairs={{0,1},{1,0},{2,3},{3,2},{4,5},{5,4},{6,7},{7,6},{8,9},{9,8},{10,11... | collective-permute-start | bytes 1179656 | tf_op jit(solution)/shard_map/ppermute | solution.py:32
  47.9 5.7 %collective-permute-start.11 = (bf16[8,32,384]{2,1,0:T(8,128)(2,1)S(1)}, bf16[8,32,384]{2,1,0:T(8,128)(2,1)S(1)}, u32[]{:S(2)}, u32[]{:S(2)}) collective-permute-start(bf16[8,32,384]{2,1,0:T(8,128)(2,1)S(1)} %slice.80), channel_id=1, source_target_pairs={{0,2},{1,17},{2,0},{3,19},{4,6},{5,21},{6,4},{7,23},{8,10},{9,25},... | collective-permute-start | bytes 589832 | tf_op jit(solution)/shard_map/ppermute | solution.py:32
  53.7 4.7 %collective-permute-start.12 = (bf16[4,32,384]{2,1,0:T(8,128)(2,1)S(1)}, bf16[4,32,384]{2,1,0:T(8,128)(2,1)S(1)}, u32[]{:S(2)}, u32[]{:S(2)}) collective-permute-start(bf16[4,32,384]{2,1,0:T(8,128)(2,1)S(1)} %slice.81), channel_id=1, source_target_pairs={{0,16},{1,3},{2,18},{3,1},{4,20},{5,7},{6,22},{7,5},{8,24},{9,11},... | collective-permute-start | bytes 294920 | tf_op jit(solution)/shard_map/ppermute | solution.py:32
  58.4 4.7 %collective-permute-start.13 = (f32[2,32,384]{2,1,0:T(8,128)S(1)}, f32[2,32,384]{2,1,0:T(8,128)S(1)}, u32[]{:S(2)}, u32[]{:S(2)}) collective-permute-start(f32[2,32,384]{2,1,0:T(8,128)S(1)} %slice.55), channel_id=1, source_target_pairs={{0,4},{1,5},{2,6},{3,7},{4,0},{5,1},{6,2},{7,3},{8,12},{9,13},{10,... | collective-permute-start | bytes 294920 | tf_op jit(solution)/shard_map/ppermute | solution.py:32
  63.2 5.1 %collective-permute-start.14 = (f32[1,32,384]{2,1,0:T(8,128)S(1)}, f32[1,32,384]{2,1,0:T(8,128)S(1)}, u32[]{:S(2)}, u32[]{:S(2)}) collective-permute-start(f32[1,32,384]{2,1,0:T(8,128)S(1)} %slice.57), channel_id=1, source_target_pairs={{0,8},{1,9},{2,10},{3,11},{4,12},{5,13},{6,14},{7,15},{8,0},{9,1},... | collective-permute-start | bytes 147464 | tf_op jit(solution)/shard_map/ppermute | solution.py:32

commit v5 on v4

--- a/solution.py
+++ b/solution.py
@@ -86,12 +86,13 @@
     return jnp.concatenate([jnp.concatenate([block[:, k * width:(k + 1) * width] for block in blocks], axis=1) for k in range(2)], axis=0)
 
 
-def assemble_kernel(gather_masks, groups, shards, t0, t1, t2, t3, full):
+def assemble_kernel(gather_masks, groups, shards, t0, t1, t2, t3, full, xt):
     rows, width = t0.shape[1], t0.shape[2] // 2
     for g in range(groups):
         for pair in range(shards // 2):
             at = (slice(2 * g * rows, 2 * (g + 1) * rows), slice(2 * pair * width, 2 * (pair + 1) * width))
             full[at] = chip_columns(gather_masks, groups, shards, (t0, t1), (t2, t3), g, pair)
+    xt[...] = full[...].T
 
 
 def assemble(gather_masks, groups, shards, parts, shape):
@@ -100,9 +101,9 @@
 
     return pl.pallas_call(
         kernel,
-        out_shape=pltpu.VMEM(shape, BF),
+        out_shape=(pltpu.VMEM(shape, BF), pltpu.VMEM(shape[::-1], BF)),
         in_specs=[VM] * 4,
-        out_specs=VM,
+        out_specs=(VM, VM),
         compiler_params=pltpu.CompilerParams(vmem_limit_bytes=8 * MIB),
         name="assemble",
     )(*parts)
@@ -217,14 +218,8 @@
     )(ids.T, weights.T, after)
 
 
-def weight_kernel(units, blocks, transposed, *refs):
-    rows, grads = refs[0], refs[1]
-    if transposed:
-        out_gate, out_up, token, made, sems = refs[-5:]
-        xt = rows
-    else:
-        out_gate, out_up, token, xt, made, sems = refs[-6:]
-        xt[...] = rows[...].T
+def weight_kernel(units, blocks, xt, grads, *refs):
+    out_gate, out_up, token, made, sems = refs[-5:]
     features, hidden = xt.shape[0], out_gate.shape[2]
     block = features // blocks
     copies = []
@@ -242,19 +237,18 @@
 
 def weight_grads(rows, grads, after, so_far, units, blocks, shape, piece):
     experts, features, hidden = shape
-    transposed = bool(so_far)
     array, zero = jax.ShapeDtypeStruct(shape, BF), pltpu.VMEM((1,) + piece[1:], F32)
     anywhere = pl.BlockSpec(memory_space=pl.ANY)
 
     def kernel(*refs):
-        weight_kernel(units, blocks, transposed, *refs)
+        weight_kernel(units, blocks, *refs)
 
     return pl.pallas_call(
         kernel,
-        out_shape=(array, array, zero) + (() if transposed else (pltpu.VMEM((features, rows.shape[0]), BF),)),
+        out_shape=(array, array, zero),
         in_specs=[VM] * 3 + [anywhere] * len(so_far),
-        out_specs=(anywhere, anywhere, VM) + (() if transposed else (VM,)),
-        input_output_aliases={3: 0, 4: 1} if transposed else {},
+        out_specs=(anywhere, anywhere, VM),
+        input_output_aliases={3: 0, 4: 1} if so_far else {},
         scratch_shapes=[pltpu.VMEM((2, max(1, len(units)), features // blocks, hidden), BF), pltpu.SemaphoreType.DMA((2, max(1, len(units))))],
         compiler_params=pltpu.CompilerParams(vmem_limit_bytes=16 * MIB),
         cost_estimate=pl.CostEstimate(flops=4 * features * grads.shape[1] * hidden, bytes_accessed=4 * features * hidden, transcendentals=0),
@@ -317,7 +311,7 @@
         forward_kernel(gather_masks, scatter_masks, groups, shards, experts, early, *refs)
 
     loaded = [pltpu.with_memory_space_constraint(a, pltpu.VMEM) for a in loaded]
-    full = assemble(gather_masks, groups, shards, gathered[:4], (total_rows, features))
+    full, xt = assemble(gather_masks, groups, shards, gathered[:4], (total_rows, features))
     grads, keep, send = pl.pallas_call(
         forward,
         out_shape=(pltpu.VMEM((experts, total_rows, 2 * hidden), BF),
@@ -334,18 +328,18 @@
     blocks = 8
     shares = [3, 11, 9, 6] + [3] * (count - 3)
     ends = [experts * blocks * sum(shares[:i + 1]) // sum(shares) for i in range(len(shares))]
-    so_far, source, after = (), full, send
+    so_far, after = (), send
     kept = None
     for step in range(count + 1):
         units = list(range(ends[step - 1] if step else 0, ends[step]))
-        grad_gate, grad_up, token, *made = weight_grads(source, grads, after, so_far, units, blocks, w_gate.shape, piece)
-        so_far, source = (grad_gate, grad_up), made[0] if made else source
+        grad_gate, grad_up, token = weight_grads(xt, grads, after, so_far, units, blocks, w_gate.shape, piece)
+        so_far = (grad_gate, grad_up)
         if step == 0:
             kept = keep + swap(send, groups, shards, (1, 1)).astype(F32) + token
         else:
             half = kept.shape[0] // 2
             sent = kept[half:]
-            if 2 * (step - 1) < count:
+            if step < count:
                 sent = sent.astype(BF)
             kept = kept[:half] + swap(sent, groups, shards, step_masks(scatter_masks, step - 1)).astype(F32) + token
         after = kept

time: 69.2 us -> 68.5 us (0.990)
  waiting for transfers between devices: 4.72 us -> 3.79 us
    ppermute x15, waiting for transfers between devices: 4.72 us -> 3.79 us  [swap(): return lax.ppermute(x, BOTH, pairs)]
  transfers between devices with their start and end apart: 15 -> 15, of which waited for: 9 -> 9; matrix products, arithmetic and copies ran while one was open for 1% -> 1% of each run, Pallas kernels for 38% -> 39%
where the time goes in v5:
time: 68.5 us; the launch traced here: 68.2 us
  Pallas kernels  43.3 us (63%)
  starting transfers between devices  18.4 us (27%)
  waiting for transfers between devices  3.79 us (6%)
  other arithmetic  1.72 us (3%)
  between operations  0.85 us (1%)
    ppermute x15, starting transfers between devices, swap(): return lax.ppermute(x, BOTH, pairs)  18.4 us
    pallas_call x1, Pallas kernels, body(): pl.pallas_call(forward, out_shape=(pltpu.VMEM((experts, total_rows, 2 * h...  16 us
    pallas_call x5, Pallas kernels, weight_grads(): pl.pallas_call(kernel, out_shape=(array, array, zero), in_specs=[VM] * 3...  13 us
    pallas_call x3, Pallas kernels, load(): pl.pallas_call(kernel, out_shape=tuple((pltpu.VMEM(w.shape[1:], BF) for w...  12.2 us
    ppermute x15, waiting for transfers between devices, swap(): return lax.ppermute(x, BOTH, pairs)  3.79 us
  transfers between devices with their start and end apart: 15, of which 9 were waited for; matrix products, arithmetic and copies ran while one was open for 1% of the time, Pallas kernels for 39%

profile of v5, /device:TPU:0, one launch (start us, length us, event | category | flops | bytes accessed | tf_op | source)
XLA Modules:
  0.0 68.2 jit_solution(3799823015007725304)
XLA Ops:
  0.6 0.9 %pack.1.after = bf16[2,1,32,384]{3,2,1,0:T(8,128)(2,1)S(1)} custom-call(bf16[64,192]{1,0:T(8,128)(2,1)} %tokens.1, bf16[64,192]{1,0:T(8,128)(2,1)} %cotangent.1), custom_call_target="tpu_custom_call" | custom-call | tf_op jit(solution)/shard_map/pack/pallas_call | solution.py:202
  1.5 4.1 %collective-permute-start = (bf16[2,1,32,384]{3,2,1,0:T(8,128)(2,1)S(1)}, bf16[2,1,32,384]{3,2,1,0:T(8,128)(2,1)S(1)}, u32[]{:S(2)}, u32[]{:S(2)}) collective-permute-start(bf16[2,1,32,384]{3,2,1,0:T(8,128)(2,1)S(1)} %pack.1.after), channel_id=1, source_target_pairs={{0,8},{1,9},{2,10},{3,11},{4,12},{5,13},{6,14},{7,15},{8,0},{9,1},... | collective-permute-start | bytes 147464 | tf_op jit(solution)/shard_map/ppermute | solution.py:32
  5.6 0.7 %pack_routes.1 = f32[1,8,64]{2,1,0:T(8,128)S(1)} custom-call(s32[2,64]{1,0:T(2,128)} %bitcast.16, f32[2,64]{1,0:T(2,128)} %bitcast.17, bf16[2,1,32,384]{3,2,1,0:T(8,128)(2,1)} %copy-done), custom_call_target="tpu_custom_call" | custom-call | tf_op jit(solution)/shard_map/pack_routes/pallas_call | solution.py:212
  6.3 1.5 %collective-permute-start.2 = (f32[1,8,64]{2,1,0:T(8,128)S(1)}, f32[1,8,64]{2,1,0:T(8,128)S(1)}, u32[]{:S(2)}, u32[]{:S(2)}) collective-permute-start(f32[1,8,64]{2,1,0:T(8,128)S(1)} %pack_routes.1), channel_id=1, source_target_pairs={{0,16},{1,17},{2,18},{3,19},{4,20},{5,21},{6,22},{7,23},{8,24},{9,... | collective-permute-start | bytes 6152 | tf_op jit(solution)/shard_map/ppermute | solution.py:32
  8.2 0.8 %pad_maximum_fusion.2.refs_2_ = bf16[2,2,32,384]{3,2,1,0:T(8,128)(2,1)S(1)} fusion(bf16[2,1,32,384]{3,2,1,0:T(8,128)(2,1)S(1)} %collective-permute-done, bf16[2,1,32,384]{3,2,1,0:T(8,128)(2,1)} %copy-done), kind=kLoop, calls=%fused_computation.14 | loop fusion | flops 49152 | bytes 196608 | tf_op jit(solution)/shard_map/concatenate | solution.py:287
  9.0 1.4 %collective-permute-start.1 = (bf16[2,2,32,384]{3,2,1,0:T(8,128)(2,1)S(1)}, bf16[2,2,32,384]{3,2,1,0:T(8,128)(2,1)S(1)}, u32[]{:S(2)}, u32[]{:S(2)}) collective-permute-start(bf16[2,2,32,384]{3,2,1,0:T(8,128)(2,1)S(1)} %pad_maximum_fusion.2.refs_2_), channel_id=1, source_target_pairs={{0,4},{1,5},{2,6},{3,7},{4,0},{5,1},{6,2},{7,3},{8,12},{9,13},{10,... | collective-permute-start | bytes 294920 | tf_op jit(solution)/shard_map/ppermute | solution.py:32
  10.5 2.9 %load.3 = (bf16[3072,512]{1,0:T(8,128)(2,1)S(1)}, bf16[3072,512]{1,0:T(8,128)(2,1)S(1)}, f32[8,128]{1,0:T(8,128)S(1)}) custom-call(bf16[4,3072,512]{2,1,0:T(8,128)(2,1)} %refs_16_.1, bf16[4,3072,512]{2,1,0:T(8,128)(2,1)} %refs_17_.1, bf16[2,2,32,384]{3,2,1,0:T(8,128)(2,1)S(1)} %pad_maximum_fusion.2.refs_2_), custom_call_target="tpu_custom_call" | custom-call | bytes 6291456 | tf_op jit(solution)/shard_map/load/pallas_call | solution.py:62
  13.7 1.8 %collective-permute-start.3 = (bf16[2,4,32,384]{3,2,1,0:T(8,128)(2,1)S(1)}, bf16[2,4,32,384]{3,2,1,0:T(8,128)(2,1)S(1)}, u32[]{:S(2)}, u32[]{:S(2)}) collective-permute-start(bf16[2,4,32,384]{3,2,1,0:T(8,128)(2,1)S(1)} %pad_maximum_fusion.1.refs_4_), channel_id=1, source_target_pairs={{0,16},{1,3},{2,18},{3,1},{4,20},{5,7},{6,22},{7,5},{8,24},{9,11},... | collective-permute-start | bytes 589832 | tf_op jit(solution)/shard_map/ppermute | solution.py:32
  15.5 4.7 %load.4 = (bf16[512,3072]{1,0:T(8,128)(2,1)S(1)}, bf16[3072,512]{1,0:T(8,128)(2,1)S(1)}, bf16[3072,512]{1,0:T(8,128)(2,1)S(1)}, bf16[512,3072]{1,0:T(8,128)(2,1)S(1)}, f32[8,128]{1,0:T(8,128)S(1)}) custom-call(bf16[4,512,3072]{2,1,0:T(8,128)(2,1)} %refs_18_.1, bf16[4,3072,512]{2,1,0:T(8,128)(2,1)} %refs_16_.1, bf16[4,3072,512]{2,1,0:T(8,128)(2,1)} %refs_17_.1, ...), custom_call_target="tpu_custom_call" | custom-call | bytes 12582912 | tf_op jit(solution)/shard_map/load/pallas_call | solution.py:62
  20.4 1.6 %collective-permute-start.4 = (bf16[8,32,384]{2,1,0:T(8,128)(2,1)S(1)}, bf16[8,32,384]{2,1,0:T(8,128)(2,1)S(1)}, u32[]{:S(2)}, u32[]{:S(2)}) collective-permute-start(bf16[8,32,384]{2,1,0:T(8,128)(2,1)S(1)} %get-tuple-element.86.refs_0_), channel_id=1, source_target_pairs={{0,2},{1,17},{2,0},{3,19},{4,6},{5,21},{6,4},{7,23},{8,10},{9,25},... | collective-permute-start | bytes 589832 | tf_op jit(solution)/shard_map/ppermute | solution.py:32
  22.5 4.7 %load.5 = (bf16[3072,512]{1,0:T(8,128)(2,1)S(1)}, bf16[3072,512]{1,0:T(8,128)(2,1)S(1)}, bf16[512,3072]{1,0:T(8,128)(2,1)S(1)}, bf16[3072,512]{1,0:T(8,128)(2,1)S(1)}, f32[8,128]{1,0:T(8,128)S(1)}) custom-call(bf16[4,3072,512]{2,1,0:T(8,128)(2,1)} %refs_16_.1, bf16[4,3072,512]{2,1,0:T(8,128)(2,1)} %refs_17_.1, bf16[4,512,3072]{2,1,0:T(8,128)(2,1)} %refs_18_.1, ...), custom_call_target="tpu_custom_call" | custom-call | bytes 12582912 | tf_op jit(solution)/shard_map/load/pallas_call | solution.py:62
  28.2 0.6 collective-permute-done.7.refs_3_
  29.7 16.0 %forward.1 = (bf16[4,128,1024]{2,1,0:T(8,128)(2,1)S(1)}, f32[16,32,384]{2,1,0:T(8,128)S(1)}, bf16[16,32,384]{2,1,0:T(8,128)(2,1)S(1)}) custom-call(bf16[128,3072]{1,0:T(8,128)(2,1)S(1)} %get-tuple-element.51.refs_0_, bf16[8,32,384]{2,1,0:T(8,128)(2,1)S(1)} %get-tuple-element.85.refs_1_, bf16[8,32,384]{2,1,0:T(8,128)(2,1)S(1)} %collective-permute-done.8.refs_2_, ...), custom_call_target="tpu_custom_call" | custom-call | flops 8053063680 | bytes 37748736 | tf_op jit(solution)/shard_map/forward/pallas_call | solution.py:315
  45.9 1.7 %weight_grads.5 = (bf16[4,3072,512]{2,1,0:T(8,128)(2,1)}, bf16[4,3072,512]{2,1,0:T(8,128)(2,1)}, f32[1,32,384]{2,1,0:T(8,128)S(1)}) custom-call(bf16[3072,128]{1,0:T(8,128)(2,1)S(1)} %get-tuple-element.68.refs_0_, bf16[4,128,1024]{2,1,0:T(8,128)(2,1)S(1)} %get-tuple-element.69.refs_1_, bf16[16,32,384]{2,1,0:T(8,128)(2,1)S(1)} %get-tuple-element.67.refs_2_), custom_call_target="tpu_custom_call" | custom-call | flops 805306368 | bytes 6291456 | tf_op jit(solution)/shard_map/weight_grads/pallas_call | solution.py:246
  47.7 1.6 %collective-permute-start.11 = (bf16[8,32,384]{2,1,0:T(8,128)(2,1)S(1)}, bf16[8,32,384]{2,1,0:T(8,128)(2,1)S(1)}, u32[]{:S(2)}, u32[]{:S(2)}) collective-permute-start(bf16[8,32,384]{2,1,0:T(8,128)(2,1)S(1)} %slice.82), channel_id=1, source_target_pairs={{0,2},{1,17},{2,0},{3,19},{4,6},{5,21},{6,4},{7,23},{8,10},{9,25},... | collective-permute-start | bytes 589832 | tf_op jit(solution)/shard_map/ppermute | solution.py:32
  49.4 3.8 %weight_grads.6 = (bf16[4,3072,512]{2,1,0:T(8,128)(2,1)}, bf16[4,3072,512]{2,1,0:T(8,128)(2,1)}, f32[1,32,384]{2,1,0:T(8,128)S(1)}) custom-call(bf16[3072,128]{1,0:T(8,128)(2,1)S(1)} %get-tuple-element.68.refs_0_, bf16[4,128,1024]{2,1,0:T(8,128)(2,1)S(1)} %get-tuple-element.69.refs_1_, ...), custom_call_target="tpu_custom_call", output_to_operand_aliasing={{0}: (3, {}), {1}: (4, {})} | custom-call | flops 805306368 | bytes 6291456 | tf_op jit(solution)/shard_map/weight_grads/pallas_call | solution.py:246
  53.6 1.1 %collective-permute-start.12 = (bf16[4,32,384]{2,1,0:T(8,128)(2,1)S(1)}, bf16[4,32,384]{2,1,0:T(8,128)(2,1)S(1)}, u32[]{:S(2)}, u32[]{:S(2)}) collective-permute-start(bf16[4,32,384]{2,1,0:T(8,128)(2,1)S(1)} %slice.83), channel_id=1, source_target_pairs={{0,16},{1,3},{2,18},{3,1},{4,20},{5,7},{6,22},{7,5},{8,24},{9,11},... | collective-permute-start | bytes 294920 | tf_op jit(solution)/shard_map/ppermute | solution.py:32
  54.6 3.3 %weight_grads.7 = (bf16[4,3072,512]{2,1,0:T(8,128)(2,1)}, bf16[4,3072,512]{2,1,0:T(8,128)(2,1)}, f32[1,32,384]{2,1,0:T(8,128)S(1)}) custom-call(bf16[3072,128]{1,0:T(8,128)(2,1)S(1)} %get-tuple-element.68.refs_0_, bf16[4,128,1024]{2,1,0:T(8,128)(2,1)S(1)} %get-tuple-element.69.refs_1_, ...), custom_call_target="tpu_custom_call", output_to_operand_aliasing={{0}: (3, {}), {1}: (4, {})} | custom-call | flops 805306368 | bytes 6291456 | tf_op jit(solution)/shard_map/weight_grads/pallas_call | solution.py:246
  58.3 1.2 %collective-permute-start.13 = (bf16[2,32,384]{2,1,0:T(8,128)(2,1)S(1)}, bf16[2,32,384]{2,1,0:T(8,128)(2,1)S(1)}, u32[]{:S(2)}, u32[]{:S(2)}) collective-permute-start(bf16[2,32,384]{2,1,0:T(8,128)(2,1)S(1)} %slice.84), channel_id=1, source_target_pairs={{0,4},{1,5},{2,6},{3,7},{4,0},{5,1},{6,2},{7,3},{8,12},{9,13},{10,... | collective-permute-start | bytes 147464 | tf_op jit(solution)/shard_map/ppermute | solution.py:32
  59.5 2.5 %weight_grads.8 = (bf16[4,3072,512]{2,1,0:T(8,128)(2,1)}, bf16[4,3072,512]{2,1,0:T(8,128)(2,1)}, f32[1,32,384]{2,1,0:T(8,128)S(1)}) custom-call(bf16[3072,128]{1,0:T(8,128)(2,1)S(1)} %get-tuple-element.68.refs_0_, bf16[4,128,1024]{2,1,0:T(8,128)(2,1)S(1)} %get-tuple-element.69.refs_1_, ...), custom_call_target="tpu_custom_call", output_to_operand_aliasing={{0}: (3, {}), {1}: (4, {})} | custom-call | flops 805306368 | bytes 6291456 | tf_op jit(solution)/shard_map/weight_grads/pallas_call | solution.py:246
  62.5 2.7 %collective-permute-start.14 = (f32[1,32,384]{2,1,0:T(8,128)S(1)}, f32[1,32,384]{2,1,0:T(8,128)S(1)}, u32[]{:S(2)}, u32[]{:S(2)}) collective-permute-start(f32[1,32,384]{2,1,0:T(8,128)S(1)} %slice.58), channel_id=1, source_target_pairs={{0,8},{1,9},{2,10},{3,11},{4,12},{5,13},{6,14},{7,15},{8,0},{9,1},... | collective-permute-start | bytes 147464 | tf_op jit(solution)/shard_map/ppermute | solution.py:32
  65.2 1.7 %weight_grads.9 = (bf16[4,3072,512]{2,1,0:T(8,128)(2,1)}, bf16[4,3072,512]{2,1,0:T(8,128)(2,1)}, f32[1,32,384]{2,1,0:T(8,128)S(1)}) custom-call(bf16[3072,128]{1,0:T(8,128)(2,1)S(1)} %get-tuple-element.68.refs_0_, bf16[4,128,1024]{2,1,0:T(8,128)(2,1)S(1)} %get-tuple-element.69.refs_1_, ...), custom_call_target="tpu_custom_call", output_to_operand_aliasing={{0}: (3, {}), {1}: (4, {})} | custom-call | flops 805306368 | bytes 6291456 | tf_op jit(solution)/shard_map/weight_grads/pallas_call | solution.py:246
  66.9 0.6 collective-permute-done.14
  67.6 0.6 pad_maximum_fusion.3
  (38 shorter events, 4.9 us)
Async XLA Ops:
  1.5 4.1 %copy-start = (bf16[2,1,32,384]{3,2,1,0:T(8,128)(2,1)}, bf16[2,1,32,384]{3,2,1,0:T(8,128)(2,1)S(1)}, u32[]{:S(2)}) copy-start(bf16[2,1,32,384]{3,2,1,0:T(8,128)(2,1)S(1)} %pack.1.after) | copy-start | bytes 147460
  1.5 6.7 %collective-permute-start = (bf16[2,1,32,384]{3,2,1,0:T(8,128)(2,1)S(1)}, bf16[2,1,32,384]{3,2,1,0:T(8,128)(2,1)S(1)}, u32[]{:S(2)}, u32[]{:S(2)}) collective-permute-start(bf16[2,1,32,384]{3,2,1,0:T(8,128)(2,1)S(1)} %pack.1.after), channel_id=1, source_target_pairs={{0,8},{1,9},{2,10},{3,11},{4,12},{5,13},{6,14},{7,15},{8,0},{9,1},... | collective-permute-start | bytes 147464 | tf_op jit(solution)/shard_map/ppermute | solution.py:32
  6.3 4.2 %collective-permute-start.2 = (f32[1,8,64]{2,1,0:T(8,128)S(1)}, f32[1,8,64]{2,1,0:T(8,128)S(1)}, u32[]{:S(2)}, u32[]{:S(2)}) collective-permute-start(f32[1,8,64]{2,1,0:T(8,128)S(1)} %pack_routes.1), channel_id=1, source_target_pairs={{0,16},{1,17},{2,18},{3,19},{4,20},{5,21},{6,22},{7,23},{8,24},{9,... | collective-permute-start | bytes 6152 | tf_op jit(solution)/shard_map/ppermute | solution.py:32
  9.0 4.7 %collective-permute-start.1 = (bf16[2,2,32,384]{3,2,1,0:T(8,128)(2,1)S(1)}, bf16[2,2,32,384]{3,2,1,0:T(8,128)(2,1)S(1)}, u32[]{:S(2)}, u32[]{:S(2)}) collective-permute-start(bf16[2,2,32,384]{3,2,1,0:T(8,128)(2,1)S(1)} %pad_maximum_fusion.2.refs_2_), channel_id=1, source_target_pairs={{0,4},{1,5},{2,6},{3,7},{4,0},{5,1},{6,2},{7,3},{8,12},{9,13},{10,... | collective-permute-start | bytes 294920 | tf_op jit(solution)/shard_map/ppermute | solution.py:32
  10.5 3.2 %copy-start.1 = (bf16[2,1,32,384]{3,2,1,0:T(8,128)(2,1)S(1)}, bf16[2,1,32,384]{3,2,1,0:T(8,128)(2,1)}, u32[]{:S(2)}) copy-start(bf16[2,1,32,384]{3,2,1,0:T(8,128)(2,1)} %copy-done) | copy-start | bytes 147460
  13.7 6.5 %collective-permute-start.3 = (bf16[2,4,32,384]{3,2,1,0:T(8,128)(2,1)S(1)}, bf16[2,4,32,384]{3,2,1,0:T(8,128)(2,1)S(1)}, u32[]{:S(2)}, u32[]{:S(2)}) collective-permute-start(bf16[2,4,32,384]{3,2,1,0:T(8,128)(2,1)S(1)} %pad_maximum_fusion.1.refs_4_), channel_id=1, source_target_pairs={{0,16},{1,3},{2,18},{3,1},{4,20},{5,7},{6,22},{7,5},{8,24},{9,11},... | collective-permute-start | bytes 589832 | tf_op jit(solution)/shard_map/ppermute | solution.py:32
  20.3 2.2 %collective-permute-start.5 = (bf16[8,32,384]{2,1,0:T(8,128)(2,1)S(1)}, bf16[8,32,384]{2,1,0:T(8,128)(2,1)S(1)}, u32[]{:S(2)}, u32[]{:S(2)}) collective-permute-start(bf16[8,32,384]{2,1,0:T(8,128)(2,1)S(1)} %get-tuple-element.85.refs_1_), channel_id=1, source_target_pairs={{0,1},{1,0},{2,3},{3,2},{4,5},{5,4},{6,7},{7,6},{8,9},{9,8},{10,11... | collective-permute-start | bytes 589832 | tf_op jit(solution)/shard_map/ppermute | solution.py:32
  20.4 6.8 %collective-permute-start.4 = (bf16[8,32,384]{2,1,0:T(8,128)(2,1)S(1)}, bf16[8,32,384]{2,1,0:T(8,128)(2,1)S(1)}, u32[]{:S(2)}, u32[]{:S(2)}) collective-permute-start(bf16[8,32,384]{2,1,0:T(8,128)(2,1)S(1)} %get-tuple-element.86.refs_0_), channel_id=1, source_target_pairs={{0,2},{1,17},{2,0},{3,19},{4,6},{5,21},{6,4},{7,23},{8,10},{9,25},... | collective-permute-start | bytes 589832 | tf_op jit(solution)/shard_map/ppermute | solution.py:32
  22.0 6.3 %collective-permute-start.8 = (bf16[8,32,384]{2,1,0:T(8,128)(2,1)S(1)}, bf16[8,32,384]{2,1,0:T(8,128)(2,1)S(1)}, u32[]{:S(2)}, u32[]{:S(2)}) collective-permute-start(bf16[8,32,384]{2,1,0:T(8,128)(2,1)S(1)} %get-tuple-element.85.refs_1_), channel_id=1, source_target_pairs={{0,2},{1,17},{2,0},{3,19},{4,6},{5,21},{6,4},{7,23},{8,10},{9,25},... | collective-permute-start | bytes 589832 | tf_op jit(solution)/shard_map/ppermute | solution.py:32
  22.5 5.8 %collective-permute-start.6 = (bf16[8,32,384]{2,1,0:T(8,128)(2,1)S(1)}, bf16[8,32,384]{2,1,0:T(8,128)(2,1)S(1)}, u32[]{:S(2)}, u32[]{:S(2)}) collective-permute-start(bf16[8,32,384]{2,1,0:T(8,128)(2,1)S(1)} %get-tuple-element.86.refs_0_), channel_id=1, source_target_pairs={{0,1},{1,0},{2,3},{3,2},{4,5},{5,4},{6,7},{7,6},{8,9},{9,8},{10,11... | collective-permute-start | bytes 589832 | tf_op jit(solution)/shard_map/ppermute | solution.py:32
  27.2 1.6 %collective-permute-start.7 = (bf16[8,32,384]{2,1,0:T(8,128)(2,1)S(1)}, bf16[8,32,384]{2,1,0:T(8,128)(2,1)S(1)}, u32[]{:S(2)}, u32[]{:S(2)}) collective-permute-start(bf16[8,32,384]{2,1,0:T(8,128)(2,1)S(1)} %collective-permute-done.4.refs_1_), channel_id=1, source_target_pairs={{0,1},{1,0},{2,3},{3,2},{4,5},{5,4},{6,7},{7,6},{8,9},{9,8},{10,11... | collective-permute-start | bytes 589832 | tf_op jit(solution)/shard_map/ppermute | solution.py:32
  28.2 1.4 %collective-permute-start.9 = (bf16[8,32,384]{2,1,0:T(8,128)(2,1)S(1)}, bf16[8,32,384]{2,1,0:T(8,128)(2,1)S(1)}, u32[]{:S(2)}, u32[]{:S(2)}) collective-permute-start(bf16[8,32,384]{2,1,0:T(8,128)(2,1)S(1)} %collective-permute-done.8.refs_2_), channel_id=1, source_target_pairs={{0,1},{1,0},{2,3},{3,2},{4,5},{5,4},{6,7},{7,6},{8,9},{9,8},{10,11... | collective-permute-start | bytes 589832 | tf_op jit(solution)/shard_map/ppermute | solution.py:32
  45.7 1.9 %collective-permute-start.10 = (bf16[16,32,384]{2,1,0:T(8,128)(2,1)S(1)}, bf16[16,32,384]{2,1,0:T(8,128)(2,1)S(1)}, u32[]{:S(2)}, u32[]{:S(2)}) collective-permute-start(bf16[16,32,384]{2,1,0:T(8,128)(2,1)S(1)} %get-tuple-element.67.refs_2_), channel_id=1, source_target_pairs={{0,1},{1,0},{2,3},{3,2},{4,5},{5,4},{6,7},{7,6},{8,9},{9,8},{10,11... | collective-permute-start | bytes 1179656 | tf_op jit(solution)/shard_map/ppermute | solution.py:32
  47.7 5.7 %collective-permute-start.11 = (bf16[8,32,384]{2,1,0:T(8,128)(2,1)S(1)}, bf16[8,32,384]{2,1,0:T(8,128)(2,1)S(1)}, u32[]{:S(2)}, u32[]{:S(2)}) collective-permute-start(bf16[8,32,384]{2,1,0:T(8,128)(2,1)S(1)} %slice.82), channel_id=1, source_target_pairs={{0,2},{1,17},{2,0},{3,19},{4,6},{5,21},{6,4},{7,23},{8,10},{9,25},... | collective-permute-start | bytes 589832 | tf_op jit(solution)/shard_map/ppermute | solution.py:32
  53.6 4.7 %collective-permute-start.12 = (bf16[4,32,384]{2,1,0:T(8,128)(2,1)S(1)}, bf16[4,32,384]{2,1,0:T(8,128)(2,1)S(1)}, u32[]{:S(2)}, u32[]{:S(2)}) collective-permute-start(bf16[4,32,384]{2,1,0:T(8,128)(2,1)S(1)} %slice.83), channel_id=1, source_target_pairs={{0,16},{1,3},{2,18},{3,1},{4,20},{5,7},{6,22},{7,5},{8,24},{9,11},... | collective-permute-start | bytes 294920 | tf_op jit(solution)/shard_map/ppermute | solution.py:32
  58.3 4.2 %collective-permute-start.13 = (bf16[2,32,384]{2,1,0:T(8,128)(2,1)S(1)}, bf16[2,32,384]{2,1,0:T(8,128)(2,1)S(1)}, u32[]{:S(2)}, u32[]{:S(2)}) collective-permute-start(bf16[2,32,384]{2,1,0:T(8,128)(2,1)S(1)} %slice.84), channel_id=1, source_target_pairs={{0,4},{1,5},{2,6},{3,7},{4,0},{5,1},{6,2},{7,3},{8,12},{9,13},{10,... | collective-permute-start | bytes 147464 | tf_op jit(solution)/shard_map/ppermute | solution.py:32
  62.5 5.1 %collective-permute-start.14 = (f32[1,32,384]{2,1,0:T(8,128)S(1)}, f32[1,32,384]{2,1,0:T(8,128)S(1)}, u32[]{:S(2)}, u32[]{:S(2)}) collective-permute-start(f32[1,32,384]{2,1,0:T(8,128)S(1)} %slice.58), channel_id=1, source_target_pairs={{0,8},{1,9},{2,10},{3,11},{4,12},{5,13},{6,14},{7,15},{8,0},{9,1},... | collective-permute-start | bytes 147464 | tf_op jit(solution)/shard_map/ppermute | solution.py:32
